TPU v7x, 32 devices: a whole 2x2x4 slice. The times are simulated.
32 devices in a mesh: dp: 8 (over z, y), sp: 4 (over x, core).
Axes of the slice: x: 2, y: 2, z: 4, core: 2. Of those that a mesh axis runs over, the one named last changes fastest.
Arguments:
- clip_video: bfloat16 [128, 3, 32, 128], P('dp', None, 'sp'), may hold values from -6 to 6
- section_input: bfloat16 [128, 8, 16, 2048], P('dp', 'sp'), may hold values from -20 to 20
- keep_mask: int32 [128], P('dp'), may hold values from 0 to 1, as said below
- w_rgb: bfloat16 [9, 3, 64], P(None, None, 'dp'), may hold values from -1.25 to 1.25
- w_stem_diff: bfloat16 [9, 6, 64], P(None, None, 'dp'), may hold values from -0.875 to 0.875
- w_first: bfloat16 [2048, 512], P('dp'), may hold values from -0.125 to 0.125
- w_middle: bfloat16 [9, 512, 512], P(None, 'dp'), may hold values from -0.09375 to 0.09375
- w_last: bfloat16 [512, 2048], P('dp'), may hold values from -0.25 to 0.25
- w_reduce: bfloat16 [512, 128], P('dp'), may hold values from -0.25 to 0.25
- w_diff_full: bfloat16 [9, 128, 128], P(None, 'dp'), may hold values from -0.1875 to 0.1875
- w_diff_half: bfloat16 [9, 128, 128], P(None, 'dp'), may hold values from -0.1875 to 0.1875
- w_expand: bfloat16 [128, 512], P('dp'), may hold values from -0.5 to 0.5
- gain_first: bfloat16 [512], P('dp'), may hold values from 0.25 to 1.75
- bias_first: bfloat16 [512], P('dp'), may hold values from -3 to 3
- gain_middle: bfloat16 [512], P('dp'), may hold values from 0.25 to 1.75
- bias_middle: bfloat16 [512], P('dp'), may hold values from -3 to 3
- gain_last: bfloat16 [2048], P('dp'), may hold values from 0.25 to 1.75
- bias_last: bfloat16 [2048], P('dp'), may hold values from -3 to 3
- stem_cot: bfloat16 [128, 64, 32, 128], P('dp', None, 'sp'), may hold values from -6 to 6
- section_cot: bfloat16 [128, 8, 16, 2048], P('dp', 'sp'), may hold values from -6 to 6
Outputs:
- stem_features: bfloat16 [128, 64, 32, 128], P('dp', None, 'sp')
- video_grad: float32 [128, 3, 32, 128], P('dp', None, 'sp')
- section_output: bfloat16 [128, 8, 16, 2048], P('dp', 'sp')
- section_input_grad: bfloat16 [128, 8, 16, 2048], P('dp', 'sp')
- grad_rgb: float32 [9, 3, 64], P(None, None, 'dp')
- grad_stem_diff: float32 [9, 6, 64], P(None, None, 'dp')
- grad_first: float32 [2048, 512], P('dp')
- grad_middle: float32 [9, 512, 512], P(None, 'dp')
- grad_last: float32 [512, 2048], P('dp')
- grad_reduce: float32 [512, 128], P('dp')
- grad_diff_full: float32 [9, 128, 128], P(None, 'dp')
- grad_diff_half: float32 [9, 128, 128], P(None, 'dp')
- grad_expand: float32 [128, 512], P('dp')
- grad_gain_first: float32 [512], P('dp')
- grad_bias_first: float32 [512], P('dp')
- grad_gain_middle: float32 [512], P('dp')
- grad_bias_middle: float32 [512], P('dp')
- grad_gain_last: float32 [2048], P('dp')
- grad_bias_last: float32 [2048], P('dp')
Inputs may be any that keep to these rules, and one draw needn't show every extreme that they name: In each clip of 8 consecutive frames starting at a multiple of 8, keep_mask is 0 at the first frame and at exactly one other frame, where the second video starts, and 1 elsewhere.
All inputs are finite; a program needn't handle non-finite values.
Results may differ from a plain program's by a relative error of at most 0.018.
Values may be sent and summed in bfloat16 or wider, within the bound.
A program may use at most 256 MiB of HBM per device.

v0:
```python
import jax
import jax.numpy as jnp
from jax import lax
from jax.sharding import PartitionSpec as P

MICRO = 2


EPS = 1e-05


def with_halo(block, sides, width):
    for axis, dim in sides:
        count = lax.axis_size(axis)
        forward = [(i, i + 1) for i in range(count - 1)]
        backward = [(target, source) for source, target in forward]
        low = lax.ppermute(
            lax.slice_in_dim(block, block.shape[dim] - width, None, axis=dim), axis, forward
        )
        high = lax.ppermute(lax.slice_in_dim(block, 0, width, axis=dim), axis, backward)
        block = jnp.concatenate([low, block, high], axis=dim)
    return block


def silu_slope(values):
    sig_value = jax.nn.sigmoid(values)
    return sig_value * (1.0 + values * (1.0 - sig_value))


def tap_window(padded, row_off, col_off, row_count, col_count, row_axis):
    part_rows = lax.slice_in_dim(padded, row_off, row_off + row_count, axis=row_axis)
    return lax.slice_in_dim(part_rows, col_off, col_off + col_count, axis=row_axis + 1)


def pad_columns(haloed, row_axis):
    widths = [(0, 0)] * haloed.ndim
    widths[row_axis + 1] = (1, 1)
    return jnp.pad(haloed, widths)


def tap_conv(haloed, kernel, channels_last):
    row_axis = 1 if channels_last else 2
    row_count = haloed.shape[row_axis] - 2
    col_count = haloed.shape[row_axis + 1]
    padded = pad_columns(haloed, row_axis)
    einsum_form = "fhwc,cd->fhwd" if channels_last else "fchw,cd->fdhw"
    result = None
    for tap_index in range(9):
        window = tap_window(padded, tap_index // 3, tap_index % 3, row_count, col_count, row_axis)
        tap_term = jnp.einsum(
            einsum_form, window, kernel[tap_index], preferred_element_type=jnp.float32
        )
        result = tap_term if result is None else result + tap_term
    return result


def tap_conv_back(grad_halo, kernel, channels_last):
    row_axis = 1 if channels_last else 2
    row_count = grad_halo.shape[row_axis] - 2
    col_count = grad_halo.shape[row_axis + 1]
    padded = pad_columns(grad_halo, row_axis)
    einsum_form = "fhwd,cd->fhwc" if channels_last else "fdhw,cd->fchw"
    result = None
    for tap_index in range(9):
        window = tap_window(
            padded, 2 - tap_index // 3, 2 - tap_index % 3, row_count, col_count, row_axis
        )
        tap_term = jnp.einsum(
            einsum_form, window, kernel[tap_index], preferred_element_type=jnp.float32
        )
        result = tap_term if result is None else result + tap_term
    return result


def tap_kernel_grad(haloed, out_grad, channels_last):
    row_axis = 1 if channels_last else 2
    row_count = out_grad.shape[row_axis]
    col_count = out_grad.shape[row_axis + 1]
    padded = pad_columns(haloed, row_axis)
    einsum_form = "fhwc,fhwd->cd" if channels_last else "fchw,fdhw->cd"
    tap_list = []
    for tap_index in range(9):
        window = tap_window(padded, tap_index // 3, tap_index % 3, row_count, col_count, row_axis)
        tap_list.append(
            jnp.einsum(einsum_form, window, out_grad, preferred_element_type=jnp.float32)
        )
    return jnp.stack(tap_list, axis=0)


def pair_mean(values):
    return values.reshape(
        values.shape[0], values.shape[1] // 2, 2, values.shape[2] // 2, 2, values.shape[3]
    ).mean(axis=(2, 4))


def pair_total(values):
    return values.reshape(
        values.shape[0], values.shape[1] // 2, 2, values.shape[2] // 2, 2, values.shape[3]
    ).sum(axis=(2, 4))


def pair_grow(values):
    return jnp.repeat(jnp.repeat(values, 2, axis=1), 2, axis=2)


def norm_forward(pre_norm, gain, bias, pixel_count):
    local_sums = (jnp.sum(pre_norm, axis=(0, 1, 2)), jnp.sum(pre_norm * pre_norm, axis=(0, 1, 2)))
    total_sum, total_square = lax.psum((local_sums[0], local_sums[1]), "sp")
    mean_value = total_sum / pixel_count
    variance = total_square / pixel_count - mean_value * mean_value
    inverse = lax.rsqrt(variance + EPS)
    normed = (pre_norm - mean_value) * inverse
    return (normed, inverse, gain * normed + bias)


def norm_backward(out_grad, normed, inverse, gain, pixel_count):
    local_bias = jnp.sum(out_grad, axis=(0, 1, 2))
    local_gain = jnp.sum(out_grad * normed, axis=(0, 1, 2))
    total_bias, total_gain = lax.psum((local_bias, local_gain), "sp")
    pre_grad = (
        gain * inverse * (out_grad - total_bias / pixel_count - normed * total_gain / pixel_count)
    )
    return (pre_grad, local_gain, local_bias)


def reduce_grads(grads):
    summed = (
        lax.psum_scatter(grads[0], "dp", scatter_dimension=2, tiled=True),
        lax.psum_scatter(grads[1], "dp", scatter_dimension=2, tiled=True),
        lax.psum_scatter(grads[2], "dp", scatter_dimension=0, tiled=True),
        lax.psum_scatter(grads[3], "dp", scatter_dimension=1, tiled=True),
        lax.psum_scatter(grads[4], "dp", scatter_dimension=0, tiled=True),
        lax.psum_scatter(grads[5], "dp", scatter_dimension=0, tiled=True),
        lax.psum_scatter(grads[6], "dp", scatter_dimension=1, tiled=True),
        lax.psum_scatter(grads[7], "dp", scatter_dimension=1, tiled=True),
        lax.psum_scatter(grads[8], "dp", scatter_dimension=0, tiled=True),
        lax.psum_scatter(grads[9], "dp", scatter_dimension=0, tiled=True),
        lax.psum_scatter(grads[10], "dp", scatter_dimension=0, tiled=True),
        lax.psum_scatter(grads[11], "dp", scatter_dimension=0, tiled=True),
        lax.psum_scatter(grads[12], "dp", scatter_dimension=0, tiled=True),
        lax.psum_scatter(grads[13], "dp", scatter_dimension=0, tiled=True),
        lax.psum_scatter(grads[14], "dp", scatter_dimension=0, tiled=True),
    )
    return (
        lax.psum(summed[0].astype(jnp.bfloat16), "sp").astype(jnp.float32),
        lax.psum(summed[1].astype(jnp.bfloat16), "sp").astype(jnp.float32),
        lax.psum(summed[2].astype(jnp.bfloat16), "sp").astype(jnp.float32),
        lax.psum(summed[3].astype(jnp.bfloat16), "sp").astype(jnp.float32),
        lax.psum(summed[4].astype(jnp.bfloat16), "sp").astype(jnp.float32),
        lax.psum(summed[5].astype(jnp.bfloat16), "sp").astype(jnp.float32),
        lax.psum(summed[6].astype(jnp.bfloat16), "sp").astype(jnp.float32),
        lax.psum(summed[7].astype(jnp.bfloat16), "sp").astype(jnp.float32),
        lax.psum(summed[8].astype(jnp.bfloat16), "sp").astype(jnp.float32),
        lax.psum(summed[9].astype(jnp.bfloat16), "sp").astype(jnp.float32),
        lax.psum(summed[10].astype(jnp.bfloat16), "sp").astype(jnp.float32),
        lax.psum(summed[11].astype(jnp.bfloat16), "sp").astype(jnp.float32),
        lax.psum(summed[12].astype(jnp.bfloat16), "sp").astype(jnp.float32),
        lax.psum(summed[13].astype(jnp.bfloat16), "sp").astype(jnp.float32),
        lax.psum(summed[14].astype(jnp.bfloat16), "sp").astype(jnp.float32),
    )


def run_micro(
    video_part, feat_part, keep_part, stem_grad_in, section_grad_in, weights, pixel_count
):
    (
        rgb_k,
        stemd_k,
        first_k,
        middle_k,
        last_k,
        reduce_k,
        dfull_k,
        dhalf_k,
        expand_k,
        gain_one,
        bias_one,
        gain_two,
        bias_two,
        gain_three,
        bias_three,
    ) = weights
    keep_float = keep_part.astype(jnp.float32)
    keep_col = keep_float[:, None, None, None]
    next_col = jnp.roll(keep_float, -1)[:, None, None, None]
    frames_halo = with_halo(video_part, (("sp", 2),), 1)
    frames_wide = frames_halo.astype(jnp.float32)
    before = keep_col * (frames_wide - jnp.roll(frames_wide, 1, axis=0))
    after = next_col * (jnp.roll(frames_wide, -1, axis=0) - frames_wide)
    diff_stack = jnp.concatenate([before, after], axis=1).astype(jnp.bfloat16)
    stem_out = (tap_conv(frames_halo, rgb_k, False) + tap_conv(diff_stack, stemd_k, False)).astype(
        jnp.bfloat16
    )
    cot_halo = with_halo(stem_grad_in, (("sp", 2),), 1)
    direct_grad = tap_conv_back(cot_halo, rgb_k, False)
    diff_grad = tap_conv_back(cot_halo, stemd_k, False)
    before_grad = keep_col * diff_grad[:, :3]
    after_grad = next_col * diff_grad[:, 3:]
    video_grad = (
        direct_grad
        + before_grad
        - jnp.roll(before_grad, -1, axis=0)
        + jnp.roll(after_grad, 1, axis=0)
        - after_grad
    )
    rgb_grad = tap_kernel_grad(frames_halo, stem_grad_in, False)
    stemd_grad = tap_kernel_grad(diff_stack, stem_grad_in, False)
    row_count = feat_part.shape[1]
    col_count = feat_part.shape[2]
    first_pre = jnp.einsum("fhwc,cd->fhwd", feat_part, first_k, preferred_element_type=jnp.float32)
    normed_one, inverse_one, norm_one = norm_forward(
        first_pre, gain_one.astype(jnp.float32), bias_one.astype(jnp.float32), pixel_count
    )
    first_act = jax.nn.silu(norm_one)
    first_low = first_act.astype(jnp.bfloat16)
    reduced = jnp.einsum("fhwc,cd->fhwd", first_low, reduce_k, preferred_element_type=jnp.float32)
    change_low = (keep_col * (reduced - jnp.roll(reduced, 1, axis=0))).astype(jnp.bfloat16)
    change_halo = with_halo(change_low, (("sp", 1),), 2)
    near_rows = change_halo[:, 1 : row_count + 3]
    full_out = tap_conv(near_rows, dfull_k, True)
    pooled = pair_mean(change_halo.astype(jnp.float32)).astype(jnp.bfloat16)
    half_out = tap_conv(pooled, dhalf_k, True)
    combined_low = (full_out + pair_grow(half_out)).astype(jnp.bfloat16)
    gate_value = jax.nn.sigmoid(
        jnp.einsum("fhwc,cd->fhwd", combined_low, expand_k, preferred_element_type=jnp.float32)
    )
    gated_low = (first_act * (1.0 + gate_value)).astype(jnp.bfloat16)
    gated_halo = with_halo(gated_low, (("sp", 1),), 1)
    middle_pre = tap_conv(gated_halo, middle_k, True)
    normed_two, inverse_two, norm_two = norm_forward(
        middle_pre, gain_two.astype(jnp.float32), bias_two.astype(jnp.float32), pixel_count
    )
    second_low = jax.nn.silu(norm_two).astype(jnp.bfloat16)
    last_pre = jnp.einsum("fhwc,cd->fhwd", second_low, last_k, preferred_element_type=jnp.float32)
    normed_three, inverse_three, norm_three = norm_forward(
        last_pre, gain_three.astype(jnp.float32), bias_three.astype(jnp.float32), pixel_count
    )
    section_out = (feat_part.astype(jnp.float32) + norm_three).astype(jnp.bfloat16)
    out_grad = section_grad_in.astype(jnp.float32)
    last_grad, gain_three_grad, bias_three_grad = norm_backward(
        out_grad, normed_three, inverse_three, gain_three.astype(jnp.float32), pixel_count
    )
    last_grad_low = last_grad.astype(jnp.bfloat16)
    last_k_grad = jnp.einsum(
        "fhwc,fhwd->cd", second_low, last_grad_low, preferred_element_type=jnp.float32
    )
    second_grad = jnp.einsum(
        "fhwd,cd->fhwc", last_grad_low, last_k, preferred_element_type=jnp.float32
    ) * silu_slope(norm_two)
    middle_grad, gain_two_grad, bias_two_grad = norm_backward(
        second_grad, normed_two, inverse_two, gain_two.astype(jnp.float32), pixel_count
    )
    middle_low = middle_grad.astype(jnp.bfloat16)
    middle_halo = with_halo(middle_low, (("sp", 1),), 1)
    gated_grad = tap_conv_back(middle_halo, middle_k, True)
    middle_k_grad = tap_kernel_grad(gated_halo, middle_low, True)
    gate_grad = (gated_grad * first_act * gate_value * (1.0 - gate_value)).astype(jnp.bfloat16)
    expand_grad = jnp.einsum(
        "fhwc,fhwd->cd", combined_low, gate_grad, preferred_element_type=jnp.float32
    )
    combined_grad = jnp.einsum(
        "fhwd,cd->fhwc", gate_grad, expand_k, preferred_element_type=jnp.float32
    ).astype(jnp.bfloat16)
    half_grad = pair_total(combined_grad.astype(jnp.float32)).astype(jnp.bfloat16)
    stacked = jnp.concatenate([combined_grad, jnp.repeat(half_grad, 2, axis=1)], axis=2)
    stacked_halo = with_halo(stacked, (("sp", 1),), 2)
    full_grad_halo = stacked_halo[:, 1 : row_count + 3, :col_count]
    half_grad_halo = stacked_halo[:, 0::2, col_count:]
    change_grad = tap_conv_back(full_grad_halo, dfull_k, True) + 0.25 * pair_grow(
        tap_conv_back(half_grad_halo, dhalf_k, True)
    )
    dfull_grad = tap_kernel_grad(near_rows, combined_grad, True)
    dhalf_grad = tap_kernel_grad(pooled, half_grad, True)
    weighted = keep_col * change_grad
    reduced_grad = (weighted - jnp.roll(weighted, -1, axis=0)).astype(jnp.bfloat16)
    reduce_grad = jnp.einsum(
        "fhwc,fhwd->cd", first_low, reduced_grad, preferred_element_type=jnp.float32
    )
    first_sum = gated_grad * (1.0 + gate_value) + jnp.einsum(
        "fhwd,cd->fhwc", reduced_grad, reduce_k, preferred_element_type=jnp.float32
    )
    first_grad, gain_one_grad, bias_one_grad = norm_backward(
        first_sum * silu_slope(norm_one),
        normed_one,
        inverse_one,
        gain_one.astype(jnp.float32),
        pixel_count,
    )
    first_grad_low = first_grad.astype(jnp.bfloat16)
    first_k_grad = jnp.einsum(
        "fhwc,fhwd->cd", feat_part, first_grad_low, preferred_element_type=jnp.float32
    )
    input_grad = (
        out_grad
        + jnp.einsum("fhwd,cd->fhwc", first_grad_low, first_k, preferred_element_type=jnp.float32)
    ).astype(jnp.bfloat16)
    grads = (
        rgb_grad,
        stemd_grad,
        first_k_grad,
        middle_k_grad,
        last_k_grad,
        reduce_grad,
        dfull_grad,
        dhalf_grad,
        expand_grad,
        gain_one_grad,
        bias_one_grad,
        gain_two_grad,
        bias_two_grad,
        gain_three_grad,
        bias_three_grad,
    )
    return ((stem_out, video_grad, section_out, input_grad), grads)


def add_trees(first_tree, second_tree):
    if first_tree is None:
        return second_tree
    return jax.tree.map(
        lambda left_part, right_part: left_part + right_part, first_tree, second_tree
    )


def on_device(
    clip_video,
    section_input,
    keep_mask,
    w_rgb,
    w_stem_diff,
    w_first,
    w_middle,
    w_last,
    w_reduce,
    w_diff_full,
    w_diff_half,
    w_expand,
    gain_first,
    bias_first,
    gain_middle,
    bias_middle,
    gain_last,
    bias_last,
    stem_cot,
    section_cot,
):
    micro_frames = clip_video.shape[0] // MICRO
    pixel_count = (
        micro_frames * section_input.shape[1] * lax.axis_size("sp") * section_input.shape[2]
    )
    results = []
    grad_totals = None
    for micro_index in range(MICRO):
        weights = (
            lax.all_gather(w_rgb, "dp", axis=2, tiled=True),
            lax.all_gather(w_stem_diff, "dp", axis=2, tiled=True),
            lax.all_gather(w_first, "dp", axis=0, tiled=True),
            lax.all_gather(w_middle, "dp", axis=1, tiled=True),
            lax.all_gather(w_last, "dp", axis=0, tiled=True),
            lax.all_gather(w_reduce, "dp", axis=0, tiled=True),
            lax.all_gather(w_diff_full, "dp", axis=1, tiled=True),
            lax.all_gather(w_diff_half, "dp", axis=1, tiled=True),
            lax.all_gather(w_expand, "dp", axis=0, tiled=True),
            lax.all_gather(gain_first, "dp", axis=0, tiled=True),
            lax.all_gather(bias_first, "dp", axis=0, tiled=True),
            lax.all_gather(gain_middle, "dp", axis=0, tiled=True),
            lax.all_gather(bias_middle, "dp", axis=0, tiled=True),
            lax.all_gather(gain_last, "dp", axis=0, tiled=True),
            lax.all_gather(bias_last, "dp", axis=0, tiled=True),
        )
        low_end = micro_index * micro_frames
        high_end = low_end + micro_frames
        outputs, grads = run_micro(
            clip_video[low_end:high_end],
            section_input[low_end:high_end],
            keep_mask[low_end:high_end],
            stem_cot[low_end:high_end],
            section_cot[low_end:high_end],
            weights,
            pixel_count,
        )
        results.append(outputs)
        grad_totals = add_trees(grad_totals, reduce_grads(grads))
    stem_features = jnp.concatenate([item[0] for item in results], axis=0)
    video_grad = jnp.concatenate([item[1] for item in results], axis=0)
    section_output = jnp.concatenate([item[2] for item in results], axis=0)
    section_input_grad = jnp.concatenate([item[3] for item in results], axis=0)
    return (
        stem_features,
        video_grad,
        section_output,
        section_input_grad,
        grad_totals[0],
        grad_totals[1],
        grad_totals[2],
        grad_totals[3],
        grad_totals[4],
        grad_totals[5],
        grad_totals[6],
        grad_totals[7],
        grad_totals[8],
        grad_totals[9],
        grad_totals[10],
        grad_totals[11],
        grad_totals[12],
        grad_totals[13],
        grad_totals[14],
    )


def solution(mesh):
    placed = (
        P("dp", None, "sp", None),
        P("dp", "sp", None, None),
        P("dp"),
        P(None, None, "dp"),
        P(None, None, "dp"),
        P("dp", None),
        P(None, "dp", None),
        P("dp", None),
        P("dp", None),
        P(None, "dp", None),
        P(None, "dp", None),
        P("dp", None),
        P("dp"),
        P("dp"),
        P("dp"),
        P("dp"),
        P("dp"),
        P("dp"),
        P("dp", None, "sp", None),
        P("dp", "sp", None, None),
    )
    return jax.shard_map(
        on_device,
        mesh=mesh,
        in_specs=placed,
        out_specs=(
            P("dp", None, "sp", None),
            P("dp", None, "sp", None),
            P("dp", "sp", None, None),
            P("dp", "sp", None, None),
            P(None, None, "dp"),
            P(None, None, "dp"),
            P("dp", None),
            P(None, "dp", None),
            P("dp", None),
            P("dp", None),
            P(None, "dp", None),
            P(None, "dp", None),
            P("dp", None),
            P("dp"),
            P("dp"),
            P("dp"),
            P("dp"),
            P("dp"),
            P("dp"),
        ),
        check_vma=False,
    )
```

profile of v0, /device:TPU:0, one launch (start us, length us, event | category | flops | bytes accessed | tf_op | source)
XLA Modules:
  0.0 1729.1 jit_solution(4734709899466151320)
XLA Ops:
  9.7 2.4 collective-permute-start
  13.3 5.1 collective-permute-start.2
  23.6 33.4 %all_gather.67 = bf16[512,128]{1,0:T(8,128)(2,1)} all-gather(bf16[64,128]{1,0:T(8,128)(2,1)S(1)} %copy-done.172), channel_id=1, replica_groups=mesh['dp'=8,'sp'=4] {'dp'}, dimensions={0}, use_global_device_ids=true | all-gather | bytes 147456 | tf_op jit(solution)/shard_map/all_gather | solution.py:360
  57.0 31.6 %all_gather.68 = bf16[9,128,128]{2,1,0:T(8,128)(2,1)S(1)} all-gather(bf16[9,16,128]{2,1,0:T(8,128)(2,1)S(1)} %copy-done.156), channel_id=1, replica_groups=mesh['dp'=8,'sp'=4] {'dp'}, dimensions={1}, use_global_device_ids=true | all-gather | bytes 331776 | tf_op jit(solution)/shard_map/all_gather | solution.py:361
  88.6 31.9 %all_gather.69 = bf16[9,128,128]{2,1,0:T(8,128)(2,1)S(1)} all-gather(bf16[9,16,128]{2,1,0:T(8,128)(2,1)S(1)} %copy-done.157), channel_id=1, replica_groups=mesh['dp'=8,'sp'=4] {'dp'}, dimensions={1}, use_global_device_ids=true | all-gather | bytes 331776 | tf_op jit(solution)/shard_map/all_gather | solution.py:362
  120.5 33.1 %all_gather.70 = bf16[128,512]{1,0:T(8,128)(2,1)} all-gather(bf16[16,512]{1,0:T(8,128)(2,1)S(1)} %copy-done.173), channel_id=1, replica_groups=mesh['dp'=8,'sp'=4] {'dp'}, dimensions={0}, use_global_device_ids=true | all-gather | bytes 147456 | tf_op jit(solution)/shard_map/all_gather | solution.py:363
  157.1 21.1 %all-reduce.43 = (bf16[512]{0:T(512)(128)(2,1)S(1)}, bf16[512]{0:T(512)(128)(2,1)S(1)}, bf16[512]{0:T(512)(128)(2,1)S(1)}, bf16[512]{0:T(512)(128)(2,1)S(1)}) all-reduce(bf16[512]{0:T(512)(128)(2,1)S(1)} %dynamic-update-slice.2, bf16[512]{0:T(512)(128)(2,1)S(1)} %dynamic-update-slice.1, ...), channel_id=1, replica_groups=mesh['dp'=8,'sp'=4] {'dp'}, use_global_device_ids=true, to_apply=%add.20 | all-reduce | flops 2048 | bytes 8192
  180.5 16.5 all-gather
  197.6 18.3 %all-gather.1 = bf16[8,1,256]{2,1,0:T(2,128)(2,1)S(1)} all-gather(bf16[1,1,256]{2,1,0:T(2,128)(2,1)S(1)} %reshape.438), channel_id=1, replica_groups=mesh['dp'=8,'sp'=4] {'dp'}, dimensions={0}, use_global_device_ids=true | all-gather | bytes 4608 | tf_op jit(solution)/shard_map/all_gather | solution.py:369
  237.6 2.8 fusion.744
  241.5 8.2 all-reduce.42
  252.2 3.3 collective-permute-start.12
  257.2 4.4 collective-permute-start.8
  271.0 4.3 collective-permute-start.10
  276.7 4.9 collective-permute-start.14
  295.5 8.2 all-reduce.41
  304.4 3.9 fusion.735
  308.4 2.7 fusion.736
  311.1 12.7 all-reduce.40
  325.2 3.7 convert_reduce_fusion.1
  328.9 12.6 all-reduce.39
  342.9 4.9 fusion.6
  351.4 6.6 all-reduce.38
  360.9 3.0 collective-permute-start.20
  365.5 3.0 collective-permute-start.16
  381.9 4.1 collective-permute-start.22
  388.3 4.3 collective-permute-start.18
  440.1 2.4 fusion.739
  442.6 3.1 fusion.737
  445.8 37.7 %all-reduce.36 = (bf16[9,3,64]{0,1,2:T(4,128)(2,1)S(1)}, bf16[9,3,64]{0,1,2:T(4,128)(2,1)S(1)}, bf16[512]{0:T(512)(128)(2,1)S(1)}, bf16[512]{0:T(512)(128)(2,1)S...) all-reduce(f32[9,3,64]{0,1,2:T(4,128)S(1)} %copy-done.90, ...), channel_id=3, replica_groups=mesh['dp'=8,'sp'=4] {'dp'}, use_global_device_ids=true, to_apply=%region_56.57.clone | all-reduce | flops 15744 | bytes 94464
  492.9 34.5 %reduce-scatter.45.cloned.1.call-done = f32[16,512]{1,0:T(8,128)} async-done(((f32[128,512]{1,0:T(8,128)}), f32[16,512]{1,0:T(8,128)}) %reduce-scatter.45.cloned.1.call-update) | async-done | bytes 32784 | tf_op jit(solution)/shard_map/reduce_scatter | solution.py:136
  528.8 62.2 %reduce-scatter.35.cloned.1.call-done = f32[64,128]{1,0:T(8,128)} async-done(((f32[512,128]{1,0:T(8,128)}), f32[64,128]{1,0:T(8,128)}) %reduce-scatter.35.cloned.1.call-update) | async-done | bytes 32784 | tf_op jit(solution)/shard_map/reduce_scatter | solution.py:133
  592.4 62.3 %reduce-scatter.33.cloned.1.call-done = f32[64,128]{1,0:T(8,128)} async-done(((f32[512,128]{1,0:T(8,128)}), f32[64,128]{1,0:T(8,128)}) %reduce-scatter.33.cloned.1.call-update) | async-done | bytes 32784 | tf_op jit(solution)/shard_map/reduce_scatter | solution.py:133
  656.0 64.2 %reduce-scatter.39.cloned.1.call-done = f32[9,16,128]{2,1,0:T(8,128)} async-done(((f32[9,128,128]{2,1,0:T(8,128)}), f32[9,16,128]{2,1,0:T(8,128)}) %reduce-scatter.39.cloned.1.call-update) | async-done | bytes 73744 | tf_op jit(solution)/shard_map/reduce_scatter | solution.py:134
  721.7 64.6 %reduce-scatter.37.cloned.1.call-done = f32[9,16,128]{2,1,0:T(8,128)} async-done(((f32[9,128,128]{2,1,0:T(8,128)}), f32[9,16,128]{2,1,0:T(8,128)}) %reduce-scatter.37.cloned.1.call-update) | async-done | bytes 73744 | tf_op jit(solution)/shard_map/reduce_scatter | solution.py:134
  787.8 63.9 %reduce-scatter.43.cloned.1.call-done = f32[9,16,128]{2,1,0:T(8,128)} async-done(((f32[9,128,128]{2,1,0:T(8,128)}), f32[9,16,128]{2,1,0:T(8,128)}) %reduce-scatter.43.cloned.1.call-update) | async-done | bytes 73744 | tf_op jit(solution)/shard_map/reduce_scatter | solution.py:135
  853.2 64.7 %reduce-scatter.41.cloned.1.call-done = f32[9,16,128]{2,1,0:T(8,128)} async-done(((f32[9,128,128]{2,1,0:T(8,128)}), f32[9,16,128]{2,1,0:T(8,128)}) %reduce-scatter.41.cloned.1.call-update) | async-done | bytes 73744 | tf_op jit(solution)/shard_map/reduce_scatter | solution.py:135
  919.5 4.1 convolution_bitcast_fusion
  924.6 4.1 convolution_bitcast_fusion.1
  929.4 5.9 all-reduce.37
  937.5 4.0 convolution_bitcast_fusion.2
  941.5 3.9 convolution_bitcast_fusion.3
  963.8 3.7 collective-permute-start.6
  970.1 3.9 collective-permute-start.4
  974.1 27.5 %all_gather.61 = bf16[9,6,64]{0,2,1:T(8,128)(2,1)S(1)} all-gather(bf16[9,6,8]{0,2,1:T(8,128)(2,1)S(1)} %copy-done.184), channel_id=1, replica_groups=mesh['dp'=8,'sp'=4] {'dp'}, dimensions={2}, use_global_device_ids=true | all-gather | bytes 7776 | tf_op jit(solution)/shard_map/all_gather | solution.py:356
  1003.0 26.7 %all_gather.60 = bf16[9,3,64]{0,2,1:T(8,128)(2,1)S(1)} all-gather(bf16[9,3,8]{0,2,1:T(8,128)(2,1)S(1)} %copy-done.237), channel_id=1, replica_groups=mesh['dp'=8,'sp'=4] {'dp'}, dimensions={2}, use_global_device_ids=true | all-gather | bytes 3888 | tf_op jit(solution)/shard_map/all_gather | solution.py:355
  1042.0 1.8 fusion.419
  1053.0 1.8 fusion.416
  1054.8 1.9 fusion.410
  1056.7 1.8 fusion.415
  1076.6 1.9 fusion.338
  1092.5 1.8 fusion.409
  1108.8 13.1 fusion.194
  1124.1 9.4 fusion.193
  1133.8 3.1 copy.223
  1142.1 2.6 select_maximum_fusion
  1146.2 2.8 select_maximum_fusion.2
  1179.1 55.6 %reduce-scatter.23.cloned.1.call-done = f32[256,512]{0,1:T(8,128)} async-done(((f32[2048,512]{0,1:T(8,128)}), f32[256,512]{0,1:T(8,128)}) %reduce-scatter.23.cloned.1.call-update) | async-done | bytes 524304 | tf_op jit(solution)/shard_map/reduce_scatter | solution.py:130
  1236.5 90.4 %reduce-scatter.21.cloned.1.call-done = f32[256,512]{0,1:T(8,128)} async-done(((f32[2048,512]{0,1:T(8,128)}), f32[256,512]{0,1:T(8,128)}) %reduce-scatter.21.cloned.1.call-update) | async-done | bytes 524304 | tf_op jit(solution)/shard_map/reduce_scatter | solution.py:130
  1328.7 165.3 %reduce-scatter.27.cloned.1.call-done = f32[9,64,512]{2,1,0:T(8,128)} async-done(((f32[9,512,512]{2,1,0:T(8,128)}), f32[9,64,512]{2,1,0:T(8,128)}) %reduce-scatter.27.cloned.1.call-update) | async-done | bytes 1179664 | tf_op jit(solution)/shard_map/reduce_scatter | solution.py:131
  1494.0 2.2 convert_element_type.502
  1496.2 164.1 %reduce-scatter.25.cloned.1.call-done = f32[9,64,512]{2,1,0:T(8,128)} async-done(((f32[9,512,512]{2,1,0:T(8,128)}), f32[9,64,512]{2,1,0:T(8,128)}) %reduce-scatter.25.cloned.1.call-update) | async-done | bytes 1179664 | tf_op jit(solution)/shard_map/reduce_scatter | solution.py:131
  1660.3 2.2 convert_element_type.500
  1665.6 52.2 %all-reduce.51.cloned.1.call-done = (bf16[256,512]{0,1:T(8,128)(2,1)}, bf16[256,512]{0,1:T(8,128)(2,1)}, bf16[9,64,512]{2,1,0:T(8,128)(2,1)}, bf16[9,64,512]{2,1...) async-done(((bf16[256,512]{0,1:T(8,128)(2,1)}, bf16[256,512]{0,1:T(8,128)(2,1)}, bf16[9,64,512]{2,1,0:T(8,128)(2,1)}, bf16[9,64,512]{2,1,0:T(8,128)(2,1)}, ...) | async-done | bytes 2228240 | tf_op jit(solution)/shard_map/psum | solution.py:147
  (1121 shorter events, 299.3 us)
Async XLA Ops:
  7.2 230.4 %all-gather.6.cloned.1.call-start = ((), (), s32[]{:S(2)}) async-start(), calls=%async_computation.16 | async-start | bytes 2359296 | tf_op jit(solution)/shard_map/all_gather | solution.py:357
  7.9 276.0 %all-gather.8.cloned.1.call-start = ((), (), s32[]{:S(2)}) async-start(), calls=%async_computation.17 | async-start | bytes 5308416 | tf_op jit(solution)/shard_map/all_gather | solution.py:358
  8.7 295.7 %all-gather.10.cloned.1.call-start = ((), (), s32[]{:S(2)}) async-start(), calls=%async_computation.18 | async-start | bytes 2359296 | tf_op jit(solution)/shard_map/all_gather | solution.py:359
  9.7 208.9 %collective-permute-start = (bf16[8,3,1,128]{3,1,2,0:T(4,128)(2,1)S(1)}, bf16[8,3,1,128]{3,1,2,0:T(4,128)(2,1)S(1)}, u32[]{:S(2)}, u32[]{:S(2)}) collective-permute-start(bf16[8,3,1,128]{3,1,2,0:T(4,128)(2,1)S(1)} %copy.354), channel_id=1, source_target_pairs={{0,1},{1,2},{2,3},{4,5},{5,6},{6,7},{8,9},{9,10},{10,11},{12,13},{... | collective-permute-start | bytes 18440 | tf_op jit(solution)/shard_map/ppermute | solution.py:17
  12.0 206.6 %collective-permute-start.1 = (bf16[8,3,1,128]{3,1,2,0:T(4,128)(2,1)S(1)}, bf16[8,3,1,128]{3,1,2,0:T(4,128)(2,1)S(1)}, u32[]{:S(2)}, u32[]{:S(2)}) collective-permute-start(bf16[8,3,1,128]{3,1,2,0:T(4,128)(2,1)S(1)} %copy.356), channel_id=1, source_target_pairs={{1,0},{2,1},{3,2},{5,4},{6,5},{7,6},{9,8},{10,9},{11,10},{13,12},{... | collective-permute-start | bytes 18440 | tf_op jit(solution)/shard_map/ppermute | solution.py:20
  13.3 205.9 %collective-permute-start.2 = (bf16[8,3,1,128]{3,1,2,0:T(4,128)(2,1)S(1)}, bf16[8,3,1,128]{3,1,2,0:T(4,128)(2,1)S(1)}, u32[]{:S(2)}, u32[]{:S(2)}) collective-permute-start(bf16[8,3,1,128]{3,1,2,0:T(4,128)(2,1)S(1)} %copy.375), channel_id=1, source_target_pairs={{0,1},{1,2},{2,3},{4,5},{5,6},{6,7},{8,9},{9,10},{10,11},{12,13},{... | collective-permute-start | bytes 18440 | tf_op jit(solution)/shard_map/ppermute | solution.py:17
  18.5 200.9 %collective-permute-start.3 = (bf16[8,3,1,128]{3,1,2,0:T(4,128)(2,1)S(1)}, bf16[8,3,1,128]{3,1,2,0:T(4,128)(2,1)S(1)}, u32[]{:S(2)}, u32[]{:S(2)}) collective-permute-start(bf16[8,3,1,128]{3,1,2,0:T(4,128)(2,1)S(1)} %copy.377), channel_id=1, source_target_pairs={{1,0},{2,1},{3,2},{5,4},{6,5},{7,6},{9,8},{10,9},{11,10},{13,12},{... | collective-permute-start | bytes 18440 | tf_op jit(solution)/shard_map/ppermute | solution.py:20
  19.8 417.4 %reduce-scatter.19.cloned.1.call-start = ((), (), s32[]{:S(2)}) async-start(), calls=%async_computation.20 | async-start | bytes 294912 | tf_op jit(solution)/shard_map/reduce_scatter | solution.py:129
  20.7 200.5 %copy-start.71 = (bf16[8,3,8,128]{3,2,1,0:T(8,128)(2,1)}, bf16[8,3,8,128]{3,2,1,0:T(8,128)(2,1)S(1)}, u32[]{:S(2)}) copy-start(bf16[8,3,8,128]{3,2,1,0:T(8,128)(2,1)S(1)} %get-tuple-element.243) | copy-start | bytes 147460
  20.7 209.8 %copy-start.69 = (bf16[8,3,8,128]{3,2,1,0:T(8,128)(2,1)}, bf16[8,3,8,128]{3,2,1,0:T(8,128)(2,1)S(1)}, u32[]{:S(2)}) copy-start(bf16[8,3,8,128]{3,2,1,0:T(8,128)(2,1)S(1)} %get-tuple-element.242) | copy-start | bytes 147460
  21.6 229.2 %copy-start.181 = (f32[8]{0:T(128)}, f32[8]{0:T(128)S(1)}, u32[]{:S(2)}) copy-start(f32[8]{0:T(128)S(1)} %get-tuple-element.321) | copy-start | bytes 100
  21.6 234.2 %copy-start.178 = (f32[8]{0:T(128)}, f32[8]{0:T(128)S(1)}, u32[]{:S(2)}) copy-start(f32[8]{0:T(128)S(1)} %get-tuple-element.320) | copy-start | bytes 100
  21.8 158.7 %copy-start.273 = (bf16[256]{0:T(256)(128)(2,1)S(1)}, bf16[256]{0:T(256)(128)(2,1)}, u32[]{:S(2)}) copy-start(bf16[256]{0:T(256)(128)(2,1)} %param.36) | copy-start | bytes 1540
  21.8 175.8 %copy-start.274 = (bf16[256]{0:T(256)(128)(2,1)S(1)}, bf16[256]{0:T(256)(128)(2,1)}, u32[]{:S(2)}) copy-start(bf16[256]{0:T(256)(128)(2,1)} %param.37) | copy-start | bytes 1540
  23.6 203.7 %copy-start = (bf16[8,64,8,128]{3,2,1,0:T(8,128)(2,1)}, bf16[8,64,8,128]{3,2,1,0:T(8,128)(2,1)S(1)}, u32[]{:S(2)}) copy-start(bf16[8,64,8,128]{3,2,1,0:T(8,128)(2,1)S(1)} %get-tuple-element.219) | copy-start | bytes 3145732
  88.6 179.4 %copy-start.17 = (bf16[9,128,128]{2,1,0:T(8,128)(2,1)}, bf16[9,128,128]{2,1,0:T(8,128)(2,1)S(1)}, u32[]{:S(2)}) copy-start(bf16[9,128,128]{2,1,0:T(8,128)(2,1)S(1)} %all_gather.68) | copy-start | bytes 884740
  235.3 203.3 %reduce-scatter.17.cloned.1.call-start = ((), (), s32[]{:S(2)}) async-start(), calls=%async_computation.19 | async-start | bytes 294912 | tf_op jit(solution)/shard_map/reduce_scatter | solution.py:129
  237.5 254.0 %reduce-scatter.47.cloned.1.call-start = ((), (), s32[]{:S(2)}) async-start(), calls=%async_computation.34 | async-start | bytes 294912 | tf_op jit(solution)/shard_map/reduce_scatter | solution.py:136
  250.9 11.0 collective-permute-start.13
  252.2 9.7 collective-permute-start.12
  255.9 7.0 collective-permute-start.9
  257.2 5.7 collective-permute-start.8
  269.7 11.8 collective-permute-start.11
  271.0 10.5 collective-permute-start.10
  275.4 6.6 collective-permute-start.15
  276.7 5.8 collective-permute-start.14
  359.5 9.0 collective-permute-start.21
  360.9 9.0 collective-permute-start.20
  364.2 9.5 collective-permute-start.17
  365.5 8.6 collective-permute-start.16
  380.6 27.4 %collective-permute-start.23 = (bf16[8,2,24,128]{3,2,1,0:T(8,128)(2,1)}, bf16[8,2,24,128]{3,2,1,0:T(8,128)(2,1)}, u32[]{:S(2)}, u32[]{:S(2)}) collective-permute-start(bf16[8,2,24,128]{3,2,1,0:T(8,128)(2,1)} %pad_maximum_fusion.27), channel_id=1, source_target_pairs={{1,0},{2,1},{3,2},{5,4},{6,5},{7,6},{9,8},{10,9},{11,10},{13,12},{... | collective-permute-start | bytes 294920 | tf_op jit(solution)/shard_map/ppermute | solution.py:20
  381.9 26.1 %collective-permute-start.22 = (bf16[8,2,24,128]{3,2,1,0:T(8,128)(2,1)}, bf16[8,2,24,128]{3,2,1,0:T(8,128)(2,1)S(1)}, u32[]{:S(2)}, u32[]{:S(2)}) collective-permute-start(bf16[8,2,24,128]{3,2,1,0:T(8,128)(2,1)} %pad_maximum_fusion.27), channel_id=1, source_target_pairs={{0,1},{1,2},{2,3},{4,5},{5,6},{6,7},{8,9},{9,10},{10,11},{12,13},{... | collective-permute-start | bytes 294920 | tf_op jit(solution)/shard_map/ppermute | solution.py:17
  387.0 25.8 %collective-permute-start.19 = (bf16[8,2,24,128]{3,2,1,0:T(8,128)(2,1)}, bf16[8,2,24,128]{3,2,1,0:T(8,128)(2,1)}, u32[]{:S(2)}, u32[]{:S(2)}) collective-permute-start(bf16[8,2,24,128]{3,2,1,0:T(8,128)(2,1)} %pad_maximum_fusion.26), channel_id=1, source_target_pairs={{1,0},{2,1},{3,2},{5,4},{6,5},{7,6},{9,8},{10,9},{11,10},{13,12},{... | collective-permute-start | bytes 294920 | tf_op jit(solution)/shard_map/ppermute | solution.py:20
  388.3 24.6 %collective-permute-start.18 = (bf16[8,2,24,128]{3,2,1,0:T(8,128)(2,1)}, bf16[8,2,24,128]{3,2,1,0:T(8,128)(2,1)S(1)}, u32[]{:S(2)}, u32[]{:S(2)}) collective-permute-start(bf16[8,2,24,128]{3,2,1,0:T(8,128)(2,1)} %pad_maximum_fusion.26), channel_id=1, source_target_pairs={{0,1},{1,2},{2,3},{4,5},{5,6},{6,7},{8,9},{9,10},{10,11},{12,13},{... | collective-permute-start | bytes 294920 | tf_op jit(solution)/shard_map/ppermute | solution.py:17
  404.4 123.0 %reduce-scatter.45.cloned.1.call-start = ((), (), s32[]{:S(2)}) async-start(), calls=%async_computation.33 | async-start | bytes 294912 | tf_op jit(solution)/shard_map/reduce_scatter | solution.py:136
  407.8 183.2 %reduce-scatter.35.cloned.1.call-start = ((), (), s32[]{:S(2)}) async-start(), calls=%async_computation.28 | async-start | bytes 294912 | tf_op jit(solution)/shard_map/reduce_scatter | solution.py:133
  420.6 234.1 %reduce-scatter.33.cloned.1.call-start = ((), (), s32[]{:S(2)}) async-start(), calls=%async_computation.27 | async-start | bytes 294912 | tf_op jit(solution)/shard_map/reduce_scatter | solution.py:133
  422.9 297.3 %reduce-scatter.39.cloned.1.call-start = ((), (), s32[]{:S(2)}) async-start(), calls=%async_computation.30 | async-start | bytes 663552 | tf_op jit(solution)/shard_map/reduce_scatter | solution.py:134
  425.5 360.8 %reduce-scatter.37.cloned.1.call-start = ((), (), s32[]{:S(2)}) async-start(), calls=%async_computation.29 | async-start | bytes 663552 | tf_op jit(solution)/shard_map/reduce_scatter | solution.py:134
  430.0 421.7 %reduce-scatter.43.cloned.1.call-start = ((), (), s32[]{:S(2)}) async-start(), calls=%async_computation.32 | async-start | bytes 663552 | tf_op jit(solution)/shard_map/reduce_scatter | solution.py:135
  433.9 484.0 %reduce-scatter.41.cloned.1.call-start = ((), (), s32[]{:S(2)}) async-start(), calls=%async_computation.31 | async-start | bytes 663552 | tf_op jit(solution)/shard_map/reduce_scatter | solution.py:135
  436.1 730.7 %all-reduce.49.cloned.1.call-start = ((), (), s32[]{:S(2)}) async-start(), calls=%async_computation.35 | async-start | bytes 536576 | tf_op jit(solution)/shard_map/psum | solution.py:145
  442.6 476.9 %copy-start.46 = (f32[8,2,16,512]{3,2,1,0:T(8,128)S(1)}, f32[8,2,16,512]{3,2,1,0:T(8,128)}, u32[]{:S(2)}) copy-start(f32[8,2,16,512]{3,2,1,0:T(8,128)} %get-tuple-element.325) | copy-start | bytes 1572868
  919.4 256.1 %reduce-scatter.31.cloned.1.call-start = ((), (), s32[]{:S(2)}) async-start(), calls=%async_computation.26 | async-start | bytes 4718592 | tf_op jit(solution)/shard_map/reduce_scatter | solution.py:132
  923.6 253.7 %reduce-scatter.29.cloned.1.call-start = ((), (), s32[]{:S(2)}) async-start(), calls=%async_computation.25 | async-start | bytes 4718592 | tf_op jit(solution)/shard_map/reduce_scatter | solution.py:132
  928.8 305.9 %reduce-scatter.23.cloned.1.call-start = ((), (), s32[]{:S(2)}) async-start(), calls=%async_computation.22 | async-start | bytes 4718592 | tf_op jit(solution)/shard_map/reduce_scatter | solution.py:130
  941.5 385.4 %reduce-scatter.21.cloned.1.call-start = ((), (), s32[]{:S(2)}) async-start(), calls=%async_computation.21 | async-start | bytes 4718592 | tf_op jit(solution)/shard_map/reduce_scatter | solution.py:130
  945.5 548.5 %reduce-scatter.27.cloned.1.call-start = ((), (), s32[]{:S(2)}) async-start(), calls=%async_computation.24 | async-start | bytes 10616832 | tf_op jit(solution)/shard_map/reduce_scatter | solution.py:131
  958.6 701.7 %reduce-scatter.25.cloned.1.call-start = ((), (), s32[]{:S(2)}) async-start(), calls=%async_computation.23 | async-start | bytes 10616832 | tf_op jit(solution)/shard_map/reduce_scatter | solution.py:131
  961.8 178.3 %collective-permute-start.7 = (bf16[8,64,1,128]{3,1,2,0:T(8,128)(2,1)}, bf16[8,64,1,128]{3,1,2,0:T(8,128)(2,1)}, u32[]{:S(2)}, u32[]{:S(2)}) collective-permute-start(bf16[8,64,1,128]{3,1,2,0:T(8,128)(2,1)} %copy.383), channel_id=1, source_target_pairs={{1,0},{2,1},{3,2},{5,4},{6,5},{7,6},{9,8},{10,9},{11,10},{13,12},{... | collective-permute-start | bytes 393224 | tf_op jit(solution)/shard_map/ppermute | solution.py:20
  963.8 173.1 %collective-permute-start.6 = (bf16[8,64,1,128]{3,1,2,0:T(8,128)(2,1)}, bf16[8,64,1,128]{3,1,2,0:T(8,128)(2,1)}, u32[]{:S(2)}, u32[]{:S(2)}) collective-permute-start(bf16[8,64,1,128]{3,1,2,0:T(8,128)(2,1)} %copy.381), channel_id=1, source_target_pairs={{0,1},{1,2},{2,3},{4,5},{5,6},{6,7},{8,9},{9,10},{10,11},{12,13},{... | collective-permute-start | bytes 393224 | tf_op jit(solution)/shard_map/ppermute | solution.py:17
  968.2 173.0 %collective-permute-start.5 = (bf16[8,64,1,128]{3,1,2,0:T(8,128)(2,1)}, bf16[8,64,1,128]{3,1,2,0:T(8,128)(2,1)}, u32[]{:S(2)}, u32[]{:S(2)}) collective-permute-start(bf16[8,64,1,128]{3,1,2,0:T(8,128)(2,1)} %copy.380), channel_id=1, source_target_pairs={{1,0},{2,1},{3,2},{5,4},{6,5},{7,6},{9,8},{10,9},{11,10},{13,12},{... | collective-permute-start | bytes 393224 | tf_op jit(solution)/shard_map/ppermute | solution.py:20
  970.1 167.7 %collective-permute-start.4 = (bf16[8,64,1,128]{3,1,2,0:T(8,128)(2,1)}, bf16[8,64,1,128]{3,1,2,0:T(8,128)(2,1)}, u32[]{:S(2)}, u32[]{:S(2)}) collective-permute-start(bf16[8,64,1,128]{3,1,2,0:T(8,128)(2,1)} %copy.378), channel_id=1, source_target_pairs={{0,1},{1,2},{2,3},{4,5},{5,6},{6,7},{8,9},{9,10},{10,11},{12,13},{... | collective-permute-start | bytes 393224 | tf_op jit(solution)/shard_map/ppermute | solution.py:17
  1092.4 625.4 %all-reduce.51.cloned.1.call-start = ((), (), s32[]{:S(2)}) async-start(), calls=%async_computation.36 | async-start | bytes 4456448 | tf_op jit(solution)/shard_map/psum | solution.py:147
  1496.2 166.3 %copy-start.275 = (bf16[64]{0:T(256)(128)(2,1)S(1)}, bf16[64]{0:T(256)(128)(2,1)}, u32[]{:S(2)}) copy-start(bf16[64]{0:T(256)(128)(2,1)} %get-tuple-element.198) | copy-start | bytes 388
  1496.2 166.4 %copy-start.276 = (bf16[64]{0:T(256)(128)(2,1)S(1)}, bf16[64]{0:T(256)(128)(2,1)}, u32[]{:S(2)}) copy-start(bf16[64]{0:T(256)(128)(2,1)} %get-tuple-element.199) | copy-start | bytes 388
  1496.2 166.9 %copy-start.176 = (bf16[64,128]{1,0:T(8,128)(2,1)S(1)}, bf16[64,128]{1,0:T(8,128)(2,1)}, u32[]{:S(2)}) copy-start(bf16[64,128]{1,0:T(8,128)(2,1)} %get-tuple-element.184) | copy-start | bytes 49156
  1496.2 166.9 %copy-start.177 = (bf16[64,128]{1,0:T(8,128)(2,1)S(1)}, bf16[64,128]{1,0:T(8,128)(2,1)}, u32[]{:S(2)}) copy-start(bf16[64,128]{1,0:T(8,128)(2,1)} %get-tuple-element.185) | copy-start | bytes 49156
  1496.2 167.5 %copy-start.174 = (bf16[16,512]{1,0:T(8,128)(2,1)S(1)}, bf16[16,512]{1,0:T(8,128)(2,1)}, u32[]{:S(2)}) copy-start(bf16[16,512]{1,0:T(8,128)(2,1)} %get-tuple-element.190) | copy-start | bytes 49156
  1496.2 167.5 %copy-start.175 = (bf16[16,512]{1,0:T(8,128)(2,1)S(1)}, bf16[16,512]{1,0:T(8,128)(2,1)}, u32[]{:S(2)}) copy-start(bf16[16,512]{1,0:T(8,128)(2,1)} %get-tuple-element.191) | copy-start | bytes 49156
  1496.2 168.1 %copy-start.160 = (bf16[9,16,128]{2,1,0:T(8,128)(2,1)S(1)}, bf16[9,16,128]{2,1,0:T(8,128)(2,1)}, u32[]{:S(2)}) copy-start(bf16[9,16,128]{2,1,0:T(8,128)(2,1)} %get-tuple-element.186) | copy-start | bytes 110596
  1496.2 168.1 %copy-start.161 = (bf16[9,16,128]{2,1,0:T(8,128)(2,1)S(1)}, bf16[9,16,128]{2,1,0:T(8,128)(2,1)}, u32[]{:S(2)}) copy-start(bf16[9,16,128]{2,1,0:T(8,128)(2,1)} %get-tuple-element.187) | copy-start | bytes 110596
  1496.2 168.7 %copy-start.158 = (bf16[9,16,128]{2,1,0:T(8,128)(2,1)S(1)}, bf16[9,16,128]{2,1,0:T(8,128)(2,1)}, u32[]{:S(2)}) copy-start(bf16[9,16,128]{2,1,0:T(8,128)(2,1)} %get-tuple-element.188) | copy-start | bytes 110596
  1496.2 168.7 %copy-start.159 = (bf16[9,16,128]{2,1,0:T(8,128)(2,1)S(1)}, bf16[9,16,128]{2,1,0:T(8,128)(2,1)}, u32[]{:S(2)}) copy-start(bf16[9,16,128]{2,1,0:T(8,128)(2,1)} %get-tuple-element.189) | copy-start | bytes 110596
  (263 other events, 3127.0 us)
Sparse Core Ops, SparseCore 0:
  10.1 53.0 all-gather.5
  65.4 84.4 all-gather.7
  152.0 47.9 all-gather.9
  235.5 61.7 reduce-scatter.18
  300.4 60.2 reduce-scatter.16
  404.5 59.0 reduce-scatter.46
  466.9 60.4 reduce-scatter.44
  530.8 60.2 reduce-scatter.34
  594.3 60.2 reduce-scatter.32
  657.8 62.3 reduce-scatter.38
  723.9 62.3 reduce-scatter.36
  789.5 62.1 reduce-scatter.42
  855.4 62.4 reduce-scatter.40
  922.9 32.9 all-reduce.48
  959.4 92.1 reduce-scatter.30
  1055.5 87.6 reduce-scatter.28
  1146.6 88.0 reduce-scatter.22
  1238.6 88.2 reduce-scatter.20
  1330.5 163.4 reduce-scatter.26
  1497.4 162.8 reduce-scatter.24
  1664.2 53.5 all-reduce.50
where the time goes:
time: 1740 us; the launch traced here: 1730 us
  waiting for transfers between devices  946 us (54%)
  blocking collectives  332 us (19%)
  matrix products  242 us (14%)
  other arithmetic  75.5 us (4%)
  starting transfers between devices  63 us (4%)
  local copies, waits for them, and re-layouts  49.4 us (3%)
  between operations  21.3 us (1%)
    reduce_scatter x2, waiting for transfers between devices, reduce_grads(): lax.psum_scatter(grads[3], 'dp', scatter_dimension=1, tiled=True)  329 us
    reduce_scatter x2, waiting for transfers between devices, reduce_grads(): lax.psum_scatter(grads[2], 'dp', scatter_dimension=0, tiled=True)  146 us
    reduce_scatter x2, waiting for transfers between devices, reduce_grads(): lax.psum_scatter(grads[6], 'dp', scatter_dimension=1, tiled=True)  129 us
    reduce_scatter x2, waiting for transfers between devices, reduce_grads(): lax.psum_scatter(grads[7], 'dp', scatter_dimension=1, tiled=True)  129 us
    reduce_scatter x2, waiting for transfers between devices, reduce_grads(): lax.psum_scatter(grads[5], 'dp', scatter_dimension=0, tiled=True)  125 us
    dot_general x90, matrix products, tap_conv(): jnp.einsum(einsum_form, window, kernel[tap_index], preferred_element_type...  100 us
    dot_general x90, matrix products, tap_kernel_grad(): jnp.einsum(einsum_form, window, out_grad, preferred_element_type=jnp.floa...  64.7 us
    unnamed x2, blocking collectives  58.7 us
  transfers between devices with their start and end apart: 45, of which 13 were waited for; matrix products, arithmetic and copies ran while one was open for 20% of the time, Pallas kernels for 0%

commit v1 on v0

--- a/solution.py
+++ b/solution.py
@@ -1,7 +1,15 @@
+import functools
+
 import jax
 import jax.numpy as jnp
+import numpy as np
 from jax import lax
+from jax.experimental import pallas as pl
+from jax.experimental.pallas import tpu as pltpu
 from jax.sharding import PartitionSpec as P
+
+H5, HS, MID, TDM_C, C5, STEM_C = 8, 32, 512, 128, 2048, 64
+VMEM_BYTES = 63 * 2**20
 
 MICRO = 2
 
@@ -408,6 +416,1118 @@
     )
 
 
+F32 = jnp.float32
+BF16 = jnp.bfloat16
+MESH_ID = pl.DeviceIdType.MESH
+GROUP = 8
+LANES = 128
+STEP = 32
+PART = 2
+
+
+def dot_nn(left, right):
+    return lax.dot_general(left, right, (((1,), (0,)), ((), ())), preferred_element_type=F32)
+
+
+def dot_nt(left, right):
+    return lax.dot_general(left, right, (((1,), (1,)), ((), ())), preferred_element_type=F32)
+
+
+def dot_tn(left, right):
+    return lax.dot_general(left, right, (((0,), (0,)), ((), ())), preferred_element_type=F32)
+
+
+def shift_down(values, count):
+    size = values.shape[0]
+    column = lax.broadcasted_iota(jnp.int32, values.shape, 0) & 15
+    return jnp.where(column < count, 0.0, pltpu.roll(values, count, 0))
+
+
+def shift_up(values, count):
+    size = values.shape[0]
+    column = lax.broadcasted_iota(jnp.int32, values.shape, 0) & 15
+    return jnp.where(column >= 16 - count, 0.0, pltpu.roll(values, size - count, 0))
+
+
+def pair_sum(values):
+    size = values.shape[0]
+    parity = lax.broadcasted_iota(jnp.int32, values.shape, 0) & 1
+    return values + jnp.where(parity == 0, pltpu.roll(values, size - 1, 0), pltpu.roll(values, 1, 0))
+
+
+def band_table(rows):
+    table = np.zeros((rows, 96, 3 * LANES), np.float32)
+    for i in range(rows):
+        for a in range(3):
+            for b in range(3):
+                for ch in range(9):
+                    base = (b * 3 + ch // 3) * 32
+                    row = i + a - 1
+                    if row < 0:
+                        n = base + 24 + (ch % 3) * 2
+                    elif row >= rows:
+                        n = base + 24 + (ch % 3) * 2 + 1
+                    else:
+                        n = base + (ch % 3) * 8 + row
+                    table[i, (3 * a + b) * 9 + ch, n] = 1.0
+    return table
+
+
+def silu_parts(values):
+    sig = jax.nn.sigmoid(values)
+    return values * sig, sig * (1.0 + values * (1.0 - sig))
+
+
+def whole_kernel(
+    sizes, keep, uin, small, band, x_hbm, ct_hbm, sc_hbm, wf_in, wm_in, wl_in, wr_in, wd0_in, wd1_in, we_in,
+    so_hbm, vg_out, out_hbm, ig_hbm, of_out, om_out, ol_out, or_out, od_out, oe_out, osm_out,
+    ssem, rsem, lsem, wf, wm, wl, wr, wd, we, x3, ct3, sc, so, ust, uprev, unext, sm, tf, tff, tb, dg,
+    vgh, vgr, stg, stgr, stat_s, stat_r, st3_s, st3_r, z1, fab, gt, rd, chb, chr_, cs, ps, comb,
+    gb, gr, gs, z2, sab, z3, lgb, cgx, cgr, cgs, hgs, fgb, ost,
+    g_first, g_mid, g_last, g_diff, g_re, rcf, rxf, ryf, rzf, rcm, rxm, rym, rzm, rcl, rxl, ryl, rzl,
+    rcd, ryd, rzd, fdx, rxd, fdo, rcr, ryr, rzr, frx, rxr, fbf, fbm, fbl, sms, smr,
+):
+    D, S, NF = sizes
+    DZ, SX = D // 2, S // 2
+    NG = NF // GROUP
+    NW = NF * 16
+    GW = GROUP * 16
+    dp, sp = lax.axis_index("dp"), lax.axis_index("sp")
+    z, y = dp // 2, dp % 2
+    x, c = sp // 2, sp % 2
+    oy, oc = 1 - y, 1 - c
+    q_own = c * SX + x
+
+    def at_zy(zz, yy):
+        return (zz * 2 + yy, sp)
+
+    y_peer = at_zy(z, oy)
+    c_peer = (dp, x * 2 + oc)
+
+    def z_to(k):
+        return lax.rem(z + k, DZ)
+
+    def z_from(k):
+        return lax.rem(z + DZ - k, DZ)
+
+    def x_to(k):
+        return lax.rem(x + k, SX)
+
+    def x_from(k):
+        return lax.rem(x + SX - k, SX)
+
+    def x_peer(k):
+        return (dp, x_to(k) * 2 + c)
+
+    sp_peers = [(dp, lax.rem(sp + k, S)) for k in range(1, S)]
+    dp_peers = [(lax.rem(dp + k, D), sp) for k in range(1, D)]
+    has_prev, has_next = sp > 0, sp < S - 1
+    prev_dev, next_dev = (dp, sp - 1), (dp, sp + 1)
+
+    counters = {"r": 0, "l": 0}
+    sends = []
+
+    def remote(src, dst, dev):
+        i = counters["r"]
+        counters["r"] += 1
+        copy = pltpu.make_async_remote_copy(
+            src_ref=src, dst_ref=dst, send_sem=ssem.at[i], recv_sem=rsem.at[i],
+            device_id=dev, device_id_type=MESH_ID,
+        )
+        copy.start()
+        sends.append(copy)
+        return copy
+
+    def local(src, dst):
+        i = counters["l"]
+        counters["l"] += 1
+        copy = pltpu.make_async_copy(src, dst, lsem.at[i])
+        copy.start()
+        return copy
+
+    @pl.when(sp == 0)
+    def _():
+        uprev[...] = jnp.zeros_like(uprev)
+        vgr[0] = jnp.zeros(vgr.shape[1:], F32)
+        chr_[0] = jnp.zeros(chr_.shape[1:], BF16)
+        gr[0] = jnp.zeros(gr.shape[1:], BF16)
+        cgr[0] = jnp.zeros(cgr.shape[1:], BF16)
+
+    @pl.when(sp == S - 1)
+    def _():
+        unext[...] = jnp.zeros_like(unext)
+        vgr[1] = jnp.zeros(vgr.shape[1:], F32)
+        chr_[1] = jnp.zeros(chr_.shape[1:], BF16)
+        gr[1] = jnp.zeros(gr.shape[1:], BF16)
+        cgr[1] = jnp.zeros(cgr.shape[1:], BF16)
+
+    barrier = pltpu.get_barrier_semaphore()
+    for peer in sp_peers + dp_peers:
+        pl.semaphore_signal(barrier, inc=1, device_id=peer, device_id_type=MESH_ID)
+    own_small = local(small, sm.at[dp])
+    own = [
+        local(wf_in, wf.at[z, y]), local(wd0_in, wd.at[0, :, z, y]), local(wd1_in, wd.at[1, :, z, y]),
+        local(wr_in, wr.at[z, y]), local(we_in, we.at[z, y]), local(wm_in, wm.at[:, z, y]),
+        local(wl_in, wl.at[z, y]),
+    ]
+
+    def load_cot(part):
+        lo = part * PART
+        return local(sc_hbm.at[pl.ds(lo, PART)], sc.at[pl.ds(lo % (2 * PART), PART)])
+
+    load_sc = [load_cot(0), load_cot(1)]
+    load_x = [local(x_hbm.at[:, r], x3.at[pl.ds(r * NF, NF)]) for r in range(2)]
+    load_ct = [local(ct_hbm.at[:, r], ct3.at[pl.ds(r * NF, NF)]) for r in range(2)]
+    pl.semaphore_wait(barrier, S - 1 + D - 1)
+
+    halo_waits = []
+
+    def halo(to_prev, to_next, from_prev, from_next, land_prev, land_next):
+        i = counters["r"]
+        counters["r"] += 2
+
+        def up():
+            return pltpu.make_async_remote_copy(
+                src_ref=to_prev, dst_ref=land_next, send_sem=ssem.at[i], recv_sem=rsem.at[i],
+                device_id=prev_dev, device_id_type=MESH_ID)
+
+        def down():
+            return pltpu.make_async_remote_copy(
+                src_ref=to_next, dst_ref=land_prev, send_sem=ssem.at[i + 1], recv_sem=rsem.at[i + 1],
+                device_id=next_dev, device_id_type=MESH_ID)
+
+        @pl.when(has_prev)
+        def _():
+            up().start()
+
+        @pl.when(has_next)
+        def _():
+            down().start()
+
+        def wait():
+            @pl.when(has_prev)
+            def _():
+                down().wait_recv()
+
+            @pl.when(has_next)
+            def _():
+                up().wait_recv()
+
+        def finish():
+            @pl.when(has_prev)
+            def _():
+                up().wait_send()
+
+            @pl.when(has_next)
+            def _():
+                down().wait_send()
+
+        halo_waits.append(finish)
+        return wait, finish
+
+    small_copies = [remote(small, sm.at[dp], peer) for peer in dp_peers]
+    edge = uin.at[:, pl.ds(24, 8)]
+    wait_edges, _ = halo(edge, edge, None, None, uprev, unext)
+
+    def gather(mode, src, dst):
+        piece = q_own if mode == "A" else c
+        zs = [remote(src(piece), dst(z, y, piece), at_zy(z_to(k), y)) for k in range(1, DZ)]
+        ys = [remote(src(piece), dst(z, y, piece), y_peer)]
+        yield
+        xs, cores = [], []
+
+        def fan(zz, yy):
+            part = dst(zz, yy, piece)
+            if mode == "A":
+                for k in range(1, SX):
+                    xs.append((zz, yy, k, remote(part, part, x_peer(k))))
+            if mode != "D":
+                cores.append(remote(part, part, c_peer))
+
+        for k in range(1, DZ):
+            zs[k - 1].wait_recv()
+            part = dst(z_from(k), y, piece)
+            ys.append(remote(part, part, y_peer))
+            fan(z_from(k), y)
+        yield
+        for k in range(DZ):
+            ys[k].wait_recv()
+            fan(z_from(k), oy)
+        yield
+        for zz, yy, k, copy in xs:
+            copy.wait_recv()
+            part = dst(zz, yy, c * SX + x_from(k))
+            cores.append(remote(part, part, c_peer))
+        yield
+        for copy in cores:
+            copy.wait_recv()
+
+    def lane_block(index, width):
+        return pl.ds(pl.multiple_of(index * width, width), width)
+
+    fr, fw = wf_in.shape[0], wf_in.shape[1] // S
+    mw = wm_in.shape[2] // S
+    lr, lw = wl_in.shape[0], wl_in.shape[1] // S
+
+    def first_part(lo, n):
+        return gather("A", lambda q: wf_in.at[pl.ds(lo, n), lane_block(q, fw)],
+                      lambda zz, yy, q: wf.at[zz, yy, pl.ds(lo, n), lane_block(q, fw)])
+
+    def mid_part(lo, n):
+        return gather("A", lambda q: wm_in.at[pl.ds(lo, n), :, lane_block(q, mw)],
+                      lambda zz, yy, q: wm.at[pl.ds(lo, n), zz, yy, :, lane_block(q, mw)])
+
+    def last_part(lo, n):
+        return gather("A", lambda q: wl_in.at[pl.ds(lo, n), lane_block(q, lw)],
+                      lambda zz, yy, q: wl.at[zz, yy, pl.ds(lo, n), lane_block(q, lw)])
+
+    for copy in own:
+        copy.wait()
+    chunks = [
+        first_part(0, fr // 2),
+        first_part(fr // 2, fr // 2),
+        gather("D", lambda q: wr_in, lambda zz, yy, q: wr.at[zz, yy]),
+        gather("B", lambda q: wd.at[q, :, z, y], lambda zz, yy, q: wd.at[q, :, zz, yy]),
+        gather("D", lambda q: we_in, lambda zz, yy, q: we.at[zz, yy]),
+        mid_part(0, 3), mid_part(3, 3), mid_part(6, 3),
+        last_part(0, lr // 2), last_part(lr // 2, lr // 2),
+    ]
+    slot_of = [0, 1, 2, 2, 2, 3, 4, 5, 6, 7]
+    slot = [0]
+
+    def pump():
+        for start, chunk in zip(slot_of, chunks):
+            if start <= slot[0]:
+                next(chunk, None)
+        slot[0] += 1
+
+    pump()
+
+    own_small.wait()
+    for copy in small_copies:
+        copy.wait_recv()
+    wt = sm[:, 0:8, :].reshape(D * 8, LANES)[:, 0:96].astype(BF16)
+    for i in range(8):
+        rows = dot_nn(wt, band[i])
+        for n in range(3):
+            tff[n, pl.ds(i, D * 8, stride=8), :] = rows[:, n * LANES : (n + 1) * LANES]
+    for n in range(3):
+        columns = min(288 - n * LANES, LANES)
+        tf[:, n * LANES : n * LANES + columns] = tff[n, :, 0:columns].astype(BF16)
+        tb[n * LANES : n * LANES + columns, :] = tff[n].T[0:columns].astype(BF16)
+
+    per = D * LANES // 512
+
+    def mid_vec(j):
+        parts = []
+        for m in range(D // per):
+            row = sm[m * per, 8 + j : 9 + j, :]
+            for n in range(1, per):
+                row = row + sm[m * per + n, 8 + j : 9 + j, :]
+            parts.append(row)
+        return jnp.concatenate(parts, axis=1)
+
+    rows_last = 2048 // D // LANES
+
+    def last_vec(j):
+        return jnp.concatenate(
+            [sm[d, 8 + j + n : 9 + j + n, :] for d in range(D) for n in range(rows_last)], axis=1)
+
+    gain_1, bias_1, gain_2, bias_2 = [mid_vec(j) for j in range(4)]
+    gain_3, bias_3 = last_vec(4), last_vec(4 + rows_last)
+
+    wait_edges()
+    side = lax.broadcasted_iota(jnp.int32, (8, LANES), 0) & 1
+    ust[...] = uin[...]
+    for f in range(NF):
+        ust[f, 24:32, :] = jnp.where(
+            side == 0, pltpu.roll(uprev[f], 7, 0), pltpu.roll(unext[f], 1, 0))
+    zt = tff
+    zt[...] = jnp.zeros_like(zt)
+
+    def stem_frame(f, carry):
+        before_at, after_at = lax.rem(f + NF - 1, NF), lax.rem(f + 1, NF)
+        k_here, k_next = keep[f].astype(F32), keep[after_at].astype(F32)
+        frame = ust[f]
+        stacked = jnp.concatenate(
+            [frame, k_here * (frame - ust[before_at]), k_next * (ust[after_at] - frame)], axis=0)
+        stacked = stacked.astype(BF16).astype(F32)
+        lane = lax.broadcasted_iota(jnp.int32, stacked.shape, 1)
+        left = jnp.where(lane == 0, 0.0, pltpu.roll(stacked, 1, 1))
+        right = jnp.where(lane == LANES - 1, 0.0, pltpu.roll(stacked, LANES - 1, 1))
+        taps = jnp.concatenate([left, stacked, right], axis=0).astype(BF16)
+        place = lax.rem(f, 2 * PART)
+        cot = sc[place]
+        so[place] = dot_nn(tf[...], taps).astype(BF16)
+        back = dot_nn(tb[...], cot)
+        dg[f] = (
+            jnp.where(lane == LANES - 1, 0.0, pltpu.roll(back[0:96], LANES - 1, 1))
+            + back[96:192]
+            + jnp.where(lane == 0, 0.0, pltpu.roll(back[192:288], 1, 1)))
+        cross = dot_nt(cot, taps)
+        for n in range(3):
+            columns = min(288 - n * LANES, LANES)
+            zt[n, :, 0:columns] += cross[:, n * LANES : n * LANES + columns]
+        return carry
+
+    store_so = []
+    for part in range(NF // PART):
+        lo = part * PART
+        load_sc[part].wait()
+        if part >= 2:
+            store_so[part - 2].wait()
+        lax.fori_loop(lo, lo + PART, stem_frame, 0)
+        store_so.append(local(so.at[pl.ds(lo % (2 * PART), PART)], so_hbm.at[pl.ds(lo, PART)]))
+        if part + 2 < NF // PART:
+            load_sc.append(load_cot(part + 2))
+        pump()
+    for copy in store_so[-2:]:
+        copy.wait()
+
+    def video_frame(f, carry):
+        before_at, after_at = lax.rem(f + NF - 1, NF), lax.rem(f + 1, NF)
+        k_here, k_next = keep[f].astype(F32), keep[after_at].astype(F32)
+        total = (
+            dg[f, 0:32] + k_here * dg[f, 32:64] - k_next * dg[after_at, 32:64]
+            + k_here * dg[before_at, 64:96] - k_next * dg[f, 64:96])
+        vg_out[f] = total[0:24]
+        vgh[f] = total[24:32]
+        return carry
+
+    lax.fori_loop(0, NF, video_frame, 0)
+    wait_video, _ = halo(vgh, vgh, None, None, vgr.at[0], vgr.at[1])
+
+    stem_grad = jnp.zeros((D * 8, 96), F32)
+    for i in range(8):
+        for n in range(3):
+            part = zt[n, pl.ds(i, D * 8, stride=8), :]
+            high = part.astype(BF16)
+            low = (part - high.astype(F32)).astype(BF16)
+            table = band[i, :, n * LANES : (n + 1) * LANES]
+            stem_grad = stem_grad + dot_nt(high, table) + dot_nt(low, table)
+    stg[...] = jnp.concatenate([stem_grad, jnp.zeros((D * 8, LANES - 96), F32)], axis=1)
+    stem_copies = [remote(stg, stgr.at[k], peer) for k, peer in enumerate(sp_peers)]
+    pump()
+    pump()
+
+    def rows_loop(group, fn, init):
+        def body(i, carry):
+            start = (i // (GW // STEP)) * NW + group * GW + (i % (GW // STEP)) * STEP
+            return fn(pl.multiple_of(start, STEP), carry)
+        return lax.fori_loop(0, 2 * (GW // STEP), body, init)
+
+    def fold(values):
+        return values.reshape(STEP // 8, 8, values.shape[1]).sum(axis=0)
+
+    def sp_send(i, parts):
+        width = parts[0].shape[1]
+        fill = [jnp.zeros((8 - len(parts), width), F32)] if len(parts) < 8 else []
+        stat_s[i] = jnp.concatenate(parts + fill, axis=0)
+        return [remote(stat_s.at[i], stat_r.at[i, k], peer) for k, peer in enumerate(sp_peers)]
+
+    def sp_total(i, copies):
+        total = stat_s[i]
+        for k, copy in enumerate(copies):
+            copy.wait_recv()
+            total = total + stat_r[i, k]
+        return total
+
+    pixels = jnp.float32(GROUP * 2 * S * 16)
+    inv_pixels = 1.0 / (GROUP * 2 * S * 16)
+
+    def two_sums(ref):
+        parts = []
+        for group in range(NG):
+            def add(start, carry):
+                value = ref[pl.ds(start, STEP), :]
+                return carry[0] + fold(value), carry[1] + fold(value * value)
+            zero = jnp.zeros((8, ref.shape[1]), F32)
+            one, two = rows_loop(group, add, (zero, zero))
+            parts += [jnp.sum(one, axis=0, keepdims=True), jnp.sum(two, axis=0, keepdims=True)]
+        return parts
+
+    def moments(total, row):
+        mean = total[row : row + 1] * inv_pixels
+        variance = total[row + 1 : row + 2] * inv_pixels - mean * mean
+        return mean, lax.rsqrt(variance + EPS)
+
+    for copy in load_x:
+        copy.wait()
+    xs = x3[...].reshape(2 * NW, x3.shape[2])
+    for n in range(2):
+        z1[:, n * 256 : (n + 1) * 256] = dot_nn(xs, wf[:, :, :, n * 256 : (n + 1) * 256].reshape(x3.shape[2], 256))
+    copies = sp_send(0, two_sums(z1))
+    pump()
+    total = sp_total(0, copies)
+    inv_1 = []
+    for group in range(NG):
+        mean, inv = moments(total, 2 * group)
+        inv_1.append(inv)
+
+        def apply_1(start, carry):
+            normed = (z1[pl.ds(start, STEP), :] - mean) * inv
+            act = jax.nn.silu(gain_1 * normed + bias_1)
+            z1[pl.ds(start, STEP), :] = normed
+            z3[pl.ds(start, STEP), 0:512] = act
+            fab[pl.ds(start, STEP), :] = act.astype(BF16)
+            return carry
+        rows_loop(group, apply_1, 0)
+
+    rd[...] = dot_nn(fab[...], wr[...].reshape(512, LANES))
+    for r in range(2):
+        for f in range(NF):
+            here = r * NW + f * 16
+            past = r * NW + ((f - 1) % NF) * 16
+            diff = keep[f].astype(F32) * (rd[here : here + 16, :] - rd[past : past + 16, :])
+            chb[r, f * 16 : f * 16 + 16, :] = diff.astype(BF16)
+    wait_change, free_change = halo(chb, chb, None, None, chr_.at[0], chr_.at[1])
+
+    def put_shifts(ref, at, values, count, flip):
+        width = values.shape[1]
+        down, up = shift_down(values, count), shift_up(values, count)
+        low, high = (up, down) if flip else (down, up)
+        ref[at, :, 0:width] = low.astype(BF16)
+        ref[at, :, width : 2 * width] = values.astype(BF16)
+        ref[at, :, 2 * width : 3 * width] = high.astype(BF16)
+
+    change = [chb[r].astype(F32) for r in range(2)]
+    for r in range(2):
+        put_shifts(cs, 1 + r, change[r], 1, False)
+
+    def pool(upper, lower):
+        return (pair_sum(upper + lower) * 0.25).astype(BF16).astype(F32)
+
+    put_shifts(ps, 1, pool(change[0], change[1]), 2, False)
+    pump()
+    wait_change()
+    above = [chr_[0, r].astype(F32) for r in range(2)]
+    below = [chr_[1, r].astype(F32) for r in range(2)]
+    put_shifts(cs, 0, above[1], 1, False)
+    put_shifts(cs, 3, below[0], 1, False)
+    put_shifts(ps, 0, pool(above[0], above[1]), 2, False)
+    put_shifts(ps, 2, pool(below[0], below[1]), 2, False)
+    full = jnp.zeros((2 * NW, LANES), F32)
+    half = jnp.zeros((NW, LANES), F32)
+    for a in range(3):
+        full = full + dot_nn(cs[a : a + 2].reshape(2 * NW, 384), wd[0, 3 * a : 3 * a + 3].reshape(384, LANES))
+        half = half + dot_nn(ps[a], wd[1, 3 * a : 3 * a + 3].reshape(384, LANES))
+    comb[...] = (full + jnp.concatenate([half, half], axis=0)).astype(BF16)
+    gt[...] = dot_nn(comb[...], we[...].reshape(LANES, 512))
+
+    def apply_gate(i, carry):
+        start = pl.multiple_of(i * STEP, STEP)
+        gate = jax.nn.sigmoid(gt[pl.ds(start, STEP), :])
+        gt[pl.ds(start, STEP), :] = gate
+        gated = (z3[pl.ds(start, STEP), 0:512] * (1.0 + gate)).astype(BF16)
+        gb[pl.ds(start, STEP), :] = gated
+        return carry
+
+    lax.fori_loop(0, 2 * NW // STEP, apply_gate, 0)
+    wait_gated, free_gated = halo(gb.at[pl.ds(0, NW)], gb.at[pl.ds(NW, NW)], None, None, gr.at[0], gr.at[1])
+
+    def spread(dst, at, src_fn, flip):
+        def body(i, carry):
+            start = pl.multiple_of(i * STEP, STEP)
+            values = src_fn(start).astype(F32)
+            down, up = shift_down(values, 1), shift_up(values, 1)
+            low, high = (up, down) if flip else (down, up)
+            dst[at, pl.ds(start, STEP), 0:512] = low.astype(BF16)
+            dst[at, pl.ds(start, STEP), 512:1024] = values.astype(BF16)
+            dst[at, pl.ds(start, STEP), 1024:1536] = high.astype(BF16)
+            return carry
+        lax.fori_loop(0, NW // STEP, body, 0)
+
+    for r in range(2):
+        spread(gs, 1 + r, lambda start, r=r: gb[pl.ds(r * NW + start, STEP), :], False)
+    pump()
+    pump()
+    pump()
+    pump()
+
+    def taps_of(a):
+        return wm[3 * a : 3 * a + 3].reshape(1536, 512)
+
+    z2[...] = dot_nn(gs[1:3].reshape(2 * NW, 1536), taps_of(1))
+    z2[0:NW, :] += dot_nn(gs[2], taps_of(2))
+    z2[NW : 2 * NW, :] += dot_nn(gs[1], taps_of(0))
+    wait_gated()
+    spread(gs, 0, lambda start: gr[0, pl.ds(start, STEP), :], False)
+    spread(gs, 3, lambda start: gr[1, pl.ds(start, STEP), :], False)
+    z2[0:NW, :] += dot_nn(gs[0], taps_of(0))
+    z2[NW : 2 * NW, :] += dot_nn(gs[3], taps_of(2))
+    copies = sp_send(1, two_sums(z2))
+    for copy in load_ct:
+        copy.wait()
+    total = sp_total(1, copies)
+    inv_2 = []
+    for group in range(NG):
+        mean, inv = moments(total, 2 * group)
+        inv_2.append(inv)
+
+        def apply_2(start, carry):
+            normed = (z2[pl.ds(start, STEP), :] - mean) * inv
+            z2[pl.ds(start, STEP), :] = normed
+            sab[pl.ds(start, STEP), :] = jax.nn.silu(gain_2 * normed + bias_2).astype(BF16)
+            return carry
+        rows_loop(group, apply_2, 0)
+
+    def ct_rows(start, lo, width):
+        return ct3[pl.ds(start // 16, STEP // 16), :, lo : lo + width].reshape(STEP, width).astype(F32)
+
+    def x_rows(start, lo, width):
+        return x3[pl.ds(start // 16, STEP // 16), :, lo : lo + width].reshape(STEP, width).astype(F32)
+
+    last_copies = []
+    for n in range(4):
+        lo = n * 512
+        z3[:, lo : lo + 512] = dot_nn(sab[...], wl[:, :, :, lo : lo + 512].reshape(512, 512))
+        parts = []
+        for group in range(NG):
+            def add_3(start, carry):
+                value = z3[pl.ds(start, STEP), lo : lo + 512]
+                cot = ct_rows(start, lo, 512)
+                return (carry[0] + fold(value), carry[1] + fold(value * value),
+                        carry[2] + fold(cot), carry[3] + fold(cot * value))
+            zero = jnp.zeros((8, 512), F32)
+            sums = rows_loop(group, add_3, (zero, zero, zero, zero))
+            parts += [jnp.sum(item, axis=0, keepdims=True) for item in sums]
+        st3_s[n] = jnp.concatenate(parts, axis=0)
+        last_copies.append(
+            [remote(st3_s.at[n], st3_r.at[n, k], peer) for k, peer in enumerate(sp_peers)])
+    gain_3_grad, bias_3_grad = [], []
+    stores = []
+
+    def free_part():
+        if len(stores) >= 2:
+            for copy in stores[-2]:
+                copy.wait()
+
+    def store_part(n, target):
+        stores.append([local(ost.at[n % 2, pl.ds(r * NF, NF)], target.at[:, r, :, pl.ds(n * 512, 512)]) for r in range(2)])
+
+    for n in range(4):
+        lo = n * 512
+        free_part()
+        total = st3_s[n]
+        for k, copy in enumerate(last_copies[n]):
+            copy.wait_recv()
+            total = total + st3_r[n, k]
+        gain, bias = gain_3[:, lo : lo + 512], bias_3[:, lo : lo + 512]
+        gain_sum = bias_sum = jnp.zeros((1, 512), F32)
+        for group in range(NG):
+            row = 4 * group
+            mean, inv = moments(total, row)
+            cot_sum = total[row + 2 : row + 3]
+            cot_normed = inv * (total[row + 3 : row + 4] - mean * cot_sum)
+            gain_sum, bias_sum = gain_sum + cot_normed, bias_sum + cot_sum
+            cot_mean, slope_mean = cot_sum * inv_pixels, cot_normed * inv_pixels
+            scale = gain * inv
+
+            def apply_3(start, carry):
+                normed = (z3[pl.ds(start, STEP), lo : lo + 512] - mean) * inv
+                cot = ct_rows(start, lo, 512)
+                out = x_rows(start, lo, 512) + gain * normed + bias
+                ost[n % 2, pl.ds(start // 16, STEP // 16)] = out.astype(BF16).reshape(STEP // 16, 16, 512)
+                lgb[pl.ds(start, STEP), lo : lo + 512] = (
+                    scale * (cot - cot_mean - normed * slope_mean)).astype(BF16)
+                return carry
+            rows_loop(group, apply_3, 0)
+        store_part(n, out_hbm)
+        gain_3_grad.append(gain_sum)
+        bias_3_grad.append(bias_sum)
+
+    def each(count, fn):
+        def body(i, carry):
+            fn(i)
+            return carry
+        lax.fori_loop(0, count, body, 0)
+
+    def reduce_wide(grad, rc, rx, ry, rz, fb, taps, put):
+        mine = q_own
+
+        def lead(ref, head, t, tail):
+            return ref.at[head + ((t,) if taps else ()) + tail]
+
+        rows_n = taps if taps else 1
+        got = remote(grad.at[pl.ds(oc * SX, SX)], rc, c_peer)
+        yield
+        got.wait_recv()
+        for xx in range(SX):
+            def add_c(i):
+                t, zz = i // DZ, i % DZ
+                for yy in range(2):
+                    dst = lead(grad, (c * SX + xx,), t, (zz, yy))
+                    src = lead(rc, (xx,), t, (zz, yy))
+                    dst[...] = (dst[...].astype(F32) + src[...].astype(F32)).astype(BF16)
+            each(rows_n * DZ, add_c)
+        got = [remote(grad.at[c * SX + x_to(k)], rx.at[k - 1], x_peer(k)) for k in range(1, SX)]
+        yield
+        for copy in got:
+            copy.wait_recv()
+
+        def add_x(i):
+            t, zz = i // DZ, i % DZ
+            for yy in range(2):
+                dst = lead(grad, (mine,), t, (zz, yy))
+                value = dst[...].astype(F32)
+                for k in range(1, SX):
+                    value = value + lead(rx, (k - 1,), t, (zz, yy))[...].astype(F32)
+                dst[...] = value.astype(BF16)
+        each(rows_n * DZ, add_x)
+        every = (slice(None),)
+        got = remote(grad.at[(mine,) + (every if taps else ()) + (slice(None), oy)], ry, y_peer)
+        yield
+        got.wait_recv()
+
+        def add_y(i):
+            t, zz = i // DZ, i % DZ
+            dst = lead(grad, (mine,), t, (zz, y))
+            src = lead(ry, (), t, (zz,))
+            dst[...] = (dst[...].astype(F32) + src[...].astype(F32)).astype(BF16)
+        each(rows_n * DZ, add_y)
+        got = [remote(grad.at[(mine,) + (every if taps else ()) + (z_to(k), y)], rz.at[k - 1], at_zy(z_to(k), y))
+               for k in range(1, DZ)]
+        yield
+        for copy in got:
+            copy.wait_recv()
+
+        def add_z(t):
+            value = lead(grad, (mine,), t, (z, y))[...].astype(F32)
+            for k in range(1, DZ):
+                value = value + lead(rz, (k - 1,), t, ())[...].astype(F32)
+            lead(fb, (mine,), t, ())[...] = value.astype(BF16)
+        each(rows_n, add_z)
+        got = [remote(fb.at[mine], fb.at[mine], peer) for peer in sp_peers]
+        yield
+        for copy in got:
+            copy.wait_recv()
+        for qq in range(S):
+            put(qq, fb[qq].astype(F32))
+
+    def reduce_diff():
+        got = remote(g_diff.at[oc], rcd, c_peer)
+        yield
+        got.wait_recv()
+
+        def add_c(i):
+            t, zz = i // DZ, i % DZ
+            for yy in range(2):
+                value = g_diff[c, t, zz, yy].astype(F32) + rcd[t, zz, yy].astype(F32)
+                g_diff[c, t, zz, yy] = value.astype(BF16)
+        each(9 * DZ, add_c)
+        got = remote(g_diff.at[c, :, :, oy], ryd, y_peer)
+        yield
+        got.wait_recv()
+
+        def add_y(i):
+            t, zz = i // DZ, i % DZ
+            value = g_diff[c, t, zz, y].astype(F32) + ryd[t, zz].astype(F32)
+            g_diff[c, t, zz, y] = value.astype(BF16)
+        each(9 * DZ, add_y)
+        got = [remote(g_diff.at[c, :, z_to(k), y], rzd.at[k - 1], at_zy(z_to(k), y)) for k in range(1, DZ)]
+        yield
+        for copy in got:
+            copy.wait_recv()
+
+        def add_z(t):
+            value = g_diff[c, t, z, y].astype(F32)
+            for k in range(1, DZ):
+                value = value + rzd[k - 1, t].astype(F32)
+            fdx[t] = value
+        each(9, add_z)
+        got = [remote(fdx, rxd.at[k - 1], x_peer(k)) for k in range(1, SX)]
+        yield
+        for copy in got:
+            copy.wait_recv()
+
+        def add_x(t):
+            value = fdx[t]
+            for k in range(1, SX):
+                value = value + rxd[k - 1, t]
+            fdo[c, t] = value
+        each(9, add_x)
+        got = remote(fdo.at[c], fdo.at[c], c_peer)
+        yield
+        got.wait_recv()
+        od_out[...] = fdo[...]
+
+    def reduce_rest():
+        got = remote(g_re, rcr, c_peer)
+        yield
+        got.wait_recv()
+        shared = (g_re.shape[2], LANES)
+
+        def add_c(zz):
+            for yy in range(2):
+                value = g_re[zz, yy].astype(F32) + rcr[zz, yy].astype(F32)
+                rcr[zz, yy] = value.astype(BF16)
+        each(DZ, add_c)
+        got = remote(rcr.at[:, oy], ryr, y_peer)
+        yield
+        got.wait_recv()
+
+        def add_y(zz):
+            value = rcr[zz, y].astype(F32) + ryr[zz].astype(F32)
+            rcr[zz, y] = value.astype(BF16)
+        each(DZ, add_y)
+        got = [remote(rcr.at[z_to(k), y], rzr.at[k - 1], at_zy(z_to(k), y)) for k in range(1, DZ)]
+        yield
+        for copy in got:
+            copy.wait_recv()
+        value = rcr[z, y].astype(F32)
+        for k in range(1, DZ):
+            value = value + rzr[k - 1].astype(F32)
+        frx[...] = value
+        got = [remote(frx, rxr.at[k - 1], x_peer(k)) for k in range(1, SX)]
+        yield
+        for copy in got:
+            copy.wait_recv()
+        value = frx[...]
+        for k in range(1, SX):
+            value = value + rxr[k - 1]
+        n_red, n_exp = or_out.shape[0], oe_out.shape[0]
+        or_out[...] = value[0:n_red]
+        for b in range(4):
+            oe_out[:, b * LANES : (b + 1) * LANES] = value[n_red + b * n_exp : n_red + (b + 1) * n_exp]
+
+    def put_first(qq, value):
+        of_out[:, qq * fw : (qq + 1) * fw] = value
+
+    def put_mid(qq, value):
+        om_out[:, :, qq * mw : (qq + 1) * mw] = value
+
+    def put_last(qq, value):
+        ol_out[:, qq * lw : (qq + 1) * lw] = value
+
+    red_last = reduce_wide(g_last, rcl, rxl, ryl, rzl, fbl, 0, put_last)
+    red_mid = reduce_wide(g_mid, rcm, rxm, rym, rzm, fbm, 9, put_mid)
+    red_first = reduce_wide(g_first, rcf, rxf, ryf, rzf, fbf, 0, put_first)
+    red_diff, red_rest = reduce_diff(), reduce_rest()
+
+    def push(*chains):
+        for chain in chains:
+            next(chain, None)
+
+    for finish in (free_gated, free_change):
+        finish()
+        halo_waits.remove(finish)
+    mgb, mgr = gb, gr
+    sg2, gg = z3.at[:, 0:512], z3.at[:, 512:1024]
+    sg2[...] = dot_nt(lgb[...], wl[...].reshape(512, 2048))
+    parts = []
+    for group in range(NG):
+        def slope_2(start, carry):
+            normed = z2[pl.ds(start, STEP), :]
+            _, slope = silu_parts(gain_2 * normed + bias_2)
+            value = sg2[pl.ds(start, STEP), :] * slope
+            sg2[pl.ds(start, STEP), :] = value
+            return carry[0] + fold(value), carry[1] + fold(value * normed)
+        zero = jnp.zeros((8, 512), F32)
+        sums = rows_loop(group, slope_2, (zero, zero))
+        parts += [jnp.sum(item, axis=0, keepdims=True) for item in sums]
+    copies = sp_send(2, parts)
+    for n in range(4):
+        g_last[n] = dot_tn(sab[...], lgb[:, n * 512 : (n + 1) * 512]).astype(BF16).reshape(DZ, 2, lr, 512)
+    push(red_last)
+    total = sp_total(2, copies)
+    gain_2_grad = bias_2_grad = jnp.zeros((1, 512), F32)
+    for group in range(NG):
+        row = 2 * group
+        bias_sum, gain_sum = total[row : row + 1], total[row + 1 : row + 2]
+        gain_2_grad, bias_2_grad = gain_2_grad + gain_sum, bias_2_grad + bias_sum
+        scale = gain_2 * inv_2[group]
+
+        def apply_2b(start, carry):
+            value = sg2[pl.ds(start, STEP), :] - bias_sum * inv_pixels
+            value = scale * (value - z2[pl.ds(start, STEP), :] * (gain_sum * inv_pixels))
+            mgb[pl.ds(start, STEP), :] = value.astype(BF16)
+            return carry
+        rows_loop(group, apply_2b, 0)
+    wait_mid, _ = halo(mgb.at[pl.ds(0, NW)], mgb.at[pl.ds(NW, NW)], None, None, mgr.at[0], mgr.at[1])
+    push(red_last)
+    for a in range(3):
+        for b in range(3):
+            grad = dot_tn(gs[a : a + 2, :, b * 512 : (b + 1) * 512].reshape(2 * NW, 512), mgb[...]).astype(BF16)
+            for qq in range(S):
+                g_mid[qq, 3 * a + b] = grad[:, qq * mw : (qq + 1) * mw].reshape(DZ, 2, wm_in.shape[1], mw)
+    push(red_mid)
+    mgs = gs
+    for r in range(2):
+        spread(mgs, 1 + r, lambda start, r=r: mgb[pl.ds(r * NW + start, STEP), :], True)
+
+    def back_taps(lhs, a):
+        total = dot_nt(lhs[:, 0:512], wm[3 * a].reshape(512, 512))
+        for b in range(1, 3):
+            total = total + dot_nt(lhs[:, b * 512 : (b + 1) * 512], wm[3 * a + b].reshape(512, 512))
+        return total
+
+    gg[...] = back_taps(mgs[1:3].reshape(2 * NW, 1536), 1)
+    gg[0:NW, :] += back_taps(mgs[2], 0)
+    gg[NW : 2 * NW, :] += back_taps(mgs[1], 2)
+    wait_mid()
+    spread(mgs, 0, lambda start: mgr[0, pl.ds(start, STEP), :], True)
+    spread(mgs, 3, lambda start: mgr[1, pl.ds(start, STEP), :], True)
+    gg[0:NW, :] += back_taps(mgs[0], 2)
+    gg[NW : 2 * NW, :] += back_taps(mgs[3], 0)
+
+    def gate_back(i, carry):
+        start = pl.multiple_of(i * STEP, STEP)
+        gate = gt[pl.ds(start, STEP), :]
+        act = jax.nn.silu(gain_1 * z1[pl.ds(start, STEP), :] + bias_1)
+        value = gg[pl.ds(start, STEP), :] * act * gate * (1.0 - gate)
+        fgb[pl.ds(start, STEP), :] = value.astype(BF16)
+        return carry
+
+    lax.fori_loop(0, 2 * NW // STEP, gate_back, 0)
+    cg = dot_nt(fgb[...], we[...].reshape(LANES, 512)).astype(BF16)
+    cg_rows = [cg[r * NW : (r + 1) * NW].astype(F32) for r in range(2)]
+    hg = pair_sum(cg_rows[0] + cg_rows[1]).astype(BF16)
+    for r in range(2):
+        cgx[r, 0] = cg_rows[r].astype(BF16)
+        cgx[r, 1] = hg
+    wait_cg, _ = halo(cgx.at[0], cgx.at[1], None, None, cgr.at[0], cgr.at[1])
+    push(red_last)
+    n_exp = we_in.shape[0]
+    grad = dot_tn(comb[...], fgb[...]).astype(BF16)
+    n_red = wr_in.shape[0]
+    for b in range(4):
+        g_re[:, :, n_red + b * n_exp : n_red + (b + 1) * n_exp, :] = grad[
+            :, b * LANES : (b + 1) * LANES].reshape(DZ, 2, n_exp, LANES)
+    for r in range(2):
+        put_shifts(cgs, 1 + r, cg_rows[r], 1, True)
+    put_shifts(hgs, 1, hg.astype(F32), 2, True)
+    for a in range(3):
+        grad = dot_tn(cs[a : a + 2].reshape(2 * NW, 384), cg).astype(BF16)
+        g_diff[0, 3 * a : 3 * a + 3] = grad.reshape(3, DZ, 2, wd0_in.shape[1], LANES)
+        grad = (0.5 * dot_tn(ps[a], hg)).astype(BF16)
+        g_diff[1, 3 * a : 3 * a + 3] = grad.reshape(3, DZ, 2, wd0_in.shape[1], LANES)
+    push(red_diff)
+    wait_cg()
+    put_shifts(cgs, 0, cgr[0, 0].astype(F32), 1, True)
+    put_shifts(cgs, 3, cgr[1, 0].astype(F32), 1, True)
+    put_shifts(hgs, 0, cgr[0, 1].astype(F32), 2, True)
+    put_shifts(hgs, 2, cgr[1, 1].astype(F32), 2, True)
+    full = jnp.zeros((2 * NW, LANES), F32)
+    half = jnp.zeros((NW, LANES), F32)
+    for a in range(3):
+        for b in range(3):
+            lanes = slice(b * LANES, (b + 1) * LANES)
+            full = full + dot_nt(
+                cgs[2 - a : 4 - a, :, lanes].reshape(2 * NW, LANES), wd[0, 3 * a + b].reshape(LANES, LANES))
+            half = half + dot_nt(hgs[2 - a, :, lanes], wd[1, 3 * a + b].reshape(LANES, LANES))
+    rd[...] = full + 0.25 * jnp.concatenate([half, half], axis=0)
+    for r in range(2):
+        for f in range(NF):
+            here = r * NW + f * 16
+            after = r * NW + ((f + 1) % NF) * 16
+            diff = (keep[f].astype(F32) * rd[here : here + 16, :]
+                    - keep[(f + 1) % NF].astype(F32) * rd[after : after + 16, :])
+            chb[r, f * 16 : f * 16 + 16, :] = diff.astype(BF16)
+    rgb = chb[...].reshape(2 * NW, LANES)
+    sg2[...] = dot_nt(rgb, wr[...].reshape(512, LANES))
+
+    parts = []
+    for group in range(NG):
+        def slope_1(start, carry):
+            normed = z1[pl.ds(start, STEP), :]
+            _, slope = silu_parts(gain_1 * normed + bias_1)
+            value = gg[pl.ds(start, STEP), :] * (1.0 + gt[pl.ds(start, STEP), :]) + sg2[pl.ds(start, STEP), :]
+            value = value * slope
+            sg2[pl.ds(start, STEP), :] = value
+            return carry[0] + fold(value), carry[1] + fold(value * normed)
+        zero = jnp.zeros((8, 512), F32)
+        sums = rows_loop(group, slope_1, (zero, zero))
+        parts += [jnp.sum(item, axis=0, keepdims=True) for item in sums]
+    copies = sp_send(3, parts)
+    g_re[:, :, 0:n_red, :] = dot_tn(fab[...], rgb).astype(BF16).reshape(DZ, 2, n_red, LANES)
+    push(red_rest, red_mid, red_last, red_diff)
+    total = sp_total(3, copies)
+    gain_1_grad = bias_1_grad = jnp.zeros((1, 512), F32)
+    for group in range(NG):
+        row = 2 * group
+        bias_sum, gain_sum = total[row : row + 1], total[row + 1 : row + 2]
+        gain_1_grad, bias_1_grad = gain_1_grad + gain_sum, bias_1_grad + bias_sum
+        scale = gain_1 * inv_1[group]
+
+        def apply_1b(start, carry):
+            value = sg2[pl.ds(start, STEP), :] - bias_sum * inv_pixels
+            value = scale * (value - z1[pl.ds(start, STEP), :] * (gain_sum * inv_pixels))
+            fgb[pl.ds(start, STEP), :] = value.astype(BF16)
+            return carry
+        rows_loop(group, apply_1b, 0)
+
+    for k, copy in enumerate(stem_copies):
+        copy.wait_recv()
+    stem_total = stg[...]
+    for k in range(S - 1):
+        stem_total = stem_total + stgr[k]
+    gain_3_all = jnp.concatenate(gain_3_grad, axis=1)
+    bias_3_all = jnp.concatenate(bias_3_grad, axis=1)
+    for d in range(D):
+        mid_at, last_at = (d // per) * LANES, d * rows_last * LANES
+        rows = [v[:, mid_at : mid_at + LANES] for v in (gain_1_grad, bias_1_grad, gain_2_grad, bias_2_grad)]
+        for v in (gain_3_all, bias_3_all):
+            rows += [v[:, last_at + n * LANES : last_at + (n + 1) * LANES] for n in range(rows_last)]
+        sms[d, 0:8, :] = stem_total[d * 8 : d * 8 + 8]
+        sms[d, 8:16, :] = jnp.concatenate(rows, axis=0)
+    small_back = [
+        remote(sms.at[lax.rem(dp + k, D)], smr.at[k - 1], dp_peers[k - 1]) for k in range(1, D)]
+
+    for n in range(4):
+        grad = dot_tn(x3[:, :, n * 512 : (n + 1) * 512].reshape(2 * NW, 512), fgb[...]).astype(BF16)
+        per_chunk = 512 // (2 * fr)
+        for qq in range(S):
+            g_first[qq, n * per_chunk : (n + 1) * per_chunk] = grad[:, qq * fw : (qq + 1) * fw].reshape(
+                per_chunk, 2, fr, fw)
+    push(red_first, red_rest, red_mid, red_last, red_diff)
+    weights_first = wf[...].reshape(2048, 512)
+    for n in range(4):
+        lo = n * 512
+        free_part()
+        z3[:, lo : lo + 512] = dot_nt(fgb[...], weights_first[lo : lo + 512])
+
+        def apply_in(i, carry):
+            start = pl.multiple_of(i * STEP, STEP)
+            value = z3[pl.ds(start, STEP), lo : lo + 512] + ct_rows(start, lo, 512)
+            ost[n % 2, pl.ds(start // 16, STEP // 16)] = value.astype(BF16).reshape(STEP // 16, 16, 512)
+            return carry
+        lax.fori_loop(0, 2 * NW // STEP, apply_in, 0)
+        store_part(n, ig_hbm)
+    for _ in range(6):
+        push(red_first, red_rest, red_mid, red_last, red_diff)
+
+    assert counters["r"] <= ssem.shape[0] and counters["l"] <= lsem.shape[0], counters
+    wait_video()
+    row8 = lax.broadcasted_iota(jnp.int32, (8, LANES), 0)
+
+    def video_edges(f, carry):
+        for ch in range(3):
+            rows = slice(ch * 8, ch * 8 + 8)
+            from_prev = vgr[0, f, ch * 2 + 1 : ch * 2 + 2, :]
+            from_next = vgr[1, f, ch * 2 : ch * 2 + 1, :]
+            vg_out[f, rows] += jnp.where(row8 == 0, from_prev, jnp.where(row8 == 7, from_next, 0.0))
+        return carry
+
+    lax.fori_loop(0, NF, video_edges, 0)
+    value = sms[dp]
+    for k, copy in enumerate(small_back):
+        copy.wait_recv()
+        value = value + smr[k]
+    osm_out[...] = value
+    for copy in sends:
+        copy.wait_send()
+    for finish in halo_waits:
+        finish()
+    for part in stores[-2:]:
+        for copy in part:
+            copy.wait()
+
+
+def on_device_kernel(
+    clip_video, section_input, keep_mask, w_rgb, w_stem_diff, w_first, w_middle, w_last, w_reduce,
+    w_diff_full, w_diff_half, w_expand, gain_first, bias_first, gain_middle, bias_middle, gain_last,
+    bias_last, stem_cot, section_cot,
+):
+    D, S = lax.axis_size("dp"), lax.axis_size("sp")
+    DZ, SX = D // 2, S // 2
+    NF = clip_video.shape[0]
+    NW = NF * 16
+    dp = lax.axis_index("dp")
+    frames = clip_video.astype(F32)
+    edges = jnp.stack([frames[:, :, 0], frames[:, :, 7]], axis=2).reshape(NF, 6, LANES)
+    uin = jnp.concatenate([frames.reshape(NF, 24, LANES), edges, jnp.zeros((NF, 2, LANES), F32)], axis=1)
+    per = D * LANES // 512
+    width = 512 // D
+    lane = jnp.arange(LANES)
+    stem_w = jnp.concatenate([w_rgb, w_stem_diff], axis=1).astype(F32).transpose(2, 0, 1).reshape(8, 81)
+    stem_w = jnp.pad(stem_w, ((0, 0), (0, LANES - 81)))
+    mids = jnp.stack([gain_first, bias_first, gain_middle, bias_middle]).astype(F32)
+    mids = jnp.where(lane // width == dp % per, jnp.tile(mids, (1, per)), 0.0)
+    lasts = jnp.concatenate([gain_last, bias_last]).astype(F32).reshape(-1, LANES)
+    small = jnp.concatenate([stem_w, mids, lasts], axis=0)
+    band = jnp.asarray(band_table(8), BF16)
+    fr, fw = w_first.shape[0], 512 // S
+    mr, lr, rr = w_middle.shape[1], w_last.shape[0], w_reduce.shape[0]
+    dr, er = w_diff_full.shape[1], w_expand.shape[0]
+    lw = 2048 // S
+    shape = jax.ShapeDtypeStruct
+    vm = pltpu.VMEM
+    any_spec = pl.BlockSpec(memory_space=pl.ANY)
+    vmem_spec = pl.BlockSpec(memory_space=pltpu.VMEM)
+    n_rem, n_loc = 420, 64
+    re_rows = rr + 4 * er
+    scratch = [
+        pltpu.SemaphoreType.DMA((n_rem,)), pltpu.SemaphoreType.DMA((n_rem,)), pltpu.SemaphoreType.DMA((n_loc,)),
+        vm((DZ, 2, fr, 512), BF16), vm((9, DZ, 2, mr, 512), BF16), vm((DZ, 2, lr, 2048), BF16),
+        vm((DZ, 2, rr, LANES), BF16), vm((2, 9, DZ, 2, dr, LANES), BF16), vm((DZ, 2, er, 512), BF16),
+        vm((2 * NF, 16, 2048), BF16), vm((2 * NF, 16, 2048), BF16),
+        vm((2 * PART, 512, LANES), BF16), vm((2 * PART, 512, LANES), BF16),
+        vm((NF, 32, LANES), F32), vm((NF, 8, LANES), F32), vm((NF, 8, LANES), F32),
+        vm((D, 16, LANES), F32), vm((512, 288), BF16), vm((3, 512, LANES), F32), vm((288, 512), BF16),
+        vm((NF, 96, LANES), F32),
+        vm((NF, 8, LANES), F32), vm((2, NF, 8, LANES), F32), vm((D * 8, LANES), F32), vm((S - 1, D * 8, LANES), F32),
+        vm((4, 8, 512), F32), vm((4, S - 1, 8, 512), F32), vm((4, 8, 512), F32), vm((4, S - 1, 8, 512), F32),
+        vm((2 * NW, 512), F32), vm((2 * NW, 512), BF16), vm((2 * NW, 512), F32),
+        vm((2 * NW, LANES), F32), vm((2, NW, LANES), BF16), vm((2, 2, NW, LANES), BF16),
+        vm((4, NW, 384), BF16), vm((3, NW, 384), BF16), vm((2 * NW, LANES), BF16),
+        vm((2 * NW, 512), BF16), vm((2, NW, 512), BF16), vm((4, NW, 1536), BF16),
+        vm((2 * NW, 512), F32), vm((2 * NW, 512), BF16), vm((2 * NW, 2048), F32), vm((2 * NW, 2048), BF16),
+        vm((2, 2, NW, LANES), BF16), vm((2, 2, NW, LANES), BF16),
+        vm((4, NW, 384), BF16), vm((3, NW, 384), BF16), vm((2 * NW, 512), BF16), vm((2, 2 * NF, 16, 512), BF16),
+        vm((S, DZ, 2, fr, fw), BF16), vm((S, 9, DZ, 2, mr, fw), BF16), vm((S, DZ, 2, lr, lw), BF16),
+        vm((2, 9, DZ, 2, dr, LANES), BF16), vm((DZ, 2, re_rows, LANES), BF16),
+        vm((SX, DZ, 2, fr, fw), BF16), vm((SX - 1, DZ, 2, fr, fw), BF16), vm((DZ, fr, fw), BF16),
+        vm((DZ - 1, fr, fw), BF16),
+        vm((SX, 9, DZ, 2, mr, fw), BF16), vm((SX - 1, 9, DZ, 2, mr, fw), BF16), vm((9, DZ, mr, fw), BF16),
+        vm((DZ - 1, 9, mr, fw), BF16),
+        vm((SX, DZ, 2, lr, lw), BF16), vm((SX - 1, DZ, 2, lr, lw), BF16), vm((DZ, lr, lw), BF16),
+        vm((DZ - 1, lr, lw), BF16),
+        vm((9, DZ, 2, dr, LANES), BF16), vm((9, DZ, dr, LANES), BF16), vm((DZ - 1, 9, dr, LANES), BF16),
+        vm((9, dr, LANES), F32), vm((SX - 1, 9, dr, LANES), F32), vm((2, 9, dr, LANES), F32),
+        vm((DZ, 2, re_rows, LANES), BF16), vm((DZ, re_rows, LANES), BF16), vm((DZ - 1, re_rows, LANES), BF16),
+        vm((re_rows, LANES), F32), vm((SX - 1, re_rows, LANES), F32),
+        vm((S, fr, fw), BF16), vm((S, 9, mr, fw), BF16), vm((S, lr, lw), BF16),
+        vm((D, 16, LANES), F32), vm((D - 1, 16, LANES), F32),
+    ]
+    outs = pl.pallas_call(
+        functools.partial(whole_kernel, (D, S, NF)),
+        out_shape=(
+            shape((NF, 512, LANES), BF16), shape((NF, 24, LANES), F32),
+            shape(section_input.shape, BF16), shape(section_input.shape, BF16),
+            shape((fr, 512), F32), shape((9, mr, 512), F32), shape((lr, 2048), F32), shape((rr, LANES), F32),
+            shape((2, 9, dr, LANES), F32), shape((er, 512), F32), shape((16, LANES), F32),
+        ),
+        in_specs=[pl.BlockSpec(memory_space=pltpu.SMEM)] + [vmem_spec] * 3 + [any_spec] * 10,
+        out_specs=(any_spec, vmem_spec, any_spec, any_spec) + (vmem_spec,) * 7,
+        scratch_shapes=scratch,
+        compiler_params=pltpu.CompilerParams(
+            collective_id=0, has_side_effects=True, vmem_limit_bytes=VMEM_BYTES),
+        name="tdn_blocks",
+    )(
+        keep_mask, uin, small, band, section_input, section_cot, stem_cot.reshape(NF, 512, LANES),
+        w_first, w_middle, w_last, w_reduce, w_diff_full, w_diff_half, w_expand,
+    )
+    so, vg, section_output, input_grad, g_first, g_mid, g_last, g_red, g_diff, g_exp, g_small = outs
+    stem = g_small[0:8, 0:81].reshape(8, 9, 9).transpose(1, 2, 0)
+    mids = lax.dynamic_slice_in_dim(g_small[8:12], (dp % per) * width, width, axis=1)
+    rows_last = 2048 // D // LANES
+    lasts = g_small[12 : 12 + 2 * rows_last].reshape(2, rows_last * LANES)
+    return (
+        so.reshape(stem_cot.shape), vg.reshape(clip_video.shape), section_output, input_grad,
+        stem[:, 0:3], stem[:, 3:9], g_first, g_mid, g_last, g_red, g_diff[0], g_diff[1], g_exp,
+        mids[0], mids[1], mids[2], mids[3], lasts[0], lasts[1],
+    )
+
+
+def fits_kernel(mesh):
+    dp_count, sp_count = mesh.shape["dp"], mesh.shape["sp"]
+    return (
+        dp_count % 2 == 0 and sp_count % 2 == 0 and H5 == 2 * sp_count and HS == 8 * sp_count
+        and TDM_C % (16 * dp_count) == 0 and STEM_C == 8 * dp_count and MID // sp_count % LANES == 0
+        and C5 // dp_count % LANES == 0
+    )
+
+
 def solution(mesh):
     placed = (
         P("dp", None, "sp", None),
@@ -432,7 +1552,7 @@
         P("dp", "sp", None, None),
     )
     return jax.shard_map(
-        on_device,
+        on_device_kernel if fits_kernel(mesh) else on_device,
         mesh=mesh,
         in_specs=placed,
         out_specs=(

time: 1740 us -> 219 us (0.13)
  waiting for transfers between devices: 946 us -> 0 us
  blocking collectives: 332 us -> 0 us
  matrix products: 242 us -> 0 us
  Pallas kernels: 0 us -> 195 us
  other arithmetic: 75.5 us -> 4.46 us
  starting transfers between devices: 63 us -> 0 us
  local copies, waits for them, and re-layouts: 49.4 us -> 18.5 us
  between operations: 21.3 us -> 0.74 us
    reduce_scatter x16 -> x0, waiting for transfers between devices: 892 us -> none  [the longest x2 329 us: reduce_grads(): lax.psum_scatter(grads[3], 'dp', scatter_dimension=1, tiled=True)]
    dot_general x294 -> x0, matrix products: 242 us -> none  [the longest x90 100 us: tap_conv(): jnp.einsum(einsum_form, window, kernel[tap_index], preferred_element_type...]
    all_gather x8 -> x0, blocking collectives: 219 us -> none  [the longest x1 33.4 us: on_device(): lax.all_gather(w_reduce, 'dp', axis=0, tiled=True)]
    pallas_call x0 -> x1, Pallas kernels: none -> 195 us  [on_device_kernel(): pl.pallas_call(functools.partial(whole_kernel, (D, S, NF)), out_shape=(sh...]
    ppermute x24 -> x0, starting transfers between devices: 61.9 us -> none  [the longest x12 46.3 us: with_halo(): lax.ppermute(lax.slice_in_dim(block, block.shape[dim] - width, None, axis...]
    unnamed x2 -> x0, blocking collectives: 58.7 us -> none
    psum x6 -> x0, blocking collectives: 54.2 us -> none  [the longest x3 29.2 us: norm_forward(): total_sum, total_square = lax.psum((local_sums[0], local_sums[1]), 'sp')]
    psum x2 -> x0, waiting for transfers between devices: 52.2 us -> none  [the longest x1 52.2 us: reduce_grads(): lax.psum(summed[2].astype(jnp.bfloat16), 'sp').astype(jnp.float32)]
  transfers between devices with their start and end apart: 45 -> 0, of which waited for: 13 -> 0; matrix products, arithmetic and copies ran while one was open for 20% -> 0% of each run, Pallas kernels for 0% -> 0%
where the time goes in v1:
time: 219 us
  Pallas kernels  195 us (89%)
  local copies, waits for them, and re-layouts  18.5 us (8%)
  other arithmetic  4.46 us (2%)
    pallas_call x1, Pallas kernels, on_device_kernel(): pl.pallas_call(functools.partial(whole_kernel, (D, S, NF)), out_shape=(sh...  195 us
    unnamed x27, local copies, waits for them, and re-layouts  13 us

profile of v1, /device:TPU:0, one launch (start us, length us, event | category | flops | bytes accessed | tf_op | source)
XLA Modules:
  0.0 218.7 jit_solution(5823949737688471019)
XLA Ops:
  0.7 0.9 copy_convert_fusion
  1.6 0.1 copy.50
  1.7 0.1 pad.22.clone
  1.8 0.8 maximum_maximum_fusion.uin
  2.6 0.7 maximum_convert_fusion.1
  3.3 0.7 maximum_convert_fusion
  4.0 0.1 tile.10
  4.1 0.7 maximum_bitcast_fusion
  4.8 0.1 copy.45
  4.9 0.1 reshape.106
  5.1 0.6 pad_maximum_fusion.1.small
  5.7 195.0 %tdn_blocks.1 = (bf16[16,512,128]{2,1,0:T(8,128)(2,1)}, f32[16,24,128]{2,1,0:T(8,128)}, bf16[16,2,16,2048]{3,2,1,0:T(8,128)(2,1)}, bf16[16,2,16,2048]{3,2,1,0:T(...) custom-call(s32[16]{0:T(128)} %keep.1, ...), custom_call_target="tpu_custom_call" | custom-call | tf_op jit(solution)/shard_map/tdn_blocks/pallas_call | solution.py:1492
  200.6 0.7 slice.49
  201.3 0.1 reshape.110
  201.4 0.7 copy.46
  202.1 0.1 slice.64
  202.2 0.7 copy.47
  202.9 1.6 slice_bitcast_fusion
  204.5 0.7 slice.54
  205.2 0.1 constant_dynamic-slice_fusion
  205.3 0.5 slice_bitcast_fusion.4
  205.8 1.3 slice_bitcast_fusion.2
  207.1 0.0 copy-start.5
  207.1 0.0 copy-start.1
  207.1 3.3 %copy.60 = bf16[16,64,8,128]{3,2,1,0:T(8,128)(2,1)} copy(bf16[16,64,8,128]{3,2,1,0:T(8,128)(2,1)} %bitcast.33) | data formatting | bytes 4194304
  210.4 0.0 copy-done.5
  210.4 0.7 copy.61
  211.1 0.0 copy-done.1
  211.1 0.0 copy-start
  211.1 1.3 copy.62
  212.4 1.0 copy-done
  213.4 0.0 copy-start.4
  213.4 0.0 copy-start.2
  213.4 1.3 copy.63
  214.8 0.1 copy-done.4
  214.8 0.0 copy-start.3
  214.8 0.0 copy-start.7
  214.8 0.0 copy-start.6
  214.8 0.8 copy.64
  215.6 0.0 copy-done.2
  215.6 1.0 copy.65
  216.6 0.0 copy-done.3
  216.6 0.8 copy.66
  217.4 0.0 copy-done.7
  217.4 0.6 copy.67
  218.1 0.0 copy-done.6
  218.1 0.6 copy.68
  (8 shorter events, 0.1 us)
Async XLA Ops:
  207.1 3.3 %copy-start.5 = (f32[16,24,128]{2,1,0:T(8,128)S(1)}, f32[16,24,128]{2,1,0:T(8,128)}, u32[]{:S(2)}) copy-start(f32[16,24,128]{2,1,0:T(8,128)} %get-tuple-element.31) | copy-start | bytes 589828
  207.1 3.9 %copy-start.1 = (bf16[16,2,16,2048]{3,2,1,0:T(8,128)(2,1)S(1)}, bf16[16,2,16,2048]{3,2,1,0:T(8,128)(2,1)}, u32[]{:S(2)}) copy-start(bf16[16,2,16,2048]{3,2,1,0:T(8,128)(2,1)} %get-tuple-element.91) | copy-start | bytes 6291460
  211.1 2.3 %copy-start = (bf16[16,2,16,2048]{3,2,1,0:T(8,128)(2,1)S(1)}, bf16[16,2,16,2048]{3,2,1,0:T(8,128)(2,1)}, u32[]{:S(2)}) copy-start(bf16[16,2,16,2048]{3,2,1,0:T(8,128)(2,1)} %get-tuple-element.92) | copy-start | bytes 6291460
  213.4 1.4 copy-start.4
  213.4 2.2 %copy-start.2 = (f32[9,64,512]{2,1,0:T(8,128)S(1)}, f32[9,64,512]{2,1,0:T(8,128)}, u32[]{:S(2)}) copy-start(f32[9,64,512]{2,1,0:T(8,128)} %get-tuple-element.96) | copy-start | bytes 3538948
  214.8 1.8 copy-start.3
  214.8 2.6 %copy-start.7 = (f32[64,128]{1,0:T(8,128)S(1)}, f32[64,128]{1,0:T(8,128)}, u32[]{:S(2)}) copy-start(f32[64,128]{1,0:T(8,128)} %get-tuple-element.98) | copy-start | bytes 98308
  214.8 3.2 %copy-start.6 = (f32[16,512]{1,0:T(8,128)S(1)}, f32[16,512]{1,0:T(8,128)}, u32[]{:S(2)}) copy-start(f32[16,512]{1,0:T(8,128)} %get-tuple-element.101) | copy-start | bytes 98308

commit v2 on v1

--- a/solution.py
+++ b/solution.py
@@ -480,12 +480,11 @@
 
 def whole_kernel(
     sizes, keep, uin, small, band, x_hbm, ct_hbm, sc_hbm, wf_in, wm_in, wl_in, wr_in, wd0_in, wd1_in, we_in,
-    so_hbm, vg_out, out_hbm, ig_hbm, of_out, om_out, ol_out, or_out, od_out, oe_out, osm_out,
+    so_hbm, vg_out, out_hbm, ig_hbm, fbf_hbm, fbm_hbm, fbl_hbm, or_out, od_out, oe_out, osm_out,
     ssem, rsem, lsem, wf, wm, wl, wr, wd, we, x3, ct3, sc, so, ust, uprev, unext, sm, tf, tff, tb, dg,
     vgh, vgr, stg, stgr, stat_s, stat_r, st3_s, st3_r, z1, fab, gt, rd, chb, chr_, cs, ps, comb,
     gb, gr, gs, z2, sab, z3, lgb, cgx, cgr, cgs, hgs, fgb, ost,
-    g_first, g_mid, g_last, g_diff, g_re, rcf, rxf, ryf, rzf, rcm, rxm, rym, rzm, rcl, rxl, ryl, rzl,
-    rcd, ryd, rzd, fdx, rxd, fdo, rcr, ryr, rzr, frx, rxr, fbf, fbm, fbl, sms, smr,
+    g_first, g_mid, g_last, g_diff, g_re, rcd, ryd, rzd, fdx, rxd, fdo, rcr, ryr, rzr, frx, rxr, fbf, fbm, fbl, sms, smr, *bufs,
 ):
     D, S, NF = sizes
     DZ, SX = D // 2, S // 2
@@ -527,16 +526,35 @@
     counters = {"r": 0, "l": 0}
     sends = []
 
-    def remote(src, dst, dev):
+    def bundle(whole):
         i = counters["r"]
         counters["r"] += 1
-        copy = pltpu.make_async_remote_copy(
-            src_ref=src, dst_ref=dst, send_sem=ssem.at[i], recv_sem=rsem.at[i],
-            device_id=dev, device_id_type=MESH_ID,
-        )
-        copy.start()
-        sends.append(copy)
-        return copy
+
+        def start(src, dst, dev):
+            pltpu.make_async_remote_copy(
+                src_ref=src, dst_ref=dst, send_sem=ssem.at[i], recv_sem=rsem.at[i],
+                device_id=dev, device_id_type=MESH_ID,
+            ).start()
+
+        def wait():
+            pltpu.make_async_copy(whole, whole, rsem.at[i]).wait()
+
+        def finish():
+            pltpu.make_async_copy(whole, whole, ssem.at[i]).wait()
+
+        sends.append(finish)
+        return start, wait
+
+    def remote(src, dst, dev):
+        start, wait = bundle(dst)
+        start(src, dst, dev)
+        return wait
+
+    def to_peers(src, dst_of, peers, whole):
+        start, wait = bundle(whole)
+        for k, peer in enumerate(peers):
+            start(src, dst_of(k), peer)
+        return wait
 
     def local(src, dst):
         i = counters["l"]
@@ -566,9 +584,8 @@
         pl.semaphore_signal(barrier, inc=1, device_id=peer, device_id_type=MESH_ID)
     own_small = local(small, sm.at[dp])
     own = [
-        local(wf_in, wf.at[z, y]), local(wd0_in, wd.at[0, :, z, y]), local(wd1_in, wd.at[1, :, z, y]),
-        local(wr_in, wr.at[z, y]), local(we_in, we.at[z, y]), local(wm_in, wm.at[:, z, y]),
-        local(wl_in, wl.at[z, y]),
+        local(wf_in, wf.at[dp]), local(wd0_in, wd.at[0, :, dp]), local(wd1_in, wd.at[1, :, dp]),
+        local(wr_in, wr.at[dp]), local(we_in, we.at[dp]), local(wm_in, wm.at[:, dp]), local(wl_in, wl.at[dp]),
     ]
 
     def load_cot(part):
@@ -625,87 +642,103 @@
         halo_waits.append(finish)
         return wait, finish
 
-    small_copies = [remote(small, sm.at[dp], peer) for peer in dp_peers]
+    wait_small = to_peers(small, lambda k: sm.at[dp], dp_peers, sm.at[pl.ds(0, D - 1)])
     edge = uin.at[:, pl.ds(24, 8)]
     wait_edges, _ = halo(edge, edge, None, None, uprev, unext)
 
     def gather(mode, src, dst):
-        piece = q_own if mode == "A" else c
-        zs = [remote(src(piece), dst(z, y, piece), at_zy(z_to(k), y)) for k in range(1, DZ)]
-        ys = [remote(src(piece), dst(z, y, piece), y_peer)]
+        wide = {"A": 1, "B": SX, "D": S}[mode]
+        first_q = {"A": q_own, "B": c * SX, "D": 0}[mode]
+        only = pl.ds(dp, 1)
+        z_start, z_wait = bundle(dst(pl.ds(0, DZ - 1), first_q, wide))
+        y_start, y_wait = bundle(dst(pl.ds(0, DZ), first_q, wide))
+        if mode == "A":
+            x_start, x_wait = bundle(dst(pl.ds(0, (D - 1) * (SX - 1)), first_q, 1))
+        if mode != "D":
+            c_start, c_wait = bundle(dst(pl.ds(0, D - 1), c * SX, SX))
+        for k in range(1, DZ):
+            z_start(src(first_q, wide), dst(only, first_q, wide), at_zy(z_to(k), y))
+        y_start(src(first_q, wide), dst(only, first_q, wide), y_peer)
         yield
-        xs, cores = [], []
-
-        def fan(zz, yy):
-            part = dst(zz, yy, piece)
+
+        def fan(d):
+            part = dst(d, first_q, wide)
             if mode == "A":
                 for k in range(1, SX):
-                    xs.append((zz, yy, k, remote(part, part, x_peer(k))))
+                    x_start(part, part, x_peer(k))
             if mode != "D":
-                cores.append(remote(part, part, c_peer))
-
+                c_start(part, part, c_peer)
+
+        z_wait()
         for k in range(1, DZ):
-            zs[k - 1].wait_recv()
-            part = dst(z_from(k), y, piece)
-            ys.append(remote(part, part, y_peer))
-            fan(z_from(k), y)
+            d = pl.ds(z_from(k) * 2 + y, 1)
+            y_start(dst(d, first_q, wide), dst(d, first_q, wide), y_peer)
+            fan(d)
         yield
+        y_wait()
         for k in range(DZ):
-            ys[k].wait_recv()
-            fan(z_from(k), oy)
+            fan(pl.ds(z_from(k) * 2 + oy, 1))
         yield
-        for zz, yy, k, copy in xs:
-            copy.wait_recv()
-            part = dst(zz, yy, c * SX + x_from(k))
-            cores.append(remote(part, part, c_peer))
-        yield
-        for copy in cores:
-            copy.wait_recv()
-
-    def lane_block(index, width):
-        return pl.ds(pl.multiple_of(index * width, width), width)
+        if mode == "A":
+            x_wait()
+            for k in range(1, SX):
+                for n in range(1, D):
+                    part = dst(pl.ds(lax.rem(dp + n, D), 1), c * SX + x_from(k), 1)
+                    c_start(part, part, c_peer)
+            yield
+        if mode != "D":
+            c_wait()
+
+    def lane_block(index, width, count):
+        return pl.ds(pl.multiple_of(index * width, width), width * count)
 
     fr, fw = wf_in.shape[0], wf_in.shape[1] // S
     mw = wm_in.shape[2] // S
     lr, lw = wl_in.shape[0], wl_in.shape[1] // S
 
-    def first_part(lo, n):
-        return gather("A", lambda q: wf_in.at[pl.ds(lo, n), lane_block(q, fw)],
-                      lambda zz, yy, q: wf.at[zz, yy, pl.ds(lo, n), lane_block(q, fw)])
-
-    def mid_part(lo, n):
-        return gather("A", lambda q: wm_in.at[pl.ds(lo, n), :, lane_block(q, mw)],
-                      lambda zz, yy, q: wm.at[pl.ds(lo, n), zz, yy, :, lane_block(q, mw)])
-
-    def last_part(lo, n):
-        return gather("A", lambda q: wl_in.at[pl.ds(lo, n), lane_block(q, lw)],
-                      lambda zz, yy, q: wl.at[zz, yy, pl.ds(lo, n), lane_block(q, lw)])
+    def first_part(mode, lo, n):
+        rows = pl.ds(lo, n)
+        return gather(mode, lambda q, w: wf.at[pl.ds(dp, 1), rows, lane_block(q, fw, w)],
+                      lambda d, q, w: wf.at[d, rows, lane_block(q, fw, w)])
+
+    def mid_part(mode, lo, n):
+        rows = pl.ds(lo, n)
+        return gather(mode, lambda q, w: wm.at[rows, pl.ds(dp, 1), :, lane_block(q, mw, w)],
+                      lambda d, q, w: wm.at[rows, d, :, lane_block(q, mw, w)])
+
+    def last_part(mode, lo, n):
+        rows = pl.ds(lo, n)
+        return gather(mode, lambda q, w: wl.at[pl.ds(dp, 1), rows, lane_block(q, lw, w)],
+                      lambda d, q, w: wl.at[d, rows, lane_block(q, lw, w)])
 
     for copy in own:
         copy.wait()
+    part_b = fr * 3 // 8
+    part_a = (fr - part_b) // 2
     chunks = [
-        first_part(0, fr // 2),
-        first_part(fr // 2, fr // 2),
-        gather("D", lambda q: wr_in, lambda zz, yy, q: wr.at[zz, yy]),
-        gather("B", lambda q: wd.at[q, :, z, y], lambda zz, yy, q: wd.at[q, :, zz, yy]),
-        gather("D", lambda q: we_in, lambda zz, yy, q: we.at[zz, yy]),
-        mid_part(0, 3), mid_part(3, 3), mid_part(6, 3),
-        last_part(0, lr // 2), last_part(lr // 2, lr // 2),
+        (0, first_part("A", 0, part_a)),
+        (0, first_part("B", 2 * part_a, part_b)),
+        (0, first_part("A", part_a, part_a)),
+        (1, gather("D", lambda q, w: wr.at[pl.ds(dp, 1)], lambda d, q, w: wr.at[d])),
+        (1, gather("B", lambda q, w: wd.at[c, :, pl.ds(dp, 1)], lambda d, q, w: wd.at[c, :, d])),
+        (1, gather("D", lambda q, w: we.at[pl.ds(dp, 1)], lambda d, q, w: we.at[d])),
+        (1, mid_part("A", 0, 3)), (2, mid_part("B", 6, 3)), (2, mid_part("A", 3, 3)),
+        (3, last_part("A", 0, lr // 2)), (3, last_part("B", lr // 2, lr // 4)),
+        (4, last_part("A", lr * 3 // 4, lr // 4)),
     ]
-    slot_of = [0, 1, 2, 2, 2, 3, 4, 5, 6, 7]
     slot = [0]
 
-    def pump():
-        for start, chunk in zip(slot_of, chunks):
-            if start <= slot[0]:
-                next(chunk, None)
-        slot[0] += 1
+    def pump(count=1):
+        for _ in range(count):
+            for start, chunk in chunks:
+                if start <= slot[0]:
+                    next(chunk, None)
+            slot[0] += 1
 
     pump()
 
     own_small.wait()
-    for copy in small_copies:
-        copy.wait_recv()
+    wait_small()
     wt = sm[:, 0:8, :].reshape(D * 8, LANES)[:, 0:96].astype(BF16)
     for i in range(8):
         rows = dot_nn(wt, band[i])
@@ -780,7 +813,8 @@
         store_so.append(local(so.at[pl.ds(lo % (2 * PART), PART)], so_hbm.at[pl.ds(lo, PART)]))
         if part + 2 < NF // PART:
             load_sc.append(load_cot(part + 2))
-        pump()
+        if part % 2:
+            pump()
     for copy in store_so[-2:]:
         copy.wait()
 
@@ -806,9 +840,7 @@
             table = band[i, :, n * LANES : (n + 1) * LANES]
             stem_grad = stem_grad + dot_nt(high, table) + dot_nt(low, table)
     stg[...] = jnp.concatenate([stem_grad, jnp.zeros((D * 8, LANES - 96), F32)], axis=1)
-    stem_copies = [remote(stg, stgr.at[k], peer) for k, peer in enumerate(sp_peers)]
-    pump()
-    pump()
+    wait_stem = to_peers(stg, lambda k: stgr.at[k], sp_peers, stgr)
 
     def rows_loop(group, fn, init):
         def body(i, carry):
@@ -823,12 +855,12 @@
         width = parts[0].shape[1]
         fill = [jnp.zeros((8 - len(parts), width), F32)] if len(parts) < 8 else []
         stat_s[i] = jnp.concatenate(parts + fill, axis=0)
-        return [remote(stat_s.at[i], stat_r.at[i, k], peer) for k, peer in enumerate(sp_peers)]
-
-    def sp_total(i, copies):
+        return to_peers(stat_s.at[i], lambda k: stat_r.at[i, k], sp_peers, stat_r.at[i])
+
+    def sp_total(i, wait):
+        wait()
         total = stat_s[i]
-        for k, copy in enumerate(copies):
-            copy.wait_recv()
+        for k in range(S - 1):
             total = total + stat_r[i, k]
         return total
 
@@ -855,7 +887,7 @@
         copy.wait()
     xs = x3[...].reshape(2 * NW, x3.shape[2])
     for n in range(2):
-        z1[:, n * 256 : (n + 1) * 256] = dot_nn(xs, wf[:, :, :, n * 256 : (n + 1) * 256].reshape(x3.shape[2], 256))
+        z1[:, n * 256 : (n + 1) * 256] = dot_nn(xs, wf[:, :, n * 256 : (n + 1) * 256].reshape(x3.shape[2], 256))
     copies = sp_send(0, two_sums(z1))
     pump()
     total = sp_total(0, copies)
@@ -939,10 +971,6 @@
 
     for r in range(2):
         spread(gs, 1 + r, lambda start, r=r: gb[pl.ds(r * NW + start, STEP), :], False)
-    pump()
-    pump()
-    pump()
-    pump()
 
     def taps_of(a):
         return wm[3 * a : 3 * a + 3].reshape(1536, 512)
@@ -956,6 +984,7 @@
     z2[0:NW, :] += dot_nn(gs[0], taps_of(0))
     z2[NW : 2 * NW, :] += dot_nn(gs[3], taps_of(2))
     copies = sp_send(1, two_sums(z2))
+    pump(2)
     for copy in load_ct:
         copy.wait()
     total = sp_total(1, copies)
@@ -980,7 +1009,7 @@
     last_copies = []
     for n in range(4):
         lo = n * 512
-        z3[:, lo : lo + 512] = dot_nn(sab[...], wl[:, :, :, lo : lo + 512].reshape(512, 512))
+        z3[:, lo : lo + 512] = dot_nn(sab[...], wl[:, :, lo : lo + 512].reshape(512, 512))
         parts = []
         for group in range(NG):
             def add_3(start, carry):
@@ -992,8 +1021,7 @@
             sums = rows_loop(group, add_3, (zero, zero, zero, zero))
             parts += [jnp.sum(item, axis=0, keepdims=True) for item in sums]
         st3_s[n] = jnp.concatenate(parts, axis=0)
-        last_copies.append(
-            [remote(st3_s.at[n], st3_r.at[n, k], peer) for k, peer in enumerate(sp_peers)])
+        last_copies.append(to_peers(st3_s.at[n], lambda k, n=n: st3_r.at[n, k], sp_peers, st3_r.at[n]))
     gain_3_grad, bias_3_grad = [], []
     stores = []
 
@@ -1008,9 +1036,9 @@
     for n in range(4):
         lo = n * 512
         free_part()
+        last_copies[n]()
         total = st3_s[n]
-        for k, copy in enumerate(last_copies[n]):
-            copy.wait_recv()
+        for k in range(S - 1):
             total = total + st3_r[n, k]
         gain, bias = gain_3[:, lo : lo + 512], bias_3[:, lo : lo + 512]
         gain_sum = bias_sum = jnp.zeros((1, 512), F32)
@@ -1042,72 +1070,163 @@
             return carry
         lax.fori_loop(0, count, body, 0)
 
-    def reduce_wide(grad, rc, rx, ry, rz, fb, taps, put):
+    def wide_first(grad, lo, n, order, rc, rx, ry, rz, fb):
+        rows = pl.ds(lo, n)
+        half = pl.ds(c * SX, SX)
         mine = q_own
 
-        def lead(ref, head, t, tail):
-            return ref.at[head + ((t,) if taps else ()) + tail]
-
-        rows_n = taps if taps else 1
-        got = remote(grad.at[pl.ds(oc * SX, SX)], rc, c_peer)
+        def add(dst, *others):
+            value = dst[...].astype(F32)
+            for other in others:
+                value = value + other[...].astype(F32)
+            dst[...] = value.astype(BF16)
+
+        wait = remote(grad.at[pl.ds(oc * SX, SX), :, :, rows], rc, c_peer)
         yield
-        got.wait_recv()
-        for xx in range(SX):
-            def add_c(i):
+        wait()
+
+        def add_c(i):
+            for xx in range(SX):
+                for yy in range(2):
+                    add(grad.at[c * SX + xx, i, yy, rows], rc.at[xx, i, yy])
+        each(DZ, add_c)
+        if order == "xyz":
+            start, wait = bundle(rx)
+            for k in range(1, SX):
+                start(grad.at[c * SX + x_to(k), :, :, rows], rx.at[k - 1], x_peer(k))
+            yield
+            wait()
+
+            def add_x(i):
+                for yy in range(2):
+                    add(grad.at[mine, i, yy, rows], *[rx.at[k, i, yy] for k in range(SX - 1)])
+            each(DZ, add_x)
+            wait = remote(grad.at[mine, :, oy, rows], ry, y_peer)
+            yield
+            wait()
+            each(DZ, lambda i: add(grad.at[mine, i, y, rows], ry.at[i]))
+            start, wait = bundle(rz)
+            for k in range(1, DZ):
+                start(grad.at[mine, z_to(k), y, rows], rz.at[k - 1], at_zy(z_to(k), y))
+            yield
+            wait()
+            parts = [rz.at[k] for k in range(DZ - 1)]
+        else:
+            wait = remote(grad.at[half, :, oy, rows], ry, y_peer)
+            yield
+            wait()
+
+            def add_y(i):
+                for xx in range(SX):
+                    add(grad.at[c * SX + xx, i, y, rows], ry.at[xx, i])
+            each(DZ, add_y)
+            start, wait = bundle(rz)
+            for k in range(1, DZ):
+                start(grad.at[half, z_to(k), y, rows], rz.at[k - 1], at_zy(z_to(k), y))
+            yield
+            wait()
+            for xx in range(SX):
+                add(grad.at[c * SX + xx, z, y, rows], *[rz.at[k, xx] for k in range(DZ - 1)])
+            start, wait = bundle(rx)
+            for k in range(1, SX):
+                start(grad.at[c * SX + x_to(k), z, y, rows], rx.at[k - 1], x_peer(k))
+            yield
+            wait()
+            parts = [rx.at[k] for k in range(SX - 1)]
+        value = grad[mine, z, y, rows].astype(F32)
+        for part in parts:
+            value = value + part[...].astype(F32)
+        fb[mine, rows] = value.astype(BF16)
+        done = fb.at[mine, rows]
+        wait = to_peers(done, lambda k: done, sp_peers, fb.at[pl.ds(0, S - 1), rows])
+        yield
+        wait()
+
+    def wide_mid(grad, lo, n, order, rc, rx, ry, rz, fb):
+        taps = pl.ds(lo, n)
+        half = pl.ds(c * SX, SX)
+        mine = q_own
+
+        def add(dst, *others):
+            value = dst[...].astype(F32)
+            for other in others:
+                value = value + other[...].astype(F32)
+            dst[...] = value.astype(BF16)
+
+        wait = remote(grad.at[pl.ds(oc * SX, SX), taps], rc, c_peer)
+        yield
+        wait()
+
+        def add_c(i):
+            t, zz = i // DZ, i % DZ
+            for xx in range(SX):
+                add(grad.at[c * SX + xx, lo + t, zz], rc.at[xx, t, zz])
+        each(n * DZ, add_c)
+        if order == "xyz":
+            start, wait = bundle(rx)
+            for k in range(1, SX):
+                start(grad.at[c * SX + x_to(k), taps], rx.at[k - 1], x_peer(k))
+            yield
+            wait()
+
+            def add_x(i):
                 t, zz = i // DZ, i % DZ
-                for yy in range(2):
-                    dst = lead(grad, (c * SX + xx,), t, (zz, yy))
-                    src = lead(rc, (xx,), t, (zz, yy))
-                    dst[...] = (dst[...].astype(F32) + src[...].astype(F32)).astype(BF16)
-            each(rows_n * DZ, add_c)
-        got = [remote(grad.at[c * SX + x_to(k)], rx.at[k - 1], x_peer(k)) for k in range(1, SX)]
+                add(grad.at[mine, lo + t, zz], *[rx.at[k, t, zz] for k in range(SX - 1)])
+            each(n * DZ, add_x)
+            wait = remote(grad.at[mine, taps, :, oy], ry, y_peer)
+            yield
+            wait()
+
+            def add_y(i):
+                t, zz = i // DZ, i % DZ
+                add(grad.at[mine, lo + t, zz, y], ry.at[t, zz])
+            each(n * DZ, add_y)
+            start, wait = bundle(rz)
+            for k in range(1, DZ):
+                start(grad.at[mine, taps, z_to(k), y], rz.at[k - 1], at_zy(z_to(k), y))
+            yield
+            wait()
+            parts = [rz.at[k] for k in range(DZ - 1)]
+        else:
+            wait = remote(grad.at[half, taps, :, oy], ry, y_peer)
+            yield
+            wait()
+
+            def add_y(i):
+                t, zz = i // DZ, i % DZ
+                for xx in range(SX):
+                    add(grad.at[c * SX + xx, lo + t, zz, y], ry.at[xx, t, zz])
+            each(n * DZ, add_y)
+            start, wait = bundle(rz)
+            for k in range(1, DZ):
+                start(grad.at[half, taps, z_to(k), y], rz.at[k - 1], at_zy(z_to(k), y))
+            yield
+            wait()
+            for xx in range(SX):
+                each(n, lambda t, xx=xx: add(
+                    grad.at[c * SX + xx, lo + t, z, y], *[rz.at[k, xx, t] for k in range(DZ - 1)]))
+            start, wait = bundle(rx)
+            for k in range(1, SX):
+                start(grad.at[c * SX + x_to(k), taps, z, y], rx.at[k - 1], x_peer(k))
+            yield
+            wait()
+            parts = [rx.at[k] for k in range(SX - 1)]
+
+        def finish(t):
+            value = grad[mine, lo + t, z, y].astype(F32)
+            for part in parts:
+                value = value + part[t].astype(F32)
+            fb[mine, lo + t] = value.astype(BF16)
+        each(n, finish)
+        done = fb.at[mine, taps]
+        wait = to_peers(done, lambda k: done, sp_peers, fb.at[pl.ds(0, S - 1), taps])
         yield
-        for copy in got:
-            copy.wait_recv()
-
-        def add_x(i):
-            t, zz = i // DZ, i % DZ
-            for yy in range(2):
-                dst = lead(grad, (mine,), t, (zz, yy))
-                value = dst[...].astype(F32)
-                for k in range(1, SX):
-                    value = value + lead(rx, (k - 1,), t, (zz, yy))[...].astype(F32)
-                dst[...] = value.astype(BF16)
-        each(rows_n * DZ, add_x)
-        every = (slice(None),)
-        got = remote(grad.at[(mine,) + (every if taps else ()) + (slice(None), oy)], ry, y_peer)
+        wait()
+
+    def reduce_diff():
+        wait = remote(g_diff.at[oc], rcd, c_peer)
         yield
-        got.wait_recv()
-
-        def add_y(i):
-            t, zz = i // DZ, i % DZ
-            dst = lead(grad, (mine,), t, (zz, y))
-            src = lead(ry, (), t, (zz,))
-            dst[...] = (dst[...].astype(F32) + src[...].astype(F32)).astype(BF16)
-        each(rows_n * DZ, add_y)
-        got = [remote(grad.at[(mine,) + (every if taps else ()) + (z_to(k), y)], rz.at[k - 1], at_zy(z_to(k), y))
-               for k in range(1, DZ)]
-        yield
-        for copy in got:
-            copy.wait_recv()
-
-        def add_z(t):
-            value = lead(grad, (mine,), t, (z, y))[...].astype(F32)
-            for k in range(1, DZ):
-                value = value + lead(rz, (k - 1,), t, ())[...].astype(F32)
-            lead(fb, (mine,), t, ())[...] = value.astype(BF16)
-        each(rows_n, add_z)
-        got = [remote(fb.at[mine], fb.at[mine], peer) for peer in sp_peers]
-        yield
-        for copy in got:
-            copy.wait_recv()
-        for qq in range(S):
-            put(qq, fb[qq].astype(F32))
-
-    def reduce_diff():
-        got = remote(g_diff.at[oc], rcd, c_peer)
-        yield
-        got.wait_recv()
+        wait()
 
         def add_c(i):
             t, zz = i // DZ, i % DZ
@@ -1115,19 +1234,20 @@
                 value = g_diff[c, t, zz, yy].astype(F32) + rcd[t, zz, yy].astype(F32)
                 g_diff[c, t, zz, yy] = value.astype(BF16)
         each(9 * DZ, add_c)
-        got = remote(g_diff.at[c, :, :, oy], ryd, y_peer)
+        wait = remote(g_diff.at[c, :, :, oy], ryd, y_peer)
         yield
-        got.wait_recv()
+        wait()
 
         def add_y(i):
             t, zz = i // DZ, i % DZ
             value = g_diff[c, t, zz, y].astype(F32) + ryd[t, zz].astype(F32)
             g_diff[c, t, zz, y] = value.astype(BF16)
         each(9 * DZ, add_y)
-        got = [remote(g_diff.at[c, :, z_to(k), y], rzd.at[k - 1], at_zy(z_to(k), y)) for k in range(1, DZ)]
+        start, wait = bundle(rzd)
+        for k in range(1, DZ):
+            start(g_diff.at[c, :, z_to(k), y], rzd.at[k - 1], at_zy(z_to(k), y))
         yield
-        for copy in got:
-            copy.wait_recv()
+        wait()
 
         def add_z(t):
             value = g_diff[c, t, z, y].astype(F32)
@@ -1135,10 +1255,11 @@
                 value = value + rzd[k - 1, t].astype(F32)
             fdx[t] = value
         each(9, add_z)
-        got = [remote(fdx, rxd.at[k - 1], x_peer(k)) for k in range(1, SX)]
+        start, wait = bundle(rxd)
+        for k in range(1, SX):
+            start(fdx, rxd.at[k - 1], x_peer(k))
         yield
-        for copy in got:
-            copy.wait_recv()
+        wait()
 
         def add_x(t):
             value = fdx[t]
@@ -1146,42 +1267,43 @@
                 value = value + rxd[k - 1, t]
             fdo[c, t] = value
         each(9, add_x)
-        got = remote(fdo.at[c], fdo.at[c], c_peer)
+        wait = remote(fdo.at[c], fdo.at[c], c_peer)
         yield
-        got.wait_recv()
+        wait()
         od_out[...] = fdo[...]
 
     def reduce_rest():
-        got = remote(g_re, rcr, c_peer)
+        wait = remote(g_re, rcr, c_peer)
         yield
-        got.wait_recv()
-        shared = (g_re.shape[2], LANES)
+        wait()
 
         def add_c(zz):
             for yy in range(2):
                 value = g_re[zz, yy].astype(F32) + rcr[zz, yy].astype(F32)
                 rcr[zz, yy] = value.astype(BF16)
         each(DZ, add_c)
-        got = remote(rcr.at[:, oy], ryr, y_peer)
+        wait = remote(rcr.at[:, oy], ryr, y_peer)
         yield
-        got.wait_recv()
+        wait()
 
         def add_y(zz):
             value = rcr[zz, y].astype(F32) + ryr[zz].astype(F32)
             rcr[zz, y] = value.astype(BF16)
         each(DZ, add_y)
-        got = [remote(rcr.at[z_to(k), y], rzr.at[k - 1], at_zy(z_to(k), y)) for k in range(1, DZ)]
+        start, wait = bundle(rzr)
+        for k in range(1, DZ):
+            start(rcr.at[z_to(k), y], rzr.at[k - 1], at_zy(z_to(k), y))
         yield
-        for copy in got:
-            copy.wait_recv()
+        wait()
         value = rcr[z, y].astype(F32)
         for k in range(1, DZ):
             value = value + rzr[k - 1].astype(F32)
         frx[...] = value
-        got = [remote(frx, rxr.at[k - 1], x_peer(k)) for k in range(1, SX)]
+        start, wait = bundle(rxr)
+        for k in range(1, SX):
+            start(frx, rxr.at[k - 1], x_peer(k))
         yield
-        for copy in got:
-            copy.wait_recv()
+        wait()
         value = frx[...]
         for k in range(1, SX):
             value = value + rxr[k - 1]
@@ -1190,18 +1312,13 @@
         for b in range(4):
             oe_out[:, b * LANES : (b + 1) * LANES] = value[n_red + b * n_exp : n_red + (b + 1) * n_exp]
 
-    def put_first(qq, value):
-        of_out[:, qq * fw : (qq + 1) * fw] = value
-
-    def put_mid(qq, value):
-        om_out[:, :, qq * mw : (qq + 1) * mw] = value
-
-    def put_last(qq, value):
-        ol_out[:, qq * lw : (qq + 1) * lw] = value
-
-    red_last = reduce_wide(g_last, rcl, rxl, ryl, rzl, fbl, 0, put_last)
-    red_mid = reduce_wide(g_mid, rcm, rxm, rym, rzm, fbm, 9, put_mid)
-    red_first = reduce_wide(g_first, rcf, rxf, ryf, rzf, fbf, 0, put_first)
+    first_x, mid_x, last_x = fr * 5 // 8, 6, lr // 2
+    red_first_x = wide_first(g_first, 0, first_x, "xyz", *bufs[0:4], fbf)
+    red_first_y = wide_first(g_first, first_x, fr - first_x, "yzx", *bufs[4:8], fbf)
+    red_mid_x = wide_mid(g_mid, 0, mid_x, "xyz", *bufs[8:12], fbm)
+    red_mid_y = wide_mid(g_mid, mid_x, 9 - mid_x, "yzx", *bufs[12:16], fbm)
+    red_last_x = wide_first(g_last, 0, last_x, "xyz", *bufs[16:20], fbl)
+    red_last_y = wide_first(g_last, last_x, lr - last_x, "yzx", *bufs[20:24], fbl)
     red_diff, red_rest = reduce_diff(), reduce_rest()
 
     def push(*chains):
@@ -1228,7 +1345,7 @@
     copies = sp_send(2, parts)
     for n in range(4):
         g_last[n] = dot_tn(sab[...], lgb[:, n * 512 : (n + 1) * 512]).astype(BF16).reshape(DZ, 2, lr, 512)
-    push(red_last)
+    push(red_last_x, red_last_y)
     total = sp_total(2, copies)
     gain_2_grad = bias_2_grad = jnp.zeros((1, 512), F32)
     for group in range(NG):
@@ -1244,13 +1361,13 @@
             return carry
         rows_loop(group, apply_2b, 0)
     wait_mid, _ = halo(mgb.at[pl.ds(0, NW)], mgb.at[pl.ds(NW, NW)], None, None, mgr.at[0], mgr.at[1])
-    push(red_last)
+    push(red_last_x, red_last_y)
     for a in range(3):
         for b in range(3):
             grad = dot_tn(gs[a : a + 2, :, b * 512 : (b + 1) * 512].reshape(2 * NW, 512), mgb[...]).astype(BF16)
             for qq in range(S):
                 g_mid[qq, 3 * a + b] = grad[:, qq * mw : (qq + 1) * mw].reshape(DZ, 2, wm_in.shape[1], mw)
-    push(red_mid)
+    push(red_mid_x, red_mid_y)
     mgs = gs
     for r in range(2):
         spread(mgs, 1 + r, lambda start, r=r: mgb[pl.ds(r * NW + start, STEP), :], True)
@@ -1286,7 +1403,7 @@
         cgx[r, 0] = cg_rows[r].astype(BF16)
         cgx[r, 1] = hg
     wait_cg, _ = halo(cgx.at[0], cgx.at[1], None, None, cgr.at[0], cgr.at[1])
-    push(red_last)
+    push(red_mid_x, red_mid_y)
     n_exp = we_in.shape[0]
     grad = dot_tn(comb[...], fgb[...]).astype(BF16)
     n_red = wr_in.shape[0]
@@ -1301,7 +1418,7 @@
         g_diff[0, 3 * a : 3 * a + 3] = grad.reshape(3, DZ, 2, wd0_in.shape[1], LANES)
         grad = (0.5 * dot_tn(ps[a], hg)).astype(BF16)
         g_diff[1, 3 * a : 3 * a + 3] = grad.reshape(3, DZ, 2, wd0_in.shape[1], LANES)
-    push(red_diff)
+    push(red_diff, red_last_y, red_last_x)
     wait_cg()
     put_shifts(cgs, 0, cgr[0, 0].astype(F32), 1, True)
     put_shifts(cgs, 3, cgr[1, 0].astype(F32), 1, True)
@@ -1340,7 +1457,7 @@
         parts += [jnp.sum(item, axis=0, keepdims=True) for item in sums]
     copies = sp_send(3, parts)
     g_re[:, :, 0:n_red, :] = dot_tn(fab[...], rgb).astype(BF16).reshape(DZ, 2, n_red, LANES)
-    push(red_rest, red_mid, red_last, red_diff)
+    push(red_rest, red_diff, red_last_x, red_last_y)
     total = sp_total(3, copies)
     gain_1_grad = bias_1_grad = jnp.zeros((1, 512), F32)
     for group in range(NG):
@@ -1356,8 +1473,7 @@
             return carry
         rows_loop(group, apply_1b, 0)
 
-    for k, copy in enumerate(stem_copies):
-        copy.wait_recv()
+    wait_stem()
     stem_total = stg[...]
     for k in range(S - 1):
         stem_total = stem_total + stgr[k]
@@ -1370,8 +1486,9 @@
             rows += [v[:, last_at + n * LANES : last_at + (n + 1) * LANES] for n in range(rows_last)]
         sms[d, 0:8, :] = stem_total[d * 8 : d * 8 + 8]
         sms[d, 8:16, :] = jnp.concatenate(rows, axis=0)
-    small_back = [
-        remote(sms.at[lax.rem(dp + k, D)], smr.at[k - 1], dp_peers[k - 1]) for k in range(1, D)]
+    small_start, wait_small_back = bundle(smr)
+    for k in range(1, D):
+        small_start(sms.at[lax.rem(dp + k, D)], smr.at[k - 1], dp_peers[k - 1])
 
     for n in range(4):
         grad = dot_tn(x3[:, :, n * 512 : (n + 1) * 512].reshape(2 * NW, 512), fgb[...]).astype(BF16)
@@ -1379,7 +1496,8 @@
         for qq in range(S):
             g_first[qq, n * per_chunk : (n + 1) * per_chunk] = grad[:, qq * fw : (qq + 1) * fw].reshape(
                 per_chunk, 2, fr, fw)
-    push(red_first, red_rest, red_mid, red_last, red_diff)
+    push(red_first_x, red_first_y, red_rest, red_diff)
+    push(red_first_x, red_first_y)
     weights_first = wf[...].reshape(2048, 512)
     for n in range(4):
         lo = n * 512
@@ -1393,8 +1511,19 @@
             return carry
         lax.fori_loop(0, 2 * NW // STEP, apply_in, 0)
         store_part(n, ig_hbm)
-    for _ in range(6):
-        push(red_first, red_rest, red_mid, red_last, red_diff)
+        if n == 1:
+            push(red_mid_y, red_mid_x)
+    push(red_rest, red_diff, red_last_x, red_last_y)
+    push(red_mid_y, red_mid_x)
+    push(red_first_y, red_first_x)
+    push(red_rest, red_diff)
+    push(red_mid_y, red_mid_x)
+    push(red_first_y, red_first_x)
+    push(red_rest, red_diff)
+    for _ in range(3):
+        push(red_mid_y, red_mid_x, red_last_x, red_last_y, red_rest, red_diff)
+        push(red_first_y, red_first_x)
+    grad_stores = [local(fbf, fbf_hbm), local(fbm, fbm_hbm), local(fbl, fbl_hbm)]
 
     assert counters["r"] <= ssem.shape[0] and counters["l"] <= lsem.shape[0], counters
     wait_video()
@@ -1410,17 +1539,59 @@
 
     lax.fori_loop(0, NF, video_edges, 0)
     value = sms[dp]
-    for k, copy in enumerate(small_back):
-        copy.wait_recv()
+    wait_small_back()
+    for k in range(D - 1):
         value = value + smr[k]
     osm_out[...] = value
-    for copy in sends:
-        copy.wait_send()
-    for finish in halo_waits:
+    for finish in sends + halo_waits:
         finish()
+    for copy in grad_stores:
+        copy.wait()
     for part in stores[-2:]:
         for copy in part:
             copy.wait()
+
+
+def final_kernel(
+    sizes, so, vg, out, ig, fbf, fbm, fbl, gr, gd, ge, gsm,
+    so_o, vg_o, out_o, ig_o, rgb_o, stemd_o, first_o, mid_o, last_o, red_o, dfull_o, dhalf_o, exp_o,
+    g1_o, b1_o, g2_o, b2_o, g3_o, b3_o, sems, turned,
+):
+    D, S = sizes
+    copies = [
+        pltpu.make_async_copy(src, dst, sems.at[i])
+        for i, (src, dst) in enumerate(((so, so_o), (out, out_o), (ig, ig_o), (vg, vg_o)))]
+    for copy in copies:
+        copy.start()
+    fw, lw = fbf.shape[2], fbl.shape[2]
+    for q in range(S):
+        first_o[:, q * fw : (q + 1) * fw] = fbf[q].astype(F32)
+        last_o[:, q * lw : (q + 1) * lw] = fbl[q].astype(F32)
+        for t in range(9):
+            mid_o[t, :, q * fw : (q + 1) * fw] = fbm[q, t].astype(F32)
+    red_o[...] = gr[...]
+    dfull_o[...] = gd[0]
+    dhalf_o[...] = gd[1]
+    exp_o[...] = ge[...]
+    turned[:, 0:8] = gsm[0:8, :].T
+    for t in range(9):
+        rgb_o[t] = turned[t * 9 : t * 9 + 3, 0:8]
+        stemd_o[t] = turned[t * 9 + 3 : t * 9 + 9, 0:8]
+    width = g1_o.shape[0]
+    per = LANES // width
+    here = lax.rem(lax.axis_index("dp"), per)
+    for j, ref in enumerate((g1_o, b1_o, g2_o, b2_o)):
+        row = gsm[8 + j]
+        value = row[0:width]
+        for n in range(1, per):
+            value = jnp.where(here == n, row[n * width : (n + 1) * width], value)
+        ref[...] = value
+    count = g3_o.shape[0] // LANES
+    for j, ref in enumerate((g3_o, b3_o)):
+        for n in range(count):
+            ref[n * LANES : (n + 1) * LANES] = gsm[12 + j * count + n]
+    for copy in copies:
+        copy.wait()
 
 
 def on_device_kernel(
@@ -1454,12 +1625,12 @@
     vm = pltpu.VMEM
     any_spec = pl.BlockSpec(memory_space=pl.ANY)
     vmem_spec = pl.BlockSpec(memory_space=pltpu.VMEM)
-    n_rem, n_loc = 420, 64
+    n_rem, n_loc = 128, 50
     re_rows = rr + 4 * er
     scratch = [
         pltpu.SemaphoreType.DMA((n_rem,)), pltpu.SemaphoreType.DMA((n_rem,)), pltpu.SemaphoreType.DMA((n_loc,)),
-        vm((DZ, 2, fr, 512), BF16), vm((9, DZ, 2, mr, 512), BF16), vm((DZ, 2, lr, 2048), BF16),
-        vm((DZ, 2, rr, LANES), BF16), vm((2, 9, DZ, 2, dr, LANES), BF16), vm((DZ, 2, er, 512), BF16),
+        vm((D, fr, 512), BF16), vm((9, D, mr, 512), BF16), vm((D, lr, 2048), BF16),
+        vm((D, rr, LANES), BF16), vm((2, 9, D, dr, LANES), BF16), vm((D, er, 512), BF16),
         vm((2 * NF, 16, 2048), BF16), vm((2 * NF, 16, 2048), BF16),
         vm((2 * PART, 512, LANES), BF16), vm((2 * PART, 512, LANES), BF16),
         vm((NF, 32, LANES), F32), vm((NF, 8, LANES), F32), vm((NF, 8, LANES), F32),
@@ -1476,12 +1647,6 @@
         vm((4, NW, 384), BF16), vm((3, NW, 384), BF16), vm((2 * NW, 512), BF16), vm((2, 2 * NF, 16, 512), BF16),
         vm((S, DZ, 2, fr, fw), BF16), vm((S, 9, DZ, 2, mr, fw), BF16), vm((S, DZ, 2, lr, lw), BF16),
         vm((2, 9, DZ, 2, dr, LANES), BF16), vm((DZ, 2, re_rows, LANES), BF16),
-        vm((SX, DZ, 2, fr, fw), BF16), vm((SX - 1, DZ, 2, fr, fw), BF16), vm((DZ, fr, fw), BF16),
-        vm((DZ - 1, fr, fw), BF16),
-        vm((SX, 9, DZ, 2, mr, fw), BF16), vm((SX - 1, 9, DZ, 2, mr, fw), BF16), vm((9, DZ, mr, fw), BF16),
-        vm((DZ - 1, 9, mr, fw), BF16),
-        vm((SX, DZ, 2, lr, lw), BF16), vm((SX - 1, DZ, 2, lr, lw), BF16), vm((DZ, lr, lw), BF16),
-        vm((DZ - 1, lr, lw), BF16),
         vm((9, DZ, 2, dr, LANES), BF16), vm((9, DZ, dr, LANES), BF16), vm((DZ - 1, 9, dr, LANES), BF16),
         vm((9, dr, LANES), F32), vm((SX - 1, 9, dr, LANES), F32), vm((2, 9, dr, LANES), F32),
         vm((DZ, 2, re_rows, LANES), BF16), vm((DZ, re_rows, LANES), BF16), vm((DZ - 1, re_rows, LANES), BF16),
@@ -1489,16 +1654,28 @@
         vm((S, fr, fw), BF16), vm((S, 9, mr, fw), BF16), vm((S, lr, lw), BF16),
         vm((D, 16, LANES), F32), vm((D - 1, 16, LANES), F32),
     ]
+
+    def landing(rows, shape_of):
+        for order, n in (("xyz", rows[0]), ("yzx", rows[1])):
+            extra = (SX,) if order == "yzx" else ()
+            scratch.append(vm((SX,) + shape_of(n, (DZ, 2)), BF16))
+            scratch.append(vm((SX - 1,) + shape_of(n, (DZ, 2) if order == "xyz" else ()), BF16))
+            scratch.append(vm(extra + shape_of(n, (DZ,)), BF16))
+            scratch.append(vm((DZ - 1,) + extra + shape_of(n, ()), BF16))
+
+    landing((fr * 5 // 8, fr - fr * 5 // 8), lambda n, lead: lead + (n, fw))
+    landing((6, 3), lambda n, lead: (n,) + lead + (mr, fw))
+    landing((lr // 2, lr - lr // 2), lambda n, lead: lead + (n, lw))
     outs = pl.pallas_call(
         functools.partial(whole_kernel, (D, S, NF)),
         out_shape=(
             shape((NF, 512, LANES), BF16), shape((NF, 24, LANES), F32),
             shape(section_input.shape, BF16), shape(section_input.shape, BF16),
-            shape((fr, 512), F32), shape((9, mr, 512), F32), shape((lr, 2048), F32), shape((rr, LANES), F32),
+            shape((S, fr, fw), BF16), shape((S, 9, mr, fw), BF16), shape((S, lr, lw), BF16), shape((rr, LANES), F32),
             shape((2, 9, dr, LANES), F32), shape((er, 512), F32), shape((16, LANES), F32),
         ),
         in_specs=[pl.BlockSpec(memory_space=pltpu.SMEM)] + [vmem_spec] * 3 + [any_spec] * 10,
-        out_specs=(any_spec, vmem_spec, any_spec, any_spec) + (vmem_spec,) * 7,
+        out_specs=(any_spec, vmem_spec) + (any_spec,) * 5 + (vmem_spec,) * 4,
         scratch_shapes=scratch,
         compiler_params=pltpu.CompilerParams(
             collective_id=0, has_side_effects=True, vmem_limit_bytes=VMEM_BYTES),
@@ -1507,16 +1684,22 @@
         keep_mask, uin, small, band, section_input, section_cot, stem_cot.reshape(NF, 512, LANES),
         w_first, w_middle, w_last, w_reduce, w_diff_full, w_diff_half, w_expand,
     )
-    so, vg, section_output, input_grad, g_first, g_mid, g_last, g_red, g_diff, g_exp, g_small = outs
-    stem = g_small[0:8, 0:81].reshape(8, 9, 9).transpose(1, 2, 0)
-    mids = lax.dynamic_slice_in_dim(g_small[8:12], (dp % per) * width, width, axis=1)
-    rows_last = 2048 // D // LANES
-    lasts = g_small[12 : 12 + 2 * rows_last].reshape(2, rows_last * LANES)
-    return (
-        so.reshape(stem_cot.shape), vg.reshape(clip_video.shape), section_output, input_grad,
-        stem[:, 0:3], stem[:, 3:9], g_first, g_mid, g_last, g_red, g_diff[0], g_diff[1], g_exp,
-        mids[0], mids[1], mids[2], mids[3], lasts[0], lasts[1],
-    )
+    results = (
+        shape(stem_cot.shape, BF16), shape(clip_video.shape, F32), shape(section_input.shape, BF16),
+        shape(section_input.shape, BF16), shape(w_rgb.shape, F32), shape(w_stem_diff.shape, F32),
+        shape(w_first.shape, F32), shape(w_middle.shape, F32), shape(w_last.shape, F32), shape(w_reduce.shape, F32),
+        shape(w_diff_full.shape, F32), shape(w_diff_half.shape, F32), shape(w_expand.shape, F32),
+    ) + (shape((width,), F32),) * 4 + (shape((2048 // D,), F32),) * 2
+    so, vg, section_output, input_grad, *grads = outs
+    return pl.pallas_call(
+        functools.partial(final_kernel, (D, S)),
+        out_shape=results,
+        in_specs=[any_spec] * 4 + [vmem_spec] * 7,
+        out_specs=(any_spec,) * 4 + (vmem_spec,) * 15,
+        scratch_shapes=[pltpu.SemaphoreType.DMA((4,)), vm((LANES, LANES), F32)],
+        compiler_params=pltpu.CompilerParams(vmem_limit_bytes=24 * 2**20),
+        name="final_outputs",
+    )(so.reshape(stem_cot.shape), vg.reshape(clip_video.shape), section_output, input_grad, *grads)
 
 
 def fits_kernel(mesh):
@@ -1524,7 +1707,7 @@
     return (
         dp_count % 2 == 0 and sp_count % 2 == 0 and H5 == 2 * sp_count and HS == 8 * sp_count
         and TDM_C % (16 * dp_count) == 0 and STEM_C == 8 * dp_count and MID // sp_count % LANES == 0
-        and C5 // dp_count % LANES == 0
+        and C5 // dp_count % LANES == 0 and (dp_count - 1) * (sp_count // 2 - 1) <= dp_count
     )
 
 

time: 219 us -> 187 us (0.85)
  Pallas kernels: 195 us -> 168 us
  local copies, waits for them, and re-layouts: 18.5 us -> 13.7 us
    pallas_call x1, Pallas kernels: 195 us -> 164 us  [on_device_kernel(): pl.pallas_call(functools.partial(whole_kernel, (D, S, NF)), out_shape=(sh...]
    pallas_call x0 -> x1, Pallas kernels: none -> 4.18 us  [on_device_kernel(): pl.pallas_call(functools.partial(final_kernel, (D, S)), out_shape=results...]
    squeeze x3 -> x0, local copies, waits for them, and re-layouts: 3.43 us -> none  [the longest x1 1.58 us: on_device_kernel(): g_diff[1]]
    unnamed x27 -> x22, local copies, waits for them, and re-layouts: 13 us -> 11.8 us
where the time goes in v2:
time: 187 us
  Pallas kernels  168 us (90%)
  local copies, waits for them, and re-layouts  13.7 us (7%)
  other arithmetic  4.46 us (2%)
    pallas_call x1, Pallas kernels, on_device_kernel(): pl.pallas_call(functools.partial(whole_kernel, (D, S, NF)), out_shape=(sh...  164 us
    unnamed x22, local copies, waits for them, and re-layouts  11.8 us
    pallas_call x1, Pallas kernels, on_device_kernel(): pl.pallas_call(functools.partial(final_kernel, (D, S)), out_shape=results...  4.18 us

profile of v2, /device:TPU:0, one launch (start us, length us, event | category | flops | bytes accessed | tf_op | source)
XLA Modules:
  0.0 186.7 jit_solution(13126426004187384801)
XLA Ops:
  0.7 0.1 pad.22.clone
  0.8 0.7 maximum_convert_fusion
  1.5 0.1 tile.10
  1.6 0.7 maximum_convert_fusion.1
  2.3 0.7 maximum_bitcast_fusion
  3.0 0.1 copy.46
  3.1 0.1 reshape.98
  3.2 0.6 pad_maximum_fusion.1.small
  3.8 0.9 copy_convert_fusion
  4.8 0.1 copy.51
  4.9 0.8 maximum_maximum_fusion.uin
  5.7 163.6 %tdn_blocks.1 = (bf16[16,512,128]{2,1,0:T(8,128)(2,1)}, f32[16,24,128]{2,1,0:T(8,128)}, bf16[16,2,16,2048]{3,2,1,0:T(8,128)(2,1)}, bf16[16,2,16,2048]{3,2,1,0:T(...) custom-call(s32[16]{0:T(128)} %keep.1, ...), custom_call_target="tpu_custom_call" | custom-call | tf_op jit(solution)/shard_map/tdn_blocks/pallas_call | solution.py:1669
  169.3 0.0 copy-start
  169.3 1.6 copy-done
  170.9 0.0 copy-start.1
  170.9 1.6 copy-done.1
  172.4 0.0 copy-start.2
  172.4 1.6 copy-done.2
  174.0 0.0 copy-start.3
  174.0 1.1 copy-done.3
  175.1 0.0 copy-start.4
  175.1 0.9 copy-done.4
  176.1 0.0 copy-start.5
  176.1 0.9 copy-done.5
  177.0 0.0 copy-start.6
  177.0 0.9 copy-done.6
  177.9 0.0 copy-start.7
  177.9 0.9 copy-done.7
  178.8 0.0 copy-start.8
  178.8 0.8 copy-done.8
  179.6 0.0 copy-start.9
  179.6 0.8 copy-done.9
  180.4 0.0 copy-start.10
  180.4 0.7 copy-done.10
  181.1 4.2 %final_outputs.1 = (bf16[16,64,8,128]{3,2,1,0:T(8,128)(2,1)}, f32[16,3,8,128]{3,2,1,0:T(8,128)}, bf16[16,2,16,2048]{3,2,1,0:T(8,128)(2,1)}, bf16[16,2,16,2048]{3...) custom-call(bf16[16,64,8,128]{3,2,1,0:T(8,128)(2,1)S(1)} %bitcast.15, ...), custom_call_target="tpu_custom_call" | custom-call | tf_op jit(solution)/shard_map/final_outputs/pallas_call | solution.py:1694
  185.2 0.7 copy.47
  185.9 0.7 copy.48
  (8 shorter events, 0.1 us)
Async XLA Ops:
  169.3 1.6 copy-start
  170.9 1.6 copy-start.1
  172.4 1.6 copy-start.2
  174.0 1.1 copy-start.3
  175.1 0.9 copy-start.4
  176.1 0.9 copy-start.5
  177.0 0.9 copy-start.6
  177.9 0.9 copy-start.7
  178.8 0.8 copy-start.8
  179.6 0.8 copy-start.9
  180.4 0.7 copy-start.10

commit v3 on v2

--- a/solution.py
+++ b/solution.py
@@ -469,8 +469,17 @@
                         n = base + 24 + (ch % 3) * 2 + 1
                     else:
                         n = base + (ch % 3) * 8 + row
-                    table[i, (3 * a + b) * 9 + ch, n] = 1.0
+                    table[i, ch * 9 + 3 * a + b, n] = 1.0
     return table
+
+
+def portions(first_rows, taps, last_rows):
+    cut = first_rows * 5 // 16
+    return (
+        (("xyz", 0, cut), ("xyz", cut, cut), ("yzx", 2 * cut, first_rows - 2 * cut)),
+        (("xyz", 0, 3), ("xyz", 3, 3), ("yzx", 6, taps - 6)),
+        (("xyz", 0, last_rows // 2), ("yzx", last_rows // 2, last_rows // 2)),
+    )
 
 
 def silu_parts(values):
@@ -479,9 +488,9 @@
 
 
 def whole_kernel(
-    sizes, keep, uin, small, band, x_hbm, ct_hbm, sc_hbm, wf_in, wm_in, wl_in, wr_in, wd0_in, wd1_in, we_in,
+    sizes, keep, clip, rgb, stemd, g1, b1, g2, b2, g3, b3, band, x_hbm, ct_hbm, sc_hbm, wf_in, wm_in, wl_in, wr_in, wd0_in, wd1_in, we_in,
     so_hbm, vg_out, out_hbm, ig_hbm, fbf_hbm, fbm_hbm, fbl_hbm, or_out, od_out, oe_out, osm_out,
-    ssem, rsem, lsem, wf, wm, wl, wr, wd, we, x3, ct3, sc, so, ust, uprev, unext, sm, tf, tff, tb, dg,
+    ssem, rsem, lsem, wf, wm, wl, wr, wd, we, x3, ct3, sc, so, ust, uprev, unext, small, sm, tf, tff, tb, dg,
     vgh, vgr, stg, stgr, stat_s, stat_r, st3_s, st3_r, z1, fab, gt, rd, chb, chr_, cs, ps, comb,
     gb, gr, gs, z2, sab, z3, lgb, cgx, cgr, cgs, hgs, fgb, ost,
     g_first, g_mid, g_last, g_diff, g_re, rcd, ryd, rzd, fdx, rxd, fdo, rcr, ryr, rzr, frx, rxr, fbf, fbm, fbl, sms, smr, *bufs,
@@ -503,11 +512,13 @@
     y_peer = at_zy(z, oy)
     c_peer = (dp, x * 2 + oc)
 
-    def z_to(k):
-        return lax.rem(z + k, DZ)
-
-    def z_from(k):
-        return lax.rem(z + DZ - k, DZ)
+    z_bits = [1 << n for n in range(DZ.bit_length() - 1)]
+
+    def z_pair(bit):
+        return z + bit - 2 * bit * ((z // bit) % 2)
+
+    def z_class(zz, bit):
+        return [zz % (2 * bit) + 2 * bit * j for j in range(DZ // (2 * bit))]
 
     def x_to(k):
         return lax.rem(x + k, SX)
@@ -582,6 +593,17 @@
     barrier = pltpu.get_barrier_semaphore()
     for peer in sp_peers + dp_peers:
         pl.semaphore_signal(barrier, inc=1, device_id=peer, device_id_type=MESH_ID)
+    per = D * LANES // 512
+    rows_last = 2048 // D // LANES
+    small[...] = jnp.zeros_like(small)
+    for ch in range(9):
+        small[0:8, ch * 9 : ch * 9 + 9] = (rgb[ch] if ch < 3 else stemd[ch - 3]).astype(F32)
+    place = lax.broadcasted_iota(jnp.int32, (1, LANES), 1) // (LANES // per)
+    for j, ref in enumerate((g1, b1, g2, b2)):
+        row = jnp.concatenate([ref[...].astype(F32)] * per, axis=1)
+        small[8 + j : 9 + j, :] = jnp.where(place == lax.rem(dp, per), row, 0.0)
+    for j, ref in enumerate((g3, b3)):
+        small[12 + j * rows_last : 12 + (j + 1) * rows_last, :] = ref[...].astype(F32)
     own_small = local(small, sm.at[dp])
     own = [
         local(wf_in, wf.at[dp]), local(wd0_in, wd.at[0, :, dp]), local(wd1_in, wd.at[1, :, dp]),
@@ -643,41 +665,44 @@
         return wait, finish
 
     wait_small = to_peers(small, lambda k: sm.at[dp], dp_peers, sm.at[pl.ds(0, D - 1)])
-    edge = uin.at[:, pl.ds(24, 8)]
-    wait_edges, _ = halo(edge, edge, None, None, uprev, unext)
-
-    def gather(mode, src, dst):
+    wait_edges, _ = halo(clip, clip, None, None, uprev, unext)
+
+    def gather(mode, dst):
         wide = {"A": 1, "B": SX, "D": S}[mode]
         first_q = {"A": q_own, "B": c * SX, "D": 0}[mode]
         only = pl.ds(dp, 1)
-        z_start, z_wait = bundle(dst(pl.ds(0, DZ - 1), first_q, wide))
+        z_links = {bit: bundle(dst(pl.ds(0, DZ // (2 * bit)), first_q, wide)) for bit in z_bits}
         y_start, y_wait = bundle(dst(pl.ds(0, DZ), first_q, wide))
         if mode == "A":
             x_start, x_wait = bundle(dst(pl.ds(0, (D - 1) * (SX - 1)), first_q, 1))
         if mode != "D":
             c_start, c_wait = bundle(dst(pl.ds(0, D - 1), c * SX, SX))
-        for k in range(1, DZ):
-            z_start(src(first_q, wide), dst(only, first_q, wide), at_zy(z_to(k), y))
-        y_start(src(first_q, wide), dst(only, first_q, wide), y_peer)
+        mine = dst(pl.ds(dp, 1), first_q, wide)
+        for bit in reversed(z_bits):
+            z_links[bit][0](mine, mine, at_zy(z_pair(bit), y))
+        y_start(mine, mine, y_peer)
         yield
 
-        def fan(d):
-            part = dst(d, first_q, wide)
+        def fan(part):
             if mode == "A":
                 for k in range(1, SX):
                     x_start(part, part, x_peer(k))
             if mode != "D":
                 c_start(part, part, c_peer)
 
-        z_wait()
-        for k in range(1, DZ):
-            d = pl.ds(z_from(k) * 2 + y, 1)
-            y_start(dst(d, first_q, wide), dst(d, first_q, wide), y_peer)
-            fan(d)
-        yield
+        for bit in reversed(z_bits):
+            z_links[bit][1]()
+            for zz in z_class(z_pair(bit), bit):
+                part = dst(pl.ds(zz * 2 + y, 1), first_q, wide)
+                for lower in z_bits:
+                    if lower < bit:
+                        z_links[lower][0](part, part, at_zy(z_pair(lower), y))
+                y_start(part, part, y_peer)
+                fan(part)
+            yield
         y_wait()
-        for k in range(DZ):
-            fan(pl.ds(z_from(k) * 2 + oy, 1))
+        for zz in range(DZ):
+            fan(dst(pl.ds(zz * 2 + oy, 1), first_q, wide))
         yield
         if mode == "A":
             x_wait()
@@ -698,18 +723,15 @@
 
     def first_part(mode, lo, n):
         rows = pl.ds(lo, n)
-        return gather(mode, lambda q, w: wf.at[pl.ds(dp, 1), rows, lane_block(q, fw, w)],
-                      lambda d, q, w: wf.at[d, rows, lane_block(q, fw, w)])
+        return gather(mode, lambda d, q, w: wf.at[d, rows, lane_block(q, fw, w)])
 
     def mid_part(mode, lo, n):
         rows = pl.ds(lo, n)
-        return gather(mode, lambda q, w: wm.at[rows, pl.ds(dp, 1), :, lane_block(q, mw, w)],
-                      lambda d, q, w: wm.at[rows, d, :, lane_block(q, mw, w)])
+        return gather(mode, lambda d, q, w: wm.at[rows, d, :, lane_block(q, mw, w)])
 
     def last_part(mode, lo, n):
         rows = pl.ds(lo, n)
-        return gather(mode, lambda q, w: wl.at[pl.ds(dp, 1), rows, lane_block(q, lw, w)],
-                      lambda d, q, w: wl.at[d, rows, lane_block(q, lw, w)])
+        return gather(mode, lambda d, q, w: wl.at[d, rows, lane_block(q, lw, w)])
 
     for copy in own:
         copy.wait()
@@ -719,21 +741,29 @@
         (0, first_part("A", 0, part_a)),
         (0, first_part("B", 2 * part_a, part_b)),
         (0, first_part("A", part_a, part_a)),
-        (1, gather("D", lambda q, w: wr.at[pl.ds(dp, 1)], lambda d, q, w: wr.at[d])),
-        (1, gather("B", lambda q, w: wd.at[c, :, pl.ds(dp, 1)], lambda d, q, w: wd.at[c, :, d])),
-        (1, gather("D", lambda q, w: we.at[pl.ds(dp, 1)], lambda d, q, w: we.at[d])),
+        (1, gather("D", lambda d, q, w: wr.at[d])),
+        (1, gather("B", lambda d, q, w: wd.at[c, :, d])),
+        (1, gather("D", lambda d, q, w: we.at[d])),
         (1, mid_part("A", 0, 3)), (2, mid_part("B", 6, 3)), (2, mid_part("A", 3, 3)),
         (3, last_part("A", 0, lr // 2)), (3, last_part("B", lr // 2, lr // 4)),
         (4, last_part("A", lr * 3 // 4, lr // 4)),
     ]
     slot = [0]
+    arrived = set()
 
     def pump(count=1):
         for _ in range(count):
-            for start, chunk in chunks:
-                if start <= slot[0]:
-                    next(chunk, None)
+            for n, (start, chunk) in enumerate(chunks):
+                if start <= slot[0] and n not in arrived:
+                    try:
+                        next(chunk)
+                    except StopIteration:
+                        arrived.add(n)
             slot[0] += 1
+
+    def need(low, high):
+        while not arrived.issuperset(range(low, high)):
+            pump()
 
     pump()
 
@@ -749,8 +779,6 @@
         tf[:, n * LANES : n * LANES + columns] = tff[n, :, 0:columns].astype(BF16)
         tb[n * LANES : n * LANES + columns, :] = tff[n].T[0:columns].astype(BF16)
 
-    per = D * LANES // 512
-
     def mid_vec(j):
         parts = []
         for m in range(D // per):
@@ -760,8 +788,6 @@
             parts.append(row)
         return jnp.concatenate(parts, axis=1)
 
-    rows_last = 2048 // D // LANES
-
     def last_vec(j):
         return jnp.concatenate(
             [sm[d, 8 + j + n : 9 + j + n, :] for d in range(D) for n in range(rows_last)], axis=1)
@@ -770,11 +796,19 @@
     gain_3, bias_3 = last_vec(4), last_vec(4 + rows_last)
 
     wait_edges()
-    side = lax.broadcasted_iota(jnp.int32, (8, LANES), 0) & 1
-    ust[...] = uin[...]
-    for f in range(NF):
-        ust[f, 24:32, :] = jnp.where(
-            side == 0, pltpu.roll(uprev[f], 7, 0), pltpu.roll(unext[f], 1, 0))
+    row8 = lax.broadcasted_iota(jnp.int32, (8, LANES), 0)
+
+    def load_frame(f, carry):
+        ust[f, 0:24, :] = clip[f].astype(F32)
+        above, below = uprev[f].astype(F32), unext[f].astype(F32)
+        halo_rows = jnp.zeros((8, LANES), F32)
+        for ch in range(3):
+            halo_rows = jnp.where(row8 == 2 * ch, above[ch * 8 + 7 : ch * 8 + 8], halo_rows)
+            halo_rows = jnp.where(row8 == 2 * ch + 1, below[ch * 8 : ch * 8 + 1], halo_rows)
+        ust[f, 24:32, :] = halo_rows
+        return carry
+
+    lax.fori_loop(0, NF, load_frame, 0)
     zt = tff
     zt[...] = jnp.zeros_like(zt)
 
@@ -885,11 +919,12 @@
 
     for copy in load_x:
         copy.wait()
+    need(0, 3)
     xs = x3[...].reshape(2 * NW, x3.shape[2])
     for n in range(2):
         z1[:, n * 256 : (n + 1) * 256] = dot_nn(xs, wf[:, :, n * 256 : (n + 1) * 256].reshape(x3.shape[2], 256))
     copies = sp_send(0, two_sums(z1))
-    pump()
+    need(3, 6)
     total = sp_total(0, copies)
     inv_1 = []
     for group in range(NG):
@@ -975,6 +1010,7 @@
     def taps_of(a):
         return wm[3 * a : 3 * a + 3].reshape(1536, 512)
 
+    need(6, 9)
     z2[...] = dot_nn(gs[1:3].reshape(2 * NW, 1536), taps_of(1))
     z2[0:NW, :] += dot_nn(gs[2], taps_of(2))
     z2[NW : 2 * NW, :] += dot_nn(gs[1], taps_of(0))
@@ -984,7 +1020,7 @@
     z2[0:NW, :] += dot_nn(gs[0], taps_of(0))
     z2[NW : 2 * NW, :] += dot_nn(gs[3], taps_of(2))
     copies = sp_send(1, two_sums(z2))
-    pump(2)
+    need(9, 12)
     for copy in load_ct:
         copy.wait()
     total = sp_total(1, copies)
@@ -1070,6 +1106,19 @@
             return carry
         lax.fori_loop(0, count, body, 0)
 
+    def z_steps(part, rz, add):
+        at = 0
+        for bit in z_bits:
+            keep_z, give_z = z_class(z, bit), z_class(z_pair(bit), bit)
+            start, wait = bundle(rz.at[pl.ds(at, len(keep_z))])
+            for j, zz in enumerate(give_z):
+                start(part(zz), rz.at[at + j], at_zy(z_pair(bit), y))
+            yield
+            wait()
+            for j, zz in enumerate(keep_z):
+                add(part(zz), rz.at[at + j])
+            at += len(keep_z)
+
     def wide_first(grad, lo, n, order, rc, rx, ry, rz, fb):
         rows = pl.ds(lo, n)
         half = pl.ds(c * SX, SX)
@@ -1105,12 +1154,8 @@
             yield
             wait()
             each(DZ, lambda i: add(grad.at[mine, i, y, rows], ry.at[i]))
-            start, wait = bundle(rz)
-            for k in range(1, DZ):
-                start(grad.at[mine, z_to(k), y, rows], rz.at[k - 1], at_zy(z_to(k), y))
-            yield
-            wait()
-            parts = [rz.at[k] for k in range(DZ - 1)]
+            yield from z_steps(lambda zz: grad.at[mine, zz, y, rows], rz, add)
+            parts = []
         else:
             wait = remote(grad.at[half, :, oy, rows], ry, y_peer)
             yield
@@ -1120,13 +1165,10 @@
                 for xx in range(SX):
                     add(grad.at[c * SX + xx, i, y, rows], ry.at[xx, i])
             each(DZ, add_y)
-            start, wait = bundle(rz)
-            for k in range(1, DZ):
-                start(grad.at[half, z_to(k), y, rows], rz.at[k - 1], at_zy(z_to(k), y))
-            yield
-            wait()
-            for xx in range(SX):
-                add(grad.at[c * SX + xx, z, y, rows], *[rz.at[k, xx] for k in range(DZ - 1)])
+            def add_half(dst, src):
+                for xx in range(SX):
+                    add(dst.at[xx], src.at[xx])
+            yield from z_steps(lambda zz: grad.at[half, zz, y, rows], rz, add_half)
             start, wait = bundle(rx)
             for k in range(1, SX):
                 start(grad.at[c * SX + x_to(k), z, y, rows], rx.at[k - 1], x_peer(k))
@@ -1181,12 +1223,10 @@
                 t, zz = i // DZ, i % DZ
                 add(grad.at[mine, lo + t, zz, y], ry.at[t, zz])
             each(n * DZ, add_y)
-            start, wait = bundle(rz)
-            for k in range(1, DZ):
-                start(grad.at[mine, taps, z_to(k), y], rz.at[k - 1], at_zy(z_to(k), y))
-            yield
-            wait()
-            parts = [rz.at[k] for k in range(DZ - 1)]
+            def add_taps(dst, src):
+                each(n, lambda t: add(dst.at[t], src.at[t]))
+            yield from z_steps(lambda zz: grad.at[mine, taps, zz, y], rz, add_taps)
+            parts = []
         else:
             wait = remote(grad.at[half, taps, :, oy], ry, y_peer)
             yield
@@ -1197,14 +1237,10 @@
                 for xx in range(SX):
                     add(grad.at[c * SX + xx, lo + t, zz, y], ry.at[xx, t, zz])
             each(n * DZ, add_y)
-            start, wait = bundle(rz)
-            for k in range(1, DZ):
-                start(grad.at[half, taps, z_to(k), y], rz.at[k - 1], at_zy(z_to(k), y))
-            yield
-            wait()
-            for xx in range(SX):
-                each(n, lambda t, xx=xx: add(
-                    grad.at[c * SX + xx, lo + t, z, y], *[rz.at[k, xx, t] for k in range(DZ - 1)]))
+            def add_half(dst, src):
+                for xx in range(SX):
+                    each(n, lambda t, xx=xx: add(dst.at[xx, t], src.at[xx, t]))
+            yield from z_steps(lambda zz: grad.at[half, taps, zz, y], rz, add_half)
             start, wait = bundle(rx)
             for k in range(1, SX):
                 start(grad.at[c * SX + x_to(k), taps, z, y], rx.at[k - 1], x_peer(k))
@@ -1243,18 +1279,15 @@
             value = g_diff[c, t, zz, y].astype(F32) + ryd[t, zz].astype(F32)
             g_diff[c, t, zz, y] = value.astype(BF16)
         each(9 * DZ, add_y)
-        start, wait = bundle(rzd)
-        for k in range(1, DZ):
-            start(g_diff.at[c, :, z_to(k), y], rzd.at[k - 1], at_zy(z_to(k), y))
-        yield
-        wait()
-
-        def add_z(t):
-            value = g_diff[c, t, z, y].astype(F32)
-            for k in range(1, DZ):
-                value = value + rzd[k - 1, t].astype(F32)
-            fdx[t] = value
-        each(9, add_z)
+        def add_taps(dst, src):
+            def one(t):
+                dst[t] = (dst[t].astype(F32) + src[t].astype(F32)).astype(BF16)
+            each(9, one)
+        yield from z_steps(lambda zz: g_diff.at[c, :, zz, y], rzd, add_taps)
+
+        def widen(t):
+            fdx[t] = g_diff[c, t, z, y].astype(F32)
+        each(9, widen)
         start, wait = bundle(rxd)
         for k in range(1, SX):
             start(fdx, rxd.at[k - 1], x_peer(k))
@@ -1290,15 +1323,10 @@
             value = rcr[zz, y].astype(F32) + ryr[zz].astype(F32)
             rcr[zz, y] = value.astype(BF16)
         each(DZ, add_y)
-        start, wait = bundle(rzr)
-        for k in range(1, DZ):
-            start(rcr.at[z_to(k), y], rzr.at[k - 1], at_zy(z_to(k), y))
-        yield
-        wait()
-        value = rcr[z, y].astype(F32)
-        for k in range(1, DZ):
-            value = value + rzr[k - 1].astype(F32)
-        frx[...] = value
+        def add_z(dst, src):
+            dst[...] = (dst[...].astype(F32) + src[...].astype(F32)).astype(BF16)
+        yield from z_steps(lambda zz: rcr.at[zz, y], rzr, add_z)
+        frx[...] = rcr[z, y].astype(F32)
         start, wait = bundle(rxr)
         for k in range(1, SX):
             start(frx, rxr.at[k - 1], x_peer(k))
@@ -1312,13 +1340,14 @@
         for b in range(4):
             oe_out[:, b * LANES : (b + 1) * LANES] = value[n_red + b * n_exp : n_red + (b + 1) * n_exp]
 
-    first_x, mid_x, last_x = fr * 5 // 8, 6, lr // 2
-    red_first_x = wide_first(g_first, 0, first_x, "xyz", *bufs[0:4], fbf)
-    red_first_y = wide_first(g_first, first_x, fr - first_x, "yzx", *bufs[4:8], fbf)
-    red_mid_x = wide_mid(g_mid, 0, mid_x, "xyz", *bufs[8:12], fbm)
-    red_mid_y = wide_mid(g_mid, mid_x, 9 - mid_x, "yzx", *bufs[12:16], fbm)
-    red_last_x = wide_first(g_last, 0, last_x, "xyz", *bufs[16:20], fbl)
-    red_last_y = wide_first(g_last, last_x, lr - last_x, "yzx", *bufs[20:24], fbl)
+    bufs = [bufs[n : n + 4] for n in range(0, len(bufs), 4)]
+    spans_f, spans_m, spans_l = portions(fr, 9, lr)
+    red_first = [wide_first(g_first, lo, n, order, *bufs.pop(0), fbf) for order, lo, n in spans_f]
+    red_mid = [wide_mid(g_mid, lo, n, order, *bufs.pop(0), fbm) for order, lo, n in spans_m]
+    red_last = [wide_first(g_last, lo, n, order, *bufs.pop(0), fbl) for order, lo, n in spans_l]
+    fx0, fx1, fy = red_first
+    mx0, mx1, my = red_mid
+    lx, ly = red_last
     red_diff, red_rest = reduce_diff(), reduce_rest()
 
     def push(*chains):
@@ -1345,7 +1374,7 @@
     copies = sp_send(2, parts)
     for n in range(4):
         g_last[n] = dot_tn(sab[...], lgb[:, n * 512 : (n + 1) * 512]).astype(BF16).reshape(DZ, 2, lr, 512)
-    push(red_last_x, red_last_y)
+    push(lx, ly)
     total = sp_total(2, copies)
     gain_2_grad = bias_2_grad = jnp.zeros((1, 512), F32)
     for group in range(NG):
@@ -1361,13 +1390,13 @@
             return carry
         rows_loop(group, apply_2b, 0)
     wait_mid, _ = halo(mgb.at[pl.ds(0, NW)], mgb.at[pl.ds(NW, NW)], None, None, mgr.at[0], mgr.at[1])
-    push(red_last_x, red_last_y)
+    push(lx, ly)
     for a in range(3):
         for b in range(3):
             grad = dot_tn(gs[a : a + 2, :, b * 512 : (b + 1) * 512].reshape(2 * NW, 512), mgb[...]).astype(BF16)
             for qq in range(S):
                 g_mid[qq, 3 * a + b] = grad[:, qq * mw : (qq + 1) * mw].reshape(DZ, 2, wm_in.shape[1], mw)
-    push(red_mid_x, red_mid_y)
+        push(red_mid[a])
     mgs = gs
     for r in range(2):
         spread(mgs, 1 + r, lambda start, r=r: mgb[pl.ds(r * NW + start, STEP), :], True)
@@ -1381,6 +1410,7 @@
     gg[...] = back_taps(mgs[1:3].reshape(2 * NW, 1536), 1)
     gg[0:NW, :] += back_taps(mgs[2], 0)
     gg[NW : 2 * NW, :] += back_taps(mgs[1], 2)
+    push(mx0, my, ly)
     wait_mid()
     spread(mgs, 0, lambda start: mgr[0, pl.ds(start, STEP), :], True)
     spread(mgs, 3, lambda start: mgr[1, pl.ds(start, STEP), :], True)
@@ -1403,7 +1433,7 @@
         cgx[r, 0] = cg_rows[r].astype(BF16)
         cgx[r, 1] = hg
     wait_cg, _ = halo(cgx.at[0], cgx.at[1], None, None, cgr.at[0], cgr.at[1])
-    push(red_mid_x, red_mid_y)
+    push(mx1, lx, ly)
     n_exp = we_in.shape[0]
     grad = dot_tn(comb[...], fgb[...]).astype(BF16)
     n_red = wr_in.shape[0]
@@ -1418,7 +1448,7 @@
         g_diff[0, 3 * a : 3 * a + 3] = grad.reshape(3, DZ, 2, wd0_in.shape[1], LANES)
         grad = (0.5 * dot_tn(ps[a], hg)).astype(BF16)
         g_diff[1, 3 * a : 3 * a + 3] = grad.reshape(3, DZ, 2, wd0_in.shape[1], LANES)
-    push(red_diff, red_last_y, red_last_x)
+    push(red_diff, my)
     wait_cg()
     put_shifts(cgs, 0, cgr[0, 0].astype(F32), 1, True)
     put_shifts(cgs, 3, cgr[1, 0].astype(F32), 1, True)
@@ -1457,7 +1487,7 @@
         parts += [jnp.sum(item, axis=0, keepdims=True) for item in sums]
     copies = sp_send(3, parts)
     g_re[:, :, 0:n_red, :] = dot_tn(fab[...], rgb).astype(BF16).reshape(DZ, 2, n_red, LANES)
-    push(red_rest, red_diff, red_last_x, red_last_y)
+    push(red_rest, lx, ly, red_diff)
     total = sp_total(3, copies)
     gain_1_grad = bias_1_grad = jnp.zeros((1, 512), F32)
     for group in range(NG):
@@ -1496,8 +1526,10 @@
         for qq in range(S):
             g_first[qq, n * per_chunk : (n + 1) * per_chunk] = grad[:, qq * fw : (qq + 1) * fw].reshape(
                 per_chunk, 2, fr, fw)
-    push(red_first_x, red_first_y, red_rest, red_diff)
-    push(red_first_x, red_first_y)
+    push(fx0, fx1, fy)
+    push(red_rest, red_diff, lx, ly, mx0, my)
+    push(fx0, fy, fx1)
+    after_part = ((mx0, my, lx), (mx1, ly, red_rest, red_diff), (mx0, my, fy), (lx, ly))
     weights_first = wf[...].reshape(2048, 512)
     for n in range(4):
         lo = n * 512
@@ -1511,23 +1543,13 @@
             return carry
         lax.fori_loop(0, 2 * NW // STEP, apply_in, 0)
         store_part(n, ig_hbm)
-        if n == 1:
-            push(red_mid_y, red_mid_x)
-    push(red_rest, red_diff, red_last_x, red_last_y)
-    push(red_mid_y, red_mid_x)
-    push(red_first_y, red_first_x)
-    push(red_rest, red_diff)
-    push(red_mid_y, red_mid_x)
-    push(red_first_y, red_first_x)
-    push(red_rest, red_diff)
-    for _ in range(3):
-        push(red_mid_y, red_mid_x, red_last_x, red_last_y, red_rest, red_diff)
-        push(red_first_y, red_first_x)
+        push(*after_part[n])
+    for _ in range(7):
+        push(mx0, my, mx1, fx0, fy, fx1, red_rest, red_diff, lx, ly)
     grad_stores = [local(fbf, fbf_hbm), local(fbm, fbm_hbm), local(fbl, fbl_hbm)]
 
     assert counters["r"] <= ssem.shape[0] and counters["l"] <= lsem.shape[0], counters
     wait_video()
-    row8 = lax.broadcasted_iota(jnp.int32, (8, LANES), 0)
 
     def video_edges(f, carry):
         for ch in range(3):
@@ -1555,13 +1577,20 @@
 def final_kernel(
     sizes, so, vg, out, ig, fbf, fbm, fbl, gr, gd, ge, gsm,
     so_o, vg_o, out_o, ig_o, rgb_o, stemd_o, first_o, mid_o, last_o, red_o, dfull_o, dhalf_o, exp_o,
-    g1_o, b1_o, g2_o, b2_o, g3_o, b3_o, sems, turned,
+    g1_o, b1_o, g2_o, b2_o, g3_o, b3_o, sems, so_v, out_v, ig_v, vg_v,
 ):
     D, S = sizes
-    copies = [
-        pltpu.make_async_copy(src, dst, sems.at[i])
-        for i, (src, dst) in enumerate(((so, so_o), (out, out_o), (ig, ig_o), (vg, vg_o)))]
-    for copy in copies:
+    loads, copies = [], []
+    for src, through, dst in ((so, so_v, so_o), (out, out_v, out_o), (ig, ig_v, ig_o), (vg, vg_v, vg_o)):
+        half = src.shape[0] // 2
+        for rows in (pl.ds(0, half), pl.ds(half, half)):
+            n = len(loads)
+            loads.append(pltpu.make_async_copy(src.at[rows], through.at[rows], sems.at[0, n]))
+            copies.append(pltpu.make_async_copy(through.at[rows], dst.at[rows], sems.at[1, n]))
+    for copy in loads:
+        copy.start()
+    for load, copy in zip(loads, copies):
+        load.wait()
         copy.start()
     fw, lw = fbf.shape[2], fbl.shape[2]
     for q in range(S):
@@ -1573,10 +1602,12 @@
     dfull_o[...] = gd[0]
     dhalf_o[...] = gd[1]
     exp_o[...] = ge[...]
-    turned[:, 0:8] = gsm[0:8, :].T
-    for t in range(9):
-        rgb_o[t] = turned[t * 9 : t * 9 + 3, 0:8]
-        stemd_o[t] = turned[t * 9 + 3 : t * 9 + 9, 0:8]
+    for ch in range(9):
+        value = gsm[0:8, ch * 9 : ch * 9 + 9]
+        if ch < 3:
+            rgb_o[ch] = value
+        else:
+            stemd_o[ch - 3] = value
     width = g1_o.shape[0]
     per = LANES // width
     here = lax.rem(lax.axis_index("dp"), per)
@@ -1603,19 +1634,7 @@
     DZ, SX = D // 2, S // 2
     NF = clip_video.shape[0]
     NW = NF * 16
-    dp = lax.axis_index("dp")
-    frames = clip_video.astype(F32)
-    edges = jnp.stack([frames[:, :, 0], frames[:, :, 7]], axis=2).reshape(NF, 6, LANES)
-    uin = jnp.concatenate([frames.reshape(NF, 24, LANES), edges, jnp.zeros((NF, 2, LANES), F32)], axis=1)
-    per = D * LANES // 512
     width = 512 // D
-    lane = jnp.arange(LANES)
-    stem_w = jnp.concatenate([w_rgb, w_stem_diff], axis=1).astype(F32).transpose(2, 0, 1).reshape(8, 81)
-    stem_w = jnp.pad(stem_w, ((0, 0), (0, LANES - 81)))
-    mids = jnp.stack([gain_first, bias_first, gain_middle, bias_middle]).astype(F32)
-    mids = jnp.where(lane // width == dp % per, jnp.tile(mids, (1, per)), 0.0)
-    lasts = jnp.concatenate([gain_last, bias_last]).astype(F32).reshape(-1, LANES)
-    small = jnp.concatenate([stem_w, mids, lasts], axis=0)
     band = jnp.asarray(band_table(8), BF16)
     fr, fw = w_first.shape[0], 512 // S
     mr, lr, rr = w_middle.shape[1], w_last.shape[0], w_reduce.shape[0]
@@ -1625,7 +1644,7 @@
     vm = pltpu.VMEM
     any_spec = pl.BlockSpec(memory_space=pl.ANY)
     vmem_spec = pl.BlockSpec(memory_space=pltpu.VMEM)
-    n_rem, n_loc = 128, 50
+    n_rem, n_loc = 136, 48
     re_rows = rr + 4 * er
     scratch = [
         pltpu.SemaphoreType.DMA((n_rem,)), pltpu.SemaphoreType.DMA((n_rem,)), pltpu.SemaphoreType.DMA((n_loc,)),
@@ -1633,8 +1652,8 @@
         vm((D, rr, LANES), BF16), vm((2, 9, D, dr, LANES), BF16), vm((D, er, 512), BF16),
         vm((2 * NF, 16, 2048), BF16), vm((2 * NF, 16, 2048), BF16),
         vm((2 * PART, 512, LANES), BF16), vm((2 * PART, 512, LANES), BF16),
-        vm((NF, 32, LANES), F32), vm((NF, 8, LANES), F32), vm((NF, 8, LANES), F32),
-        vm((D, 16, LANES), F32), vm((512, 288), BF16), vm((3, 512, LANES), F32), vm((288, 512), BF16),
+        vm((NF, 32, LANES), F32), vm((NF, 24, LANES), BF16), vm((NF, 24, LANES), BF16),
+        vm((16, LANES), F32), vm((D, 16, LANES), F32), vm((512, 288), BF16), vm((3, 512, LANES), F32), vm((288, 512), BF16),
         vm((NF, 96, LANES), F32),
         vm((NF, 8, LANES), F32), vm((2, NF, 8, LANES), F32), vm((D * 8, LANES), F32), vm((S - 1, D * 8, LANES), F32),
         vm((4, 8, 512), F32), vm((4, S - 1, 8, 512), F32), vm((4, 8, 512), F32), vm((4, S - 1, 8, 512), F32),
@@ -1655,17 +1674,18 @@
         vm((D, 16, LANES), F32), vm((D - 1, 16, LANES), F32),
     ]
 
-    def landing(rows, shape_of):
-        for order, n in (("xyz", rows[0]), ("yzx", rows[1])):
+    def landing(spans, shape_of):
+        for order, _, n in spans:
             extra = (SX,) if order == "yzx" else ()
             scratch.append(vm((SX,) + shape_of(n, (DZ, 2)), BF16))
             scratch.append(vm((SX - 1,) + shape_of(n, (DZ, 2) if order == "xyz" else ()), BF16))
             scratch.append(vm(extra + shape_of(n, (DZ,)), BF16))
             scratch.append(vm((DZ - 1,) + extra + shape_of(n, ()), BF16))
 
-    landing((fr * 5 // 8, fr - fr * 5 // 8), lambda n, lead: lead + (n, fw))
-    landing((6, 3), lambda n, lead: (n,) + lead + (mr, fw))
-    landing((lr // 2, lr - lr // 2), lambda n, lead: lead + (n, lw))
+    spans_f, spans_m, spans_l = portions(fr, 9, lr)
+    landing(spans_f, lambda n, lead: lead + (n, fw))
+    landing(spans_m, lambda n, lead: (n,) + lead + (mr, fw))
+    landing(spans_l, lambda n, lead: lead + (n, lw))
     outs = pl.pallas_call(
         functools.partial(whole_kernel, (D, S, NF)),
         out_shape=(
@@ -1674,38 +1694,43 @@
             shape((S, fr, fw), BF16), shape((S, 9, mr, fw), BF16), shape((S, lr, lw), BF16), shape((rr, LANES), F32),
             shape((2, 9, dr, LANES), F32), shape((er, 512), F32), shape((16, LANES), F32),
         ),
-        in_specs=[pl.BlockSpec(memory_space=pltpu.SMEM)] + [vmem_spec] * 3 + [any_spec] * 10,
+        in_specs=[pl.BlockSpec(memory_space=pltpu.SMEM)] + [vmem_spec] * 10 + [any_spec] * 10,
         out_specs=(any_spec, vmem_spec) + (any_spec,) * 5 + (vmem_spec,) * 4,
         scratch_shapes=scratch,
         compiler_params=pltpu.CompilerParams(
             collective_id=0, has_side_effects=True, vmem_limit_bytes=VMEM_BYTES),
         name="tdn_blocks",
     )(
-        keep_mask, uin, small, band, section_input, section_cot, stem_cot.reshape(NF, 512, LANES),
+        keep_mask, clip_video.reshape(NF, 24, LANES), w_rgb.transpose(1, 2, 0), w_stem_diff.transpose(1, 2, 0),
+        gain_first.reshape(1, -1), bias_first.reshape(1, -1), gain_middle.reshape(1, -1), bias_middle.reshape(1, -1),
+        gain_last.reshape(-1, LANES), bias_last.reshape(-1, LANES), band, section_input, section_cot, stem_cot.reshape(NF, 512, LANES),
         w_first, w_middle, w_last, w_reduce, w_diff_full, w_diff_half, w_expand,
     )
     results = (
         shape(stem_cot.shape, BF16), shape(clip_video.shape, F32), shape(section_input.shape, BF16),
-        shape(section_input.shape, BF16), shape(w_rgb.shape, F32), shape(w_stem_diff.shape, F32),
+        shape(section_input.shape, BF16), shape((3, 8, 9), F32), shape((6, 8, 9), F32),
         shape(w_first.shape, F32), shape(w_middle.shape, F32), shape(w_last.shape, F32), shape(w_reduce.shape, F32),
         shape(w_diff_full.shape, F32), shape(w_diff_half.shape, F32), shape(w_expand.shape, F32),
     ) + (shape((width,), F32),) * 4 + (shape((2048 // D,), F32),) * 2
     so, vg, section_output, input_grad, *grads = outs
-    return pl.pallas_call(
+    finals = pl.pallas_call(
         functools.partial(final_kernel, (D, S)),
         out_shape=results,
         in_specs=[any_spec] * 4 + [vmem_spec] * 7,
         out_specs=(any_spec,) * 4 + (vmem_spec,) * 15,
-        scratch_shapes=[pltpu.SemaphoreType.DMA((4,)), vm((LANES, LANES), F32)],
-        compiler_params=pltpu.CompilerParams(vmem_limit_bytes=24 * 2**20),
+        scratch_shapes=[
+            pltpu.SemaphoreType.DMA((2, 8)), vm(stem_cot.shape, BF16), vm(section_input.shape, BF16),
+            vm(section_input.shape, BF16), vm(clip_video.shape, F32)],
+        compiler_params=pltpu.CompilerParams(vmem_limit_bytes=VMEM_BYTES),
         name="final_outputs",
     )(so.reshape(stem_cot.shape), vg.reshape(clip_video.shape), section_output, input_grad, *grads)
+    return finals[0:4] + (finals[4].transpose(2, 0, 1), finals[5].transpose(2, 0, 1)) + finals[6:]
 
 
 def fits_kernel(mesh):
     dp_count, sp_count = mesh.shape["dp"], mesh.shape["sp"]
     return (
-        dp_count % 2 == 0 and sp_count % 2 == 0 and H5 == 2 * sp_count and HS == 8 * sp_count
+        dp_count % 2 == 0 and dp_count & (dp_count - 1) == 0 and sp_count % 2 == 0 and H5 == 2 * sp_count and HS == 8 * sp_count
         and TDM_C % (16 * dp_count) == 0 and STEM_C == 8 * dp_count and MID // sp_count % LANES == 0
         and C5 // dp_count % LANES == 0 and (dp_count - 1) * (sp_count // 2 - 1) <= dp_count
     )

time: 187 us -> 164 us (0.88)
  local copies, waits for them, and re-layouts: 13.7 us -> 0 us
  Pallas kernels: 168 us -> 163 us
  other arithmetic: 4.46 us -> 0 us
    unnamed x22 -> x0, local copies, waits for them, and re-layouts: 11.8 us -> none
    pallas_call x1, Pallas kernels: 164 us -> 154 us  [on_device_kernel(): pl.pallas_call(functools.partial(whole_kernel, (D, S, NF)), out_shape=(sh...]
    pallas_call x1, Pallas kernels: 4.18 us -> 8.31 us  [on_device_kernel(): pl.pallas_call(functools.partial(final_kernel, (D, S)), out_shape=results...]
    convert_element_type x3 -> x0, other arithmetic: 2.3 us -> none  [the longest x1 0.91 us: on_device_kernel(): frames = clip_video.astype(F32)]
where the time goes in v3:
time: 164 us
  Pallas kernels  163 us (99%)
    pallas_call x1, Pallas kernels, on_device_kernel(): pl.pallas_call(functools.partial(whole_kernel, (D, S, NF)), out_shape=(sh...  154 us
    pallas_call x1, Pallas kernels, on_device_kernel(): pl.pallas_call(functools.partial(final_kernel, (D, S)), out_shape=results...  8.31 us

profile of v3, /device:TPU:0, one launch (start us, length us, event | category | flops | bytes accessed | tf_op | source)
XLA Modules:
  0.0 163.6 jit_solution(1200410307901812519)
XLA Ops:
  0.7 154.5 %tdn_blocks.1 = (bf16[16,512,128]{2,1,0:T(8,128)(2,1)}, f32[16,24,128]{2,1,0:T(8,128)}, bf16[16,2,16,2048]{3,2,1,0:T(8,128)(2,1)}, bf16[16,2,16,2048]{3,2,1,0:T(...) custom-call(s32[16]{0:T(128)} %keep.1, ...), custom_call_target="tpu_custom_call" | custom-call | tf_op jit(solution)/shard_map/tdn_blocks/pallas_call | solution.py:1689
  155.1 8.3 %final_outputs.1 = (bf16[16,64,8,128]{3,2,1,0:T(8,128)(2,1)}, f32[16,3,8,128]{3,2,1,0:T(8,128)}, bf16[16,2,16,2048]{3,2,1,0:T(8,128)(2,1)}, bf16[16,2,16,2048]{3...) custom-call(bf16[16,64,8,128]{3,2,1,0:T(8,128)(2,1)} %bitcast.15, ...), custom_call_target="tpu_custom_call" | custom-call | tf_op jit(solution)/shard_map/final_outputs/pallas_call | solution.py:1716

commit v4 on v3

--- a/solution.py
+++ b/solution.py
@@ -474,12 +474,36 @@
 
 
 def portions(first_rows, taps, last_rows):
-    cut = first_rows * 5 // 16
+    cut = first_rows // 2
     return (
-        (("xyz", 0, cut), ("xyz", cut, cut), ("yzx", 2 * cut, first_rows - 2 * cut)),
-        (("xyz", 0, 3), ("xyz", 3, 3), ("yzx", 6, taps - 6)),
+        (("xyz", 0, cut), ("yzx", cut, first_rows - cut)),
+        (("xyz", 0, 2), ("yzx", 2, 4), ("xyz", 6, taps - 6)),
         (("xyz", 0, last_rows // 2), ("yzx", last_rows // 2, last_rows // 2)),
     )
+
+
+ORDER = {
+    "dwl": ("l0", "l1"),
+    "bn2": ("l1",),
+    "mid": ("l0",),
+    "own": ("m1",),
+    "gate": ("m0", "l1"),
+    "diff": ("d", "l0", "l1"),
+    "bn1": ("r", "d", "l1", "l0",),
+    "fg": ("m2", "m0",),
+    "dwf": ("f0", "f1", "m1", "r", "d", "l0",),
+    "add": ("f0", "f1"),
+    "in0": ("m1", "m0", "l0",),
+    "in1": ("l1", "r", "d"),
+    "in2": ("m2",),
+    "in3": ("m1", "m0", "l0", "r", "d"),
+    "t0": ("f0", "f1", "m2", "l1", "m1"),
+    "t1": ("f0", "f1", "m2", "m0", "m1", "r", "d", "l0", "l1"),
+    "t2": ("f0", "f1", "m2", "m0", "m1", "r", "d", "l0", "l1"),
+    "t4": ("f0", "f1", "m2", "m1", "m0", "r", "d", "l0", "l1",),
+    "t5": ("f0", "f1", "m2", "m1", "m0", "r", "d", "l0", "l1",),
+    "t3": ("f0", "f1", "m2", "m0", "m1", "r", "d", "l0", "l1"),
+}
 
 
 def silu_parts(values):
@@ -667,7 +691,7 @@
     wait_small = to_peers(small, lambda k: sm.at[dp], dp_peers, sm.at[pl.ds(0, D - 1)])
     wait_edges, _ = halo(clip, clip, None, None, uprev, unext)
 
-    def gather(mode, dst):
+    def gather(mode, dst, eager=True):
         wide = {"A": 1, "B": SX, "D": S}[mode]
         first_q = {"A": q_own, "B": c * SX, "D": 0}[mode]
         only = pl.ds(dp, 1)
@@ -683,10 +707,13 @@
         y_start(mine, mine, y_peer)
         yield
 
+        def to_x(part):
+            for k in range(1, SX):
+                x_start(part, part, x_peer(k))
+
         def fan(part):
-            if mode == "A":
-                for k in range(1, SX):
-                    x_start(part, part, x_peer(k))
+            if eager and mode == "A":
+                to_x(part)
             if mode != "D":
                 c_start(part, part, c_peer)
 
@@ -703,6 +730,10 @@
         y_wait()
         for zz in range(DZ):
             fan(dst(pl.ds(zz * 2 + oy, 1), first_q, wide))
+        if mode == "A" and not eager:
+            yield "x"
+            for n in range(1, D):
+                to_x(dst(pl.ds(lax.rem(dp + n, D), 1), first_q, wide))
         yield
         if mode == "A":
             x_wait()
@@ -723,7 +754,7 @@
 
     def first_part(mode, lo, n):
         rows = pl.ds(lo, n)
-        return gather(mode, lambda d, q, w: wf.at[d, rows, lane_block(q, fw, w)])
+        return gather(mode, lambda d, q, w: wf.at[d, rows, lane_block(q, fw, w)], True)
 
     def mid_part(mode, lo, n):
         rows = pl.ds(lo, n)
@@ -744,26 +775,33 @@
         (1, gather("D", lambda d, q, w: wr.at[d])),
         (1, gather("B", lambda d, q, w: wd.at[c, :, d])),
         (1, gather("D", lambda d, q, w: we.at[d])),
-        (1, mid_part("A", 0, 3)), (2, mid_part("B", 6, 3)), (2, mid_part("A", 3, 3)),
-        (3, last_part("A", 0, lr // 2)), (3, last_part("B", lr // 2, lr // 4)),
-        (4, last_part("A", lr * 3 // 4, lr // 4)),
+        (1, mid_part("A", 0, 2)), (2, mid_part("B", 2, 3)), (2, mid_part("A", 5, 2)), (3, mid_part("A", 7, 2)),
+        (4, last_part("B", 0, lr // 2)), (4, last_part("A", lr // 2, lr // 2)),
     ]
     slot = [0]
     arrived = set()
 
-    def pump(count=1):
-        for _ in range(count):
-            for n, (start, chunk) in enumerate(chunks):
-                if start <= slot[0] and n not in arrived:
-                    try:
-                        next(chunk)
-                    except StopIteration:
-                        arrived.add(n)
-            slot[0] += 1
+    held = set()
+
+    def pump(free=0, low=0, high=99):
+        for n, (start, chunk) in enumerate(chunks):
+            if start > slot[0] or n in arrived or not low <= n < high:
+                continue
+            if n in held:
+                if free == 0:
+                    continue
+                free -= 1
+                held.remove(n)
+            try:
+                if next(chunk) == "x":
+                    held.add(n)
+            except StopIteration:
+                arrived.add(n)
+        slot[0] += 1
 
     def need(low, high):
         while not arrived.issuperset(range(low, high)):
-            pump()
+            pump(len(chunks), low, high)
 
     pump()
 
@@ -924,6 +962,7 @@
     for n in range(2):
         z1[:, n * 256 : (n + 1) * 256] = dot_nn(xs, wf[:, :, n * 256 : (n + 1) * 256].reshape(x3.shape[2], 256))
     copies = sp_send(0, two_sums(z1))
+    pump(2)
     need(3, 6)
     total = sp_total(0, copies)
     inv_1 = []
@@ -965,7 +1004,7 @@
         return (pair_sum(upper + lower) * 0.25).astype(BF16).astype(F32)
 
     put_shifts(ps, 1, pool(change[0], change[1]), 2, False)
-    pump()
+    pump(2)
     wait_change()
     above = [chr_[0, r].astype(F32) for r in range(2)]
     below = [chr_[1, r].astype(F32) for r in range(2)]
@@ -1010,7 +1049,7 @@
     def taps_of(a):
         return wm[3 * a : 3 * a + 3].reshape(1536, 512)
 
-    need(6, 9)
+    need(6, 10)
     z2[...] = dot_nn(gs[1:3].reshape(2 * NW, 1536), taps_of(1))
     z2[0:NW, :] += dot_nn(gs[2], taps_of(2))
     z2[NW : 2 * NW, :] += dot_nn(gs[1], taps_of(0))
@@ -1020,7 +1059,7 @@
     z2[0:NW, :] += dot_nn(gs[0], taps_of(0))
     z2[NW : 2 * NW, :] += dot_nn(gs[3], taps_of(2))
     copies = sp_send(1, two_sums(z2))
-    need(9, 12)
+    need(10, 12)
     for copy in load_ct:
         copy.wait()
     total = sp_total(1, copies)
@@ -1106,6 +1145,20 @@
             return carry
         lax.fori_loop(0, count, body, 0)
 
+    def share(block, several):
+        x_start, x_wait = bundle(several.at[pl.ds(0, SX - 1)])
+        c_start, c_wait = bundle(several)
+        for k in range(1, SX):
+            x_start(block(q_own), block(q_own), x_peer(k))
+        c_start(block(q_own), block(q_own), c_peer)
+        yield
+        x_wait()
+        for k in range(1, SX):
+            part = block(c * SX + x_from(k))
+            c_start(part, part, c_peer)
+        yield
+        c_wait()
+
     def z_steps(part, rz, add):
         at = 0
         for bit in z_bits:
@@ -1179,10 +1232,7 @@
         for part in parts:
             value = value + part[...].astype(F32)
         fb[mine, rows] = value.astype(BF16)
-        done = fb.at[mine, rows]
-        wait = to_peers(done, lambda k: done, sp_peers, fb.at[pl.ds(0, S - 1), rows])
-        yield
-        wait()
+        yield from share(lambda q: fb.at[q, rows], fb.at[pl.ds(0, SX), rows])
 
     def wide_mid(grad, lo, n, order, rc, rx, ry, rz, fb):
         taps = pl.ds(lo, n)
@@ -1254,10 +1304,7 @@
                 value = value + part[t].astype(F32)
             fb[mine, lo + t] = value.astype(BF16)
         each(n, finish)
-        done = fb.at[mine, taps]
-        wait = to_peers(done, lambda k: done, sp_peers, fb.at[pl.ds(0, S - 1), taps])
-        yield
-        wait()
+        yield from share(lambda q: fb.at[q, taps], fb.at[pl.ds(0, SX), taps])
 
     def reduce_diff():
         wait = remote(g_diff.at[oc], rcd, c_peer)
@@ -1345,14 +1392,13 @@
     red_first = [wide_first(g_first, lo, n, order, *bufs.pop(0), fbf) for order, lo, n in spans_f]
     red_mid = [wide_mid(g_mid, lo, n, order, *bufs.pop(0), fbm) for order, lo, n in spans_m]
     red_last = [wide_first(g_last, lo, n, order, *bufs.pop(0), fbl) for order, lo, n in spans_l]
-    fx0, fx1, fy = red_first
-    mx0, mx1, my = red_mid
-    lx, ly = red_last
-    red_diff, red_rest = reduce_diff(), reduce_rest()
-
-    def push(*chains):
-        for chain in chains:
-            next(chain, None)
+    chains = {"d": reduce_diff(), "r": reduce_rest()}
+    for name, parts in (("f", red_first), ("m", red_mid), ("l", red_last)):
+        chains.update({name + str(n): part for n, part in enumerate(parts)})
+
+    def at(point):
+        for name in ORDER[point]:
+            next(chains[name], None)
 
     for finish in (free_gated, free_change):
         finish()
@@ -1374,7 +1420,8 @@
     copies = sp_send(2, parts)
     for n in range(4):
         g_last[n] = dot_tn(sab[...], lgb[:, n * 512 : (n + 1) * 512]).astype(BF16).reshape(DZ, 2, lr, 512)
-    push(lx, ly)
+    at("dwl")
+    at("bn2")
     total = sp_total(2, copies)
     gain_2_grad = bias_2_grad = jnp.zeros((1, 512), F32)
     for group in range(NG):
@@ -1390,13 +1437,13 @@
             return carry
         rows_loop(group, apply_2b, 0)
     wait_mid, _ = halo(mgb.at[pl.ds(0, NW)], mgb.at[pl.ds(NW, NW)], None, None, mgr.at[0], mgr.at[1])
-    push(lx, ly)
+    at("mid")
     for a in range(3):
         for b in range(3):
             grad = dot_tn(gs[a : a + 2, :, b * 512 : (b + 1) * 512].reshape(2 * NW, 512), mgb[...]).astype(BF16)
             for qq in range(S):
                 g_mid[qq, 3 * a + b] = grad[:, qq * mw : (qq + 1) * mw].reshape(DZ, 2, wm_in.shape[1], mw)
-        push(red_mid[a])
+        next(red_mid[a])
     mgs = gs
     for r in range(2):
         spread(mgs, 1 + r, lambda start, r=r: mgb[pl.ds(r * NW + start, STEP), :], True)
@@ -1410,7 +1457,7 @@
     gg[...] = back_taps(mgs[1:3].reshape(2 * NW, 1536), 1)
     gg[0:NW, :] += back_taps(mgs[2], 0)
     gg[NW : 2 * NW, :] += back_taps(mgs[1], 2)
-    push(mx0, my, ly)
+    at("own")
     wait_mid()
     spread(mgs, 0, lambda start: mgr[0, pl.ds(start, STEP), :], True)
     spread(mgs, 3, lambda start: mgr[1, pl.ds(start, STEP), :], True)
@@ -1433,7 +1480,7 @@
         cgx[r, 0] = cg_rows[r].astype(BF16)
         cgx[r, 1] = hg
     wait_cg, _ = halo(cgx.at[0], cgx.at[1], None, None, cgr.at[0], cgr.at[1])
-    push(mx1, lx, ly)
+    at("gate")
     n_exp = we_in.shape[0]
     grad = dot_tn(comb[...], fgb[...]).astype(BF16)
     n_red = wr_in.shape[0]
@@ -1448,7 +1495,7 @@
         g_diff[0, 3 * a : 3 * a + 3] = grad.reshape(3, DZ, 2, wd0_in.shape[1], LANES)
         grad = (0.5 * dot_tn(ps[a], hg)).astype(BF16)
         g_diff[1, 3 * a : 3 * a + 3] = grad.reshape(3, DZ, 2, wd0_in.shape[1], LANES)
-    push(red_diff, my)
+    at("diff")
     wait_cg()
     put_shifts(cgs, 0, cgr[0, 0].astype(F32), 1, True)
     put_shifts(cgs, 3, cgr[1, 0].astype(F32), 1, True)
@@ -1487,7 +1534,7 @@
         parts += [jnp.sum(item, axis=0, keepdims=True) for item in sums]
     copies = sp_send(3, parts)
     g_re[:, :, 0:n_red, :] = dot_tn(fab[...], rgb).astype(BF16).reshape(DZ, 2, n_red, LANES)
-    push(red_rest, lx, ly, red_diff)
+    at("bn1")
     total = sp_total(3, copies)
     gain_1_grad = bias_1_grad = jnp.zeros((1, 512), F32)
     for group in range(NG):
@@ -1520,16 +1567,15 @@
     for k in range(1, D):
         small_start(sms.at[lax.rem(dp + k, D)], smr.at[k - 1], dp_peers[k - 1])
 
+    at("fg")
     for n in range(4):
         grad = dot_tn(x3[:, :, n * 512 : (n + 1) * 512].reshape(2 * NW, 512), fgb[...]).astype(BF16)
         per_chunk = 512 // (2 * fr)
         for qq in range(S):
             g_first[qq, n * per_chunk : (n + 1) * per_chunk] = grad[:, qq * fw : (qq + 1) * fw].reshape(
                 per_chunk, 2, fr, fw)
-    push(fx0, fx1, fy)
-    push(red_rest, red_diff, lx, ly, mx0, my)
-    push(fx0, fy, fx1)
-    after_part = ((mx0, my, lx), (mx1, ly, red_rest, red_diff), (mx0, my, fy), (lx, ly))
+    at("dwf")
+    at("add")
     weights_first = wf[...].reshape(2048, 512)
     for n in range(4):
         lo = n * 512
@@ -1543,9 +1589,13 @@
             return carry
         lax.fori_loop(0, 2 * NW // STEP, apply_in, 0)
         store_part(n, ig_hbm)
-        push(*after_part[n])
-    for _ in range(7):
-        push(mx0, my, mx1, fx0, fy, fx1, red_rest, red_diff, lx, ly)
+        at("in" + str(n))
+    for point in sorted(ORDER):
+        if point[0] == "t":
+            at(point)
+    for chain in chains.values():
+        for _ in chain:
+            pass
     grad_stores = [local(fbf, fbf_hbm), local(fbm, fbm_hbm), local(fbl, fbl_hbm)]
 
     assert counters["r"] <= ssem.shape[0] and counters["l"] <= lsem.shape[0], counters
@@ -1644,7 +1694,7 @@
     vm = pltpu.VMEM
     any_spec = pl.BlockSpec(memory_space=pl.ANY)
     vmem_spec = pl.BlockSpec(memory_space=pltpu.VMEM)
-    n_rem, n_loc = 136, 48
+    n_rem, n_loc = 146, 48
     re_rows = rr + 4 * er
     scratch = [
         pltpu.SemaphoreType.DMA((n_rem,)), pltpu.SemaphoreType.DMA((n_rem,)), pltpu.SemaphoreType.DMA((n_loc,)),

time: 164 us -> 151 us (0.921)
  Pallas kernels: 163 us -> 150 us
    pallas_call x1, Pallas kernels: 154 us -> 141 us  [on_device_kernel(): pl.pallas_call(functools.partial(whole_kernel, (D, S, NF)), out_shape=(sh...]
where the time goes in v4:
time: 151 us
  Pallas kernels  150 us (99%)
    pallas_call x1, Pallas kernels, on_device_kernel(): pl.pallas_call(functools.partial(whole_kernel, (D, S, NF)), out_shape=(sh...  141 us
    pallas_call x1, Pallas kernels, on_device_kernel(): pl.pallas_call(functools.partial(final_kernel, (D, S)), out_shape=results...  8.31 us

profile of v4, /device:TPU:0, one launch (start us, length us, event | category | flops | bytes accessed | tf_op | source)
XLA Modules:
  0.0 150.6 jit_solution(8609503639907340595)
XLA Ops:
  0.7 141.4 %tdn_blocks.1 = (bf16[16,512,128]{2,1,0:T(8,128)(2,1)}, f32[16,24,128]{2,1,0:T(8,128)}, bf16[16,2,16,2048]{3,2,1,0:T(8,128)(2,1)}, bf16[16,2,16,2048]{3,2,1,0:T(...) custom-call(s32[16]{0:T(128)} %keep.1, ...), custom_call_target="tpu_custom_call" | custom-call | tf_op jit(solution)/shard_map/tdn_blocks/pallas_call | solution.py:1739
  142.1 8.3 %final_outputs.1 = (bf16[16,64,8,128]{3,2,1,0:T(8,128)(2,1)}, f32[16,3,8,128]{3,2,1,0:T(8,128)}, bf16[16,2,16,2048]{3,2,1,0:T(8,128)(2,1)}, bf16[16,2,16,2048]{3...) custom-call(bf16[16,64,8,128]{3,2,1,0:T(8,128)(2,1)} %bitcast.15, ...), custom_call_target="tpu_custom_call" | custom-call | tf_op jit(solution)/shard_map/final_outputs/pallas_call | solution.py:1766

commit v5 on v4

--- a/solution.py
+++ b/solution.py
@@ -490,8 +490,8 @@
     "gate": ("m0", "l1"),
     "diff": ("d", "l0", "l1"),
     "bn1": ("r", "d", "l1", "l0",),
-    "fg": ("m2", "m0",),
-    "dwf": ("f0", "f1", "m1", "r", "d", "l0",),
+    "fg": ("m2",),
+    "dwf": ("f0", "f1", "m0", "m1", "r", "d", "l0",),
     "add": ("f0", "f1"),
     "in0": ("m1", "m0", "l0",),
     "in1": ("l1", "r", "d"),

time: 151 us -> 151 us (level)
  no operation moved by 1% of the time
where the time goes in v5:
time: 151 us
  Pallas kernels  150 us (99%)
    pallas_call x1, Pallas kernels, on_device_kernel(): pl.pallas_call(functools.partial(whole_kernel, (D, S, NF)), out_shape=(sh...  141 us
    pallas_call x1, Pallas kernels, on_device_kernel(): pl.pallas_call(functools.partial(final_kernel, (D, S)), out_shape=results...  8.31 us

profile of v5, /device:TPU:0, one launch (start us, length us, event | category | flops | bytes accessed | tf_op | source)
XLA Modules:
  0.0 150.6 jit_solution(1021890095687825435)
XLA Ops:
  0.7 141.4 %tdn_blocks.1 = (bf16[16,512,128]{2,1,0:T(8,128)(2,1)}, f32[16,24,128]{2,1,0:T(8,128)}, bf16[16,2,16,2048]{3,2,1,0:T(8,128)(2,1)}, bf16[16,2,16,2048]{3,2,1,0:T(...) custom-call(s32[16]{0:T(128)} %keep.1, ...), custom_call_target="tpu_custom_call" | custom-call | tf_op jit(solution)/shard_map/tdn_blocks/pallas_call | solution.py:1739
  142.1 8.3 %final_outputs.1 = (bf16[16,64,8,128]{3,2,1,0:T(8,128)(2,1)}, f32[16,3,8,128]{3,2,1,0:T(8,128)}, bf16[16,2,16,2048]{3,2,1,0:T(8,128)(2,1)}, bf16[16,2,16,2048]{3...) custom-call(bf16[16,64,8,128]{3,2,1,0:T(8,128)(2,1)} %bitcast.15, ...), custom_call_target="tpu_custom_call" | custom-call | tf_op jit(solution)/shard_map/final_outputs/pallas_call | solution.py:1766
